TPU v7x, 128 devices: a whole 4x4x4 slice. The times are simulated.
128 devices in a mesh: ctx: 32 (over x, z, core), head: 4 (over y).
Axes of the slice: x: 4, y: 4, z: 4, core: 2. Of those that a mesh axis runs over, the one named last changes fastest.
Arguments:
- queries: float32 [32768, 2048], P('ctx', 'head'), may hold values from -6 to 6
- keys: float32 [32768, 2048], P('ctx', 'head'), may hold values from -6 to 6
- values: float32 [32768, 2048], P('ctx', 'head'), may hold values from -6 to 6
- gate_logit: float32 [16], P('head'), may hold values from -2 to 2
- out_weight: float32 [2048, 4096], P('head'), may hold values from -0.125 to 0.125
- out_grad: float32 [32768, 4096], P('ctx', 'head'), may hold values from -6 to 6
Outputs:
- query_grad: float32 [32768, 2048], P('ctx', 'head')
- key_grad: float32 [32768, 2048], P('ctx', 'head')
- value_grad: float32 [32768, 2048], P('ctx', 'head')
- weight_grad: float32 [4096, 2048], P('ctx', 'head')
- gate_grad: float32 [16], P('head')
All inputs are finite; a program needn't handle non-finite values.
Results may differ from a plain program's by a relative error of at most 0.0003.
Values sent between devices are 32-bit elements; how exact they have to be, the bound alone decides.
No kernel may reach another device: no remote copies, remote signals or barrier semaphores. Data moves between devices by JAX's collectives and lax.ppermute only.
A program may use at most 192 MiB of HBM per device.

v0:
```python
import functools
import math

import jax
import jax.numpy as jnp
from jax import lax
from jax.experimental import pallas as pl
from jax.experimental.pallas import tpu as pltpu
from jax.sharding import PartitionSpec as P

SEG = 1024
HEAD = 128
ROWS = 136
FORWARD_QB = 512
BACKWARD_QB = 256
MOST = SEG // 2
REST = SEG - MOST
STEP = 256
LIGHT = 2**16
VMEM_LIMIT = 60 * 2**20
MICROSECOND = 3_600_000

f32 = jnp.float32
bf16 = jnp.bfloat16
HIGH = lax.Precision.HIGH


def lifted(x):
    return jnp.where(x > 0, x + 1.0, jnp.exp(jnp.minimum(x, 0.0)))


def lifted_slope(x):
    return jnp.where(x > 0, 1.0, jnp.exp(jnp.minimum(x, 0.0)))


def halves(x):
    hi = x.astype(bf16)
    return hi, (x - hi.astype(f32)).astype(bf16)


def mm(a, b, contract):
    dims = ((contract[:1], contract[1:]), ((), ()))

    def one(x, y):
        return lax.dot_general(x, y, dims, preferred_element_type=f32)

    return one(a[0], b[0]) + (one(a[0], b[1]) + one(a[1], b[0]))


NN = (1, 0)
NT = (1, 1)
TN = (0, 0)


def dot(a, b, contract):
    return lax.dot_general(
        a, b, ((contract[:1], contract[1:]), ((), ())), preferred_element_type=f32
    )


def wide(pair):
    return jnp.concatenate(pair, axis=1)


def doubled(x):
    return jnp.concatenate([x, x], axis=1)


def scores_of(a_wide, b_hi_twice, b_lo):
    return dot(a_wide, b_hi_twice, NT) + dot(a_wide[:, :HEAD], b_lo, NT)


def times_wide(a, b_wide):
    both = dot(a[0], b_wide, NN)
    return both[:, :HEAD] + (both[:, HEAD:] + dot(a[1], b_wide[:, :HEAD], NN))


def tall_times(a_tall, b):
    both = dot(a_tall, b[0], NN)
    return both[:HEAD] + (both[HEAD:] + dot(a_tall[:HEAD], b[1], NN))


def update_kernel(k_ref, v_ref, out_ref):
    lk = lifted(k_ref[...])
    out_ref[0, :HEAD, :] = mm(halves(lk.T), halves(v_ref[...]), NN)
    out_ref[0, HEAD : HEAD + 1, :] = jnp.sum(lk, axis=0, keepdims=True)
    out_ref[0, HEAD + 1 :, :] = jnp.zeros((ROWS - HEAD - 1, HEAD), f32)


LOG2E = math.log2(math.e)
TEMPER = 1.0 / math.sqrt(HEAD)


def parts_of(qb, size):
    return ([(0, qb * size, False)] if qb else []) + [(qb * size, (qb + 1) * size, True)]


def causal(size):
    t = lax.broadcasted_iota(jnp.int32, (size, size), 0)
    return t <= lax.broadcasted_iota(jnp.int32, (size, size), 1)


def forward_kernel(q_ref, k_ref, v_ref, *refs):
    out_ref, lse_ref = refs[-2:]
    key = wide(halves(k_ref[...]))
    value_t = jnp.concatenate(halves(v_ref[...].T), axis=0)
    q_hi, q_lo = halves(q_ref[...] * (TEMPER * LOG2E))
    q_twice = doubled(q_hi)
    seen = causal(FORWARD_QB)
    for qb in range(SEG // FORWARD_QB):
        at = slice(qb * FORWARD_QB, (qb + 1) * FORWARD_QB)
        scores = []
        for low, high, own in parts_of(qb, FORWARD_QB):
            part = scores_of(key[low:high], q_twice[at], q_lo[at])
            scores.append(jnp.where(seen, part, -1e30) if own else part)
        top = functools.reduce(
            jnp.maximum, [jnp.max(part, axis=0, keepdims=True) for part in scores]
        )
        total, out_t = 0.0, 0.0
        for (low, high, _), part in zip(parts_of(qb, FORWARD_QB), scores):
            weights = jnp.exp2(part - top)
            total = total + jnp.sum(weights, axis=0, keepdims=True)
            out_t = out_t + tall_times(value_t[:, low:high], halves(weights))
        out_ref[at, :] = (out_t * (1.0 / total)).T
        lse_ref[0, :, at] = top + jnp.log2(total)


def mix_kernel(q_ref, local_ref, mem_ref, g_ref, hi_ref, lo_ref, memout_ref, lqd_ref):
    g = g_ref[0]
    lq = lifted(q_ref[...])
    norm = mem_ref[0, HEAD : HEAD + 1, :]
    denom = jnp.sum(lq * norm, axis=1, keepdims=True) + 1.0
    inverse = 1.0 / denom
    memory_out = mm(halves(lq), halves(mem_ref[0, :HEAD, :]), NN) * inverse
    memout_ref[...] = memory_out
    mixed = g * memory_out + (1.0 - g) * local_ref[...]
    hi_ref[...], lo_ref[...] = halves(mixed.T)
    lqd_ref[...] = lq * (inverse * g)


def add_weight_part(mixed, block, first, start, mine_ref, send_ref):
    part = mm(mixed, block, NN)
    groups = part.shape[1] // (2 * HEAD)
    for k in range(groups):
        even = part[:, 2 * k * HEAD : (2 * k + 1) * HEAD]
        odd = part[:, (2 * k + 1) * HEAD : (2 * k + 2) * HEAD]
        mine_ref[start + k] += jnp.where(first, even, odd)
        send_ref[start + k] += jnp.where(first, odd, even)


def block_kernel(at_ref, *refs, blocks, added, summed):
    refs = list(refs)

    def take(n):
        taken, refs[:] = refs[:n], refs[n:]
        return taken

    acc, block_refs, w_refs, mixed_refs = take(added), take(blocks), take(blocks), take(2)
    before, (out_ref,), by_core = take(summed), take(1), take(2)

    @pl.when(pl.program_id(0) == 0)
    def _():
        for n, w_ref in enumerate(w_refs):
            refs[2 * n][...], refs[2 * n + 1][...] = halves(w_ref[...])
        for n, ref in enumerate(by_core):
            ref[...] = before[n][...] if summed else jnp.zeros_like(ref)

    mixed = tuple(ref[...] for ref in mixed_refs)
    total = acc[0][...] if added else None
    start = 0
    for n, block_ref in enumerate(block_refs):
        block = halves(block_ref[...])
        product = mm(block, (refs[2 * n][...], refs[2 * n + 1][...]), NT)
        total = product if total is None else total + product
        add_weight_part(mixed, block, at_ref[blocks] == 0, start, *by_core)
        start += block_ref.shape[1] // (2 * HEAD)
    out_ref[...] = total


def tail_kernel(at_ref, *refs):
    acc_ref, a_ref, b_ref, wa_ref, wb_ref, lqd_ref, memout_ref, local_ref = refs[:8]
    mhi_ref, mlo_ref, *before = refs[8:-8]
    mg_ref, state_ref, mine_ref, send_ref, *w = refs[-8:]

    @pl.when(pl.program_id(0) == 0)
    def _():
        w[0][...], w[1][...] = halves(wa_ref[...])
        w[2][...], w[3][...] = halves(wb_ref[...])
        for n, ref in enumerate((state_ref, mine_ref, send_ref)):
            ref[...] = before[n][...] if before else jnp.zeros_like(ref)

    a, b = halves(a_ref[...]), halves(b_ref[...])
    mg = acc_ref[...] + mm(a, (w[0][...], w[1][...]), NT)
    mg = mg + mm(b, (w[2][...], w[3][...]), NT)
    mg_ref[...] = mg
    for h in range(state_ref.shape[0]):
        at = slice(h * HEAD, (h + 1) * HEAD)
        here, lqd, memory_out = mg[:, at], lqd_ref[:, at], memout_ref[:, at]
        state_ref[h, :HEAD, :] += mm(halves(lqd.T), halves(here), NN)
        r = jnp.sum(here * memory_out, axis=1, keepdims=True)
        state_ref[h, HEAD : HEAD + 1, :] -= jnp.sum(lqd * r, axis=0, keepdims=True)
        state_ref[h, HEAD + 1 : HEAD + 2, :] += jnp.sum(
            here * (memory_out - local_ref[:, at]), axis=0, keepdims=True
        )
    mixed, first = (mhi_ref[...], mlo_ref[...]), at_ref[2] == 0
    groups = a_ref.shape[1] // (2 * HEAD)
    add_weight_part(mixed, a, first, 0, mine_ref, send_ref)
    add_weight_part(mixed, b, first, groups, mine_ref, send_ref)


def rows_of(width, first=0):
    return pl.BlockSpec((STEP, width), lambda i, at: (i + first // STEP, 0))


def weight_specs(width, blocks):
    return [
        pl.BlockSpec(
            (width, block.shape[1]), lambda i, at, k=k: (0, at[k]), pipeline_mode=pl.Buffered(1)
        )
        for k, block in enumerate(blocks)
    ]


def tail_kernel(at_ref, *refs):
    acc_ref, a_ref, b_ref, wa_ref, wb_ref, lqd_ref, memout_ref, local_ref = refs[:8]
    mhi_ref, mlo_ref, *before = refs[8:-8]
    mg_ref, state_ref, mine_ref, send_ref, *w = refs[-8:]

    @pl.when(pl.program_id(0) == 0)
    def _():
        w[0][...], w[1][...] = halves(wa_ref[...])
        w[2][...], w[3][...] = halves(wb_ref[...])
        for n, ref in enumerate((state_ref, mine_ref, send_ref)):
            ref[...] = before[n][...] if before else jnp.zeros_like(ref)

    a, b = halves(a_ref[...]), halves(b_ref[...])
    mg = acc_ref[...] + mm(a, (w[0][...], w[1][...]), NT)
    mg = mg + mm(b, (w[2][...], w[3][...]), NT)
    mg_ref[...] = mg
    for h in range(state_ref.shape[0]):
        at = slice(h * HEAD, (h + 1) * HEAD)
        here, lqd, memory_out = mg[:, at], lqd_ref[:, at], memout_ref[:, at]
        state_ref[h, :HEAD, :] += mm(halves(lqd.T), halves(here), NN)
        r = jnp.sum(here * memory_out, axis=1, keepdims=True)
        state_ref[h, HEAD : HEAD + 1, :] -= jnp.sum(lqd * r, axis=0, keepdims=True)
        state_ref[h, HEAD + 1 : HEAD + 2, :] += jnp.sum(
            here * (memory_out - local_ref[:, at]), axis=0, keepdims=True
        )
    mixed, first = (mhi_ref[...], mlo_ref[...]), at_ref[2] == 0
    groups = a_ref.shape[1] // (2 * HEAD)
    add_weight_part(mixed, a, first, 0, mine_ref, send_ref)
    add_weight_part(mixed, b, first, groups, mine_ref, send_ref)


def rows_of(width, first=0):
    return pl.BlockSpec((STEP, width), lambda i, at: (i + first // STEP, 0))


def weight_specs(width, blocks):
    return [
        pl.BlockSpec(
            (width, block.shape[1]), lambda i, at, k=k: (0, at[k]), pipeline_mode=pl.Buffered(1)
        )
        for k, block in enumerate(blocks)
    ]


def tail_kernel(at_ref, *refs):
    acc_ref, a_ref, b_ref, wa_ref, wb_ref, lqd_ref, memout_ref, local_ref = refs[:8]
    mhi_ref, mlo_ref, *before = refs[8:-8]
    mg_ref, state_ref, mine_ref, send_ref, *w = refs[-8:]

    @pl.when(pl.program_id(0) == 0)
    def _():
        w[0][...], w[1][...] = halves(wa_ref[...])
        w[2][...], w[3][...] = halves(wb_ref[...])
        for n, ref in enumerate((state_ref, mine_ref, send_ref)):
            ref[...] = before[n][...] if before else jnp.zeros_like(ref)

    a, b = halves(a_ref[...]), halves(b_ref[...])
    mg = acc_ref[...] + mm(a, (w[0][...], w[1][...]), NT)
    mg = mg + mm(b, (w[2][...], w[3][...]), NT)
    mg_ref[...] = mg
    for h in range(state_ref.shape[0]):
        at = slice(h * HEAD, (h + 1) * HEAD)
        here, lqd, memory_out = mg[:, at], lqd_ref[:, at], memout_ref[:, at]
        state_ref[h, :HEAD, :] += mm(halves(lqd.T), halves(here), NN)
        r = jnp.sum(here * memory_out, axis=1, keepdims=True)
        state_ref[h, HEAD : HEAD + 1, :] -= jnp.sum(lqd * r, axis=0, keepdims=True)
        state_ref[h, HEAD + 1 : HEAD + 2, :] += jnp.sum(
            here * (memory_out - local_ref[:, at]), axis=0, keepdims=True
        )
    mixed, first = (mhi_ref[...], mlo_ref[...]), at_ref[2] == 0
    groups = a_ref.shape[1] // (2 * HEAD)
    add_weight_part(mixed, a, first, 0, mine_ref, send_ref)
    add_weight_part(mixed, b, first, groups, mine_ref, send_ref)


def rows_of(width, first=0):
    return pl.BlockSpec((STEP, width), lambda i, at: (i + first // STEP, 0))


def weight_specs(width, blocks):
    return [
        pl.BlockSpec(
            (width, block.shape[1]), lambda i, at, k=k: (0, at[k]), pipeline_mode=pl.Buffered(1)
        )
        for k, block in enumerate(blocks)
    ]


def tail_kernel(at_ref, *refs):
    acc_ref, a_ref, b_ref, wa_ref, wb_ref, lqd_ref, memout_ref, local_ref = refs[:8]
    mhi_ref, mlo_ref, *before = refs[8:-8]
    mg_ref, state_ref, mine_ref, send_ref, *w = refs[-8:]

    @pl.when(pl.program_id(0) == 0)
    def _():
        w[0][...], w[1][...] = halves(wa_ref[...])
        w[2][...], w[3][...] = halves(wb_ref[...])
        for n, ref in enumerate((state_ref, mine_ref, send_ref)):
            ref[...] = before[n][...] if before else jnp.zeros_like(ref)

    a, b = halves(a_ref[...]), halves(b_ref[...])
    mg = acc_ref[...] + mm(a, (w[0][...], w[1][...]), NT)
    mg = mg + mm(b, (w[2][...], w[3][...]), NT)
    mg_ref[...] = mg
    for h in range(state_ref.shape[0]):
        at = slice(h * HEAD, (h + 1) * HEAD)
        here, lqd, memory_out = mg[:, at], lqd_ref[:, at], memout_ref[:, at]
        state_ref[h, :HEAD, :] += mm(halves(lqd.T), halves(here), NN)
        r = jnp.sum(here * memory_out, axis=1, keepdims=True)
        state_ref[h, HEAD : HEAD + 1, :] -= jnp.sum(lqd * r, axis=0, keepdims=True)
        state_ref[h, HEAD + 1 : HEAD + 2, :] += jnp.sum(
            here * (memory_out - local_ref[:, at]), axis=0, keepdims=True
        )
    mixed, first = (mhi_ref[...], mlo_ref[...]), at_ref[2] == 0
    groups = a_ref.shape[1] // (2 * HEAD)
    add_weight_part(mixed, a, first, 0, mine_ref, send_ref)
    add_weight_part(mixed, b, first, groups, mine_ref, send_ref)


def rows_of(width, first=0):
    return pl.BlockSpec((STEP, width), lambda i, at: (i + first // STEP, 0))


def weight_specs(width, blocks):
    return [
        pl.BlockSpec(
            (width, block.shape[1]), lambda i, at, k=k: (0, at[k]), pipeline_mode=pl.Buffered(1)
        )
        for k, block in enumerate(blocks)
    ]


def round_of(acc, blocks, places, out_weight, mixed, core, first=0, before=(), micros=0):
    rows = blocks[0].shape[0]
    width = out_weight.shape[0]
    n = len(blocks)
    groups = sum(block.shape[1] for block in blocks) // (2 * HEAD)
    at = jnp.stack([*places, core]).astype(jnp.int32)
    acc = [] if acc is None else [acc]
    by_core = pl.BlockSpec((groups, width, HEAD), lambda i, at: (0, 0, 0))
    by_core_shape = jax.ShapeDtypeStruct((groups, width, HEAD), f32)
    return pl.pallas_call(
        functools.partial(block_kernel, blocks=n, added=len(acc), summed=len(before)),
        grid_spec=pltpu.PrefetchScalarGridSpec(
            num_scalar_prefetch=1,
            grid=(rows // STEP,),
            in_specs=[rows_of(width, first) for _ in acc]
            + [rows_of(block.shape[1]) for block in blocks]
            + weight_specs(width, blocks)
            + [pl.BlockSpec((width, STEP), lambda i, at: (0, i + first // STEP))] * 2
            + [by_core] * len(before),
            out_specs=[rows_of(width, first)] + [by_core] * 2,
            scratch_shapes=[
                pltpu.VMEM((width, block.shape[1]), bf16) for block in blocks for _ in range(2)
            ],
        ),
        out_shape=[jax.ShapeDtypeStruct((SEG, width), f32)] + [by_core_shape] * 2,
        input_output_aliases={1: 0} if acc else {},
        compiler_params=pltpu.CompilerParams(vmem_limit_bytes=VMEM_LIMIT),
        cost_estimate=pl.CostEstimate(flops=LIGHT, bytes_accessed=LIGHT, transcendentals=0),
        name="round",
    )(at, *acc, *blocks, *([out_weight] * n), *mixed, *before)


def tail_of(second, acc, blocks, places, out_weight, mixed, core, whole, before):
    rows, deep = blocks[0].shape
    width = out_weight.shape[0]
    first = second * MOST
    by_core = deep // HEAD, width, HEAD
    sums = [(width // HEAD, ROWS, HEAD), by_core, by_core]
    sum_specs = [pl.BlockSpec(shape, lambda i, at: (0, 0, 0)) for shape in sums]
    return pl.pallas_call(
        tail_kernel,
        grid_spec=pltpu.PrefetchScalarGridSpec(
            num_scalar_prefetch=1,
            grid=(rows // STEP,),
            in_specs=[rows_of(width, first)]
            + [rows_of(deep)] * 2
            + weight_specs(width, blocks)
            + [rows_of(width, first)] * 3
            + [pl.BlockSpec((width, STEP), lambda i, at: (0, i + first // STEP))] * 2
            + sum_specs[: len(before)],
            out_specs=[rows_of(width), *sum_specs],
            scratch_shapes=[pltpu.VMEM((width, deep), bf16) for _ in range(4)],
        ),
        out_shape=[jax.ShapeDtypeStruct(shape, f32) for shape in [(rows, width), *sums]],
        compiler_params=pltpu.CompilerParams(vmem_limit_bytes=VMEM_LIMIT),
        cost_estimate=pl.CostEstimate(flops=LIGHT, bytes_accessed=LIGHT, transcendentals=0),
        name="tail",
    )(
        jnp.stack([*places, core]).astype(jnp.int32),
        acc, *blocks, out_weight, out_weight, *whole, *mixed, *before,
    )


def backward_kernel(*refs, first):
    q_ref, k_ref, v_ref, mg_ref, local_ref, memout_ref, lse_ref, mem_ref, g_ref = refs[:9]
    dq_ref, dk_ref, dv_ref = refs[-3:]
    g = g_ref[0]
    q = q_ref[...]
    mg = mg_ref[...]
    local_grad = (1.0 - g) * TEMPER * mg
    key = halves(k_ref[...])
    key_t = jnp.concatenate([key[0].T, key[1].T], axis=0)
    key = wide(key)
    value = wide(halves(v_ref[...]))
    query = halves(q * (TEMPER * LOG2E))
    q_twice, q_wide = doubled(query[0]), wide(query)
    grad = halves(local_grad)
    g_twice, g_wide = doubled(grad[0]), wide(grad)
    delta = jnp.sum((local_grad * local_ref[...]).T, axis=0, keepdims=True)
    lq = lifted(q)
    norm = mem_ref[0, HEAD : HEAD + 1, :]
    inverse = 1.0 / (jnp.sum(lq * norm, axis=1, keepdims=True) + 1.0)
    r = jnp.sum(mg * memout_ref[...], axis=1, keepdims=True)
    lift_grad = mm(halves(mg), halves(mem_ref[0, :HEAD, :].T), NN) - r * norm
    dq_ref[...] = lift_grad * (inverse * g) * lifted_slope(q)
    for ref, before in zip((dk_ref, dv_ref), refs[9:11] if first else (None, None)):
        ref[first:, :] = jnp.zeros(q.shape, f32)
        if first:
            ref[:first, :] = before[...]
    seen = causal(BACKWARD_QB)
    for qb in range(q.shape[0] // BACKWARD_QB):
        at = slice(qb * BACKWARD_QB, (qb + 1) * BACKWARD_QB)
        dq_t = 0.0
        for low, high, own in parts_of(qb + first // BACKWARD_QB, BACKWARD_QB):
            scores = scores_of(key[low:high], q_twice[at], query[1][at])
            if own:
                scores = jnp.where(seen, scores, -1e30)
            weights = jnp.exp2(scores - lse_ref[0, :, at])
            dp = scores_of(value[low:high], g_twice[at], grad[1][at])
            ds = halves(weights * (dp - delta[:, at]))
            dv_ref[low:high, :] += times_wide(halves(weights), g_wide[at])
            dk_ref[low:high, :] += times_wide(ds, q_wide[at])
            dq_t = dq_t + tall_times(key_t[:, low:high], ds)
        dq_ref[at, :] += dq_t.T
    if first:
        dk_ref[...] = dk_ref[...] * (1.0 / (TEMPER * LOG2E))
        dv_ref[...] = dv_ref[...] * (1.0 / TEMPER)


def backward_of(second, heads, ins, before, earlier, micros):
    width = ins[0].shape[1]
    low, count = heads

    def rows(n, at=0):
        return pl.BlockSpec((n, HEAD), lambda h: (at, h + low))

    def of_head(x, n=None, at=0):
        return pl.BlockSpec((1, x.shape[1], n or x.shape[2]), lambda h: (h + low, 0, at))

    size, at_part = (REST, MOST // REST) if second else (MOST, 0)
    here = rows(size, at_part)
    seen = rows(SEG if second else MOST)
    shapes = [(SEG, width)] + [(SEG if second else MOST, width)] * 2
    return pl.pallas_call(
        functools.partial(backward_kernel, first=second * MOST),
        grid=(count,),
        in_specs=[here, seen, seen, rows(size), here, here]
        + [of_head(ins[6], size, at_part), of_head(ins[7]), of_head(ins[8])]
        + [rows(MOST)] * len(before)
        + [pl.BlockSpec(memory_space=pl.ANY)] * len(earlier),
        out_specs=[here, seen, seen],
        out_shape=[jax.ShapeDtypeStruct(shape, f32) for shape in shapes],
        input_output_aliases={len(ins) + len(before) + i: i for i in range(len(earlier))},
        compiler_params=pltpu.CompilerParams(vmem_limit_bytes=VMEM_LIMIT),
        cost_estimate=pl.CostEstimate(
            flops=LIGHT, bytes_accessed=micros * MICROSECOND or LIGHT, transcendentals=0
        ),
        name="backward",
    )(*ins, *before, *earlier)


def forward_of(heads, ins, earlier):
    width = ins[0].shape[1]
    low, count = heads
    column = pl.BlockSpec((SEG, HEAD), lambda h: (0, h + low))
    line = pl.BlockSpec((1, 1, SEG), lambda h: (h + low, 0, 0))
    return pl.pallas_call(
        forward_kernel,
        grid=(count,),
        in_specs=[column] * 3 + [pl.BlockSpec(memory_space=pl.ANY)] * len(earlier),
        out_specs=[column, line],
        out_shape=[
            jax.ShapeDtypeStruct((SEG, width), f32),
            jax.ShapeDtypeStruct((width // HEAD, 1, SEG), f32),
        ],
        input_output_aliases={len(ins) + i: i for i in range(len(earlier))},
        compiler_params=pltpu.CompilerParams(vmem_limit_bytes=VMEM_LIMIT),
        cost_estimate=pl.CostEstimate(flops=LIGHT, bytes_accessed=LIGHT, transcendentals=0),
        name="forward",
    )(*ins, *earlier)


def finish_kernel(k_ref, v_ref, dk_ref, dv_ref, state_ref, kg_ref, vg_ref):
    key = k_ref[...]
    state = state_ref[0, :HEAD, :]
    norm = state_ref[0, HEAD : HEAD + 1, :]
    lift_grad = mm(halves(v_ref[...]), halves(state.T), NN) + norm
    kg_ref[...] = dk_ref[...] + lift_grad * lifted_slope(key)
    vg_ref[...] = dv_ref[...] + mm(halves(lifted(key)), halves(state), NN)


def columns():
    return pl.BlockSpec((SEG, HEAD), lambda h: (0, h))


def state():
    return pl.BlockSpec((1, ROWS, HEAD), lambda h: (h, 0, 0))


def row(width):
    return pl.BlockSpec((1, 1, width), lambda h: (h, 0, 0))


def per_head(kernel, heads, ins, outs, name):
    width = heads * HEAD
    kinds = {
        "c": (columns(), jax.ShapeDtypeStruct((SEG, width), f32)),
        "s": (state(), jax.ShapeDtypeStruct((heads, ROWS, HEAD), f32)),
        "g": (row(HEAD), jax.ShapeDtypeStruct((heads, 1, HEAD), f32)),
        "t": (
            pl.BlockSpec((HEAD, SEG), lambda h: (h, 0)),
            jax.ShapeDtypeStruct((width, SEG), bf16),
        ),
        "l": (row(SEG), jax.ShapeDtypeStruct((heads, 1, SEG), f32)),
    }
    return pl.pallas_call(
        kernel,
        grid=(heads,),
        in_specs=[kinds[i][0] for i in ins],
        out_specs=[kinds[o][0] for o in outs],
        out_shape=[kinds[o][1] for o in outs],
        compiler_params=pltpu.CompilerParams(vmem_limit_bytes=VMEM_LIMIT),
        cost_estimate=pl.CostEstimate(
            flops=LIGHT, bytes_accessed=LIGHT, transcendentals=0
        ),
        name=name,
    )


def ring(n, step):
    return [(i, (i + step) % n) for i in range(n)]


def grid_sizes():
    heads = lax.axis_size("head")
    return heads, lax.axis_size("ctx") // (2 * heads)


def place():
    xs, zs = grid_sizes()
    at = lax.axis_index("ctx")
    return at // (2 * zs), (at // 2) % zs, at % 2


def core_swap(block):
    n = lax.axis_size("ctx")
    return lax.ppermute(block, "ctx", [(i, i ^ 1) for i in range(n)])


def moved(block, axis, to):
    xs, zs = grid_sizes()
    pairs = []
    for x in range(xs):
        for z in range(zs):
            x_to, z_to = (to(x), z) if axis == "x" else (x, to(z))
            if x_to is not None and z_to is not None:
                for c in range(2):
                    pairs.append(((x * zs + z) * 2 + c, (x_to * zs + z_to) * 2 + c))
    return lax.ppermute(block, "ctx", pairs)


def scan_of_four(block, axis, at, later, beside_first, beside_second):
    near = beside_first(moved(block, axis, lambda i: i ^ 1))
    pair = block + near
    other = beside_second(moved(pair, axis, lambda i: 3 - i))
    counts_near = (at % 2 == 0) if later else (at % 2 == 1)
    counts_other = (at < 2) if later else (at >= 2)
    return jnp.where(counts_near, near, 0.0) + jnp.where(counts_other, other, 0.0), pair + other


def scan_over_ctx(packed, later, work=None):
    xs, zs = grid_sizes()
    x, z, core = place()
    half = packed.shape[0] // 2
    first, second = packed[:half], packed[half:]
    is_first = core == 0
    mine = jnp.where(is_first, first, second)
    theirs = core_swap(jnp.where(is_first, second, first))
    chip = mine + theirs

    def beside_step(i):
        def tie(arrived):
            if work is None:
                return arrived
            done = work(i)
            arrived, *done[:] = lax.optimization_barrier((arrived, *done))
            return arrived

        return tie

    before_z, total_z = scan_of_four(chip, "z", z, later, beside_step(0), beside_step(1))
    before_x, total = scan_of_four(
        total_z, "x", x, later, beside_step(2), beside_step(3)
    )
    outside = before_z + before_x
    counts_other = is_first if later else jnp.logical_not(is_first)
    for_me = outside + jnp.where(counts_other, theirs, 0.0)
    for_other = outside + jnp.where(counts_other, 0.0, mine)
    row = lax.broadcasted_iota(jnp.int32, (1, ROWS, 1), 1)
    totals = jnp.where(row == ROWS - 1, total[:, HEAD + 1 : HEAD + 2, :], 0.0)
    for_me, for_other = for_me + totals, for_other + totals
    swapped = core_swap(for_other)
    low = jnp.where(is_first, for_me, swapped)
    high = jnp.where(is_first, swapped, for_me)
    return jnp.concatenate([low, high], axis=0)


def across(i):
    return 3 - i


def beside(i):
    return i ^ 1


def outgoing(piece, at, first, second):
    far = first(at)
    return jnp.stack([piece(far), piece(second(far))])


def half_scattered(piece, axis, at, first, second, sent=None):
    sent = outgoing(piece, at, first, second) if sent is None else sent
    came = moved(sent, axis, first)
    return piece(at) + came[0], piece(second(at)) + came[1]


def scattered(kept, passed, axis, second):
    return kept + moved(passed, axis, second)


def at_place(pieces, i):
    return lax.dynamic_index_in_dim(pieces, i, 0, keepdims=False)


def on_device(queries, keys, values, gate_logit, out_weight, out_grad):
    heads = gate_logit.shape[0]
    width = heads * HEAD
    hs = lax.axis_size("head")
    head = lax.axis_index("head")
    xs, zs = grid_sizes()
    x, z, core = place()
    rows, cols = out_grad.shape

    half = cols // 2

    def up(block):
        return lax.ppermute(block, "head", ring(hs, 1))

    def down(block):
        return lax.ppermute(block, "head", ring(hs, -1))

    left, right = up(out_grad), down(out_grad)

    gate = jax.nn.sigmoid(gate_logit)
    g = jnp.broadcast_to(gate[:, None, None], (heads, 1, HEAD))

    (packed,) = per_head(update_kernel, heads, "cc", "s", "update")(keys, values)
    forwards = []

    def forward(step):
        if step % 2 == 0:
            forwards[:] = forward_of((step, heads // 2), (queries, keys, values), forwards)
        return forwards

    before = scan_over_ctx(packed, False, forward)
    local_out, lse = forwards
    *mixed, memory_out, lqd = per_head(mix_kernel, heads, "ccsg", "ttcc", "mix")(
        queries, local_out, before, g
    )

    def block_at(distance):
        return (head + hs - distance) % hs

    own_at, left_at, far_at, right_at = (block_at(d) for d in range(4))
    add = functools.partial(round_of, out_weight=out_weight, mixed=mixed, core=core)

    def chip_piece(mine, came, start=0):
        return lambda i: at_place(mine, start + i) + at_place(came, start + i)

    mg, mine_own, send_own = add(None, [out_grad], [own_at])
    came_own = core_swap(send_own)
    own_parts = half_scattered(chip_piece(mine_own, came_own), "z", z, across, beside)
    left, right, *own_parts = lax.optimization_barrier((left, right, *own_parts))
    far_1 = up(left[:MOST, :half]), down(right[:MOST, half:])
    far_2 = up(left[MOST:, :half]), down(right[MOST:, half:])

    mg, mine_sides, send_sides = add(mg, [left, right], [left_at, right_at])
    *far_1, mine_sides, send_sides = lax.optimization_barrier((*far_1, mine_sides, send_sides))
    came_sides = core_swap(send_sides)
    far_places = [2 * far_at, 2 * far_at + 1]
    tail = functools.partial(
        tail_of, places=far_places, out_weight=out_weight, mixed=mixed, core=core,
        whole=(lqd, memory_out, local_out),
    )
    mg_1, *far_sums = tail(0, mg, far_1, before=())
    attended = queries, keys, values

    def backward_ins(part):
        return (*attended, part, local_out, memory_out, lse, before, g)

    sum_own = scattered(*own_parts, "z", beside)
    mg_1, came_sides = lax.optimization_barrier((mg_1, came_sides))
    left_parts = half_scattered(chip_piece(mine_sides, came_sides), "z", z, across, beside)
    right_parts = half_scattered(chip_piece(mine_sides, came_sides, zs), "z", z, beside, across)
    early = backward_of(0, (0, heads), backward_ins(mg_1), (), (), 0)
    *far_2, dq, dk, dv, left_kept, left_passed, right_kept, right_passed, sum_own = (
        lax.optimization_barrier((*far_2, *early, *left_parts, *right_parts, sum_own))
    )
    mg_2, back, mine_far, send_far = tail(1, mg, far_2, before=far_sums)
    sum_left = scattered(left_kept, left_passed, "z", beside)
    sum_right = scattered(right_kept, right_passed, "z", across)
    came_far = core_swap(send_far)
    far_parts = half_scattered(chip_piece(mine_far, came_far), "z", z, across, beside)

    pairs = [(0, heads // 2), (heads // 2, heads // 2)]
    held = {}

    def beside_scan(step):
        if step == 0:
            grads = backward_of(1, pairs[0], backward_ins(mg_2), (dk, dv), [dq], 6)
            held[0] = [*grads, sum_left, sum_right]
        elif step == 1:
            held[1] = list(far_parts)
        elif step == 2:
            grads = backward_of(1, pairs[1], backward_ins(mg_2), (dk, dv), held[0][:3], 6)
            held[2] = [*grads, scattered(*held[1], "z", beside)]
        else:
            held[3] = [outgoing(piece_x, x, across, beside)]
        return held[step]

    def piece_x(i):
        parts = jnp.stack([sum_own, held[0][3], held[2][3], held[0][4]])
        return at_place(parts, (head + hs - i) % hs)

    after = scan_over_ctx(back, True, beside_scan)
    x_parts = half_scattered(piece_x, "x", x, across, beside, held[3][0])
    weight_grad = scattered(*x_parts, "x", beside).T

    key_grad, value_grad = per_head(finish_kernel, heads, "ccccs", "cc", "finish")(
        keys, values, *held[2][1:3], after
    )
    dq = held[2][0]

    gate_sum = jnp.sum(after[:, ROWS - 1, :], axis=-1)
    gate_grad = gate_sum * gate * (1.0 - gate)
    return dq, key_grad, value_grad, weight_grad, gate_grad


def solution(mesh):
    in_specs = (
        P("ctx", "head"),
        P("ctx", "head"),
        P("ctx", "head"),
        P("head"),
        P("head", None),
        P("ctx", "head"),
    )
    out_specs = (P("ctx", "head"), P("ctx", "head"), P("ctx", "head"), P("ctx", "head"), P("head"))
    return jax.shard_map(
        on_device, mesh=mesh, in_specs=in_specs, out_specs=out_specs, check_vma=False
    )
```

profile of v0, /device:TPU:4, one launch (start us, length us, event | category | flops | bytes accessed | tf_op | source)
XLA Modules:
  0.0 256.8 jit_solution(4414320493259410410)
XLA Ops:
  0.6 1.6 collective-permute-start.6
  2.3 1.7 collective-permute-start.7
  3.9 4.7 %update.1 = f32[4,136,128]{2,1,0:T(8,128)} custom-call(f32[1024,512]{1,0:T(8,128)} %k_ref.7, f32[1024,512]{1,0:T(8,128)} %v_ref.7), custom_call_target="tpu_custom_call" | custom-call | flops 65536 | bytes 65536 | tf_op jit(solution)/shard_map/update/pallas_call | solution.py:692
  8.7 1.0 slice_select_fusion
  9.8 1.3 collective-permute-done
  11.1 1.0 fusion.13
  12.1 2.0 collective-permute-start.1
  14.1 6.4 %forward.2 = (f32[1024,512]{1,0:T(8,128)}, f32[4,1,1024]{2,1,0:T(1,128)}) custom-call(f32[1024,512]{1,0:T(8,128)} %refs_0_.7, f32[1024,512]{1,0:T(8,128)} %k_ref.7, f32[1024,512]{1,0:T(8,128)} %v_ref.7), custom_call_target="tpu_custom_call" | custom-call | flops 65536 | bytes 65536 | tf_op jit(solution)/shard_map/forward/pallas_call | solution.py:502
  20.5 2.6 %collective-permute-start.2 = (f32[2,136,128]{2,1,0:T(8,128)S(1)}, f32[2,136,128]{2,1,0:T(8,128)S(1)}, u32[]{:S(2)}, u32[]{:S(2)}) collective-permute-start(f32[2,136,128]{2,1,0:T(8,128)S(1)} %add.378), channel_id=1, source_target_pairs={{0,24},{4,28},{8,16},{12,20},{16,8},{20,12},{24,0},{28,4},{32,56},... | collective-permute-start | bytes 417800 | tf_op jit(solution)/shard_map/ppermute | solution.py:594
  23.1 4.1 %collective-permute-done.2 = f32[2,136,128]{2,1,0:T(8,128)S(1)} collective-permute-done((f32[2,136,128]{2,1,0:T(8,128)S(1)}, f32[2,136,128]{2,1,0:T(8,128)S(1)}, u32[]{:S(2)}, u32[]{:S(2)}) %collective-permute-start.2) | collective-permute-done | bytes 139296 | tf_op jit(solution)/shard_map/ppermute | solution.py:594
  27.3 1.3 collective-permute-start.3
  28.6 6.4 %forward.3 = (f32[1024,512]{1,0:T(8,128)}, f32[4,1,1024]{2,1,0:T(1,128)}) custom-call(f32[1024,512]{1,0:T(8,128)} %refs_0_.7, f32[1024,512]{1,0:T(8,128)} %k_ref.7, f32[1024,512]{1,0:T(8,128)} %v_ref.7, f32[1024,512]{1,0:T(8,128)} %get-tuple-element.92.refs_0_, f32[4,1,1024]{2,1,0:T(1,128)} %get-tuple-element.93.refs_1_), custom_call_target="tpu_custom_call", output_to_operand_aliasing={{0}: (3, {}), {1}: (4, {})} | custom-call | flops 65536 | bytes 65536 | tf_op jit(solution)/shard_map/forward/pallas_call | solution.py:502
  35.2 4.9 %collective-permute-done.4 = f32[2,136,128]{2,1,0:T(8,128)S(1)} collective-permute-done((f32[2,136,128]{2,1,0:T(8,128)S(1)}, f32[2,136,128]{2,1,0:T(8,128)S(1)}, u32[]{:S(2)}, u32[]{:S(2)}) %collective-permute-start.4) | collective-permute-done | bytes 139296 | tf_op jit(solution)/shard_map/ppermute | solution.py:594
  40.4 0.6 pad_add_fusion.at_ref
  41.0 0.7 collective-permute-done.5
  41.8 0.7 pad_maximum_fusion.7.mem_ref.refs_7_
  42.5 0.6 broadcast_in_dim.59.g_ref.refs_8_
  43.2 5.8 %mix.1 = (bf16[512,1024]{1,0:T(8,128)(2,1)}, bf16[512,1024]{1,0:T(8,128)(2,1)}, f32[1024,512]{1,0:T(8,128)}, f32[1024,512]{1,0:T(8,128)}) custom-call(f32[1024,512]{1,0:T(8,128)} %refs_0_.7, f32[1024,512]{1,0:T(8,128)} %get-tuple-element.99.local_ref.refs_7_.refs_4_, f32[4,136,128]{2,1,0:T(8,128)} %pad_maximum_fusion.7.mem_ref.refs_7_, ...), custom_call_target="tpu_custom_call" | custom-call | flops 65536 | bytes 65536 | tf_op jit(solution)/shard_map/mix/pallas_call | solution.py:702
  49.0 12.1 %round.2 = (f32[1024,512]{1,0:T(8,128)}, f32[4,512,128]{2,1,0:T(8,128)}, f32[4,512,128]{2,1,0:T(8,128)}) custom-call(s32[2]{0:T(128)} %pad_add_fusion.at_ref, f32[1024,1024]{1,0:T(8,128)} %refs_0_.4, f32[512,4096]{1,0:T(8,128)} %refs_4_.5, bf16[512,1024]{1,0:T(8,128)(2,1)} %get-tuple-element.101.refs_2_.refs_5_.refs_8_, ...), custom_call_target="tpu_custom_call" | custom-call | flops 65536 | bytes 65536 | tf_op jit(solution)/shard_map/round/pallas_call | solution.py:365
  61.1 0.2 collective-permute-start.8
  61.3 2.7 %collective-permute-done.8 = f32[4,512,128]{2,1,0:T(8,128)S(1)} collective-permute-done((f32[4,512,128]{2,1,0:T(8,128)}, f32[4,512,128]{2,1,0:T(8,128)S(1)}, u32[]{:S(2)}, u32[]{:S(2)}) %collective-permute-start.8) | collective-permute-done | bytes 1048608 | tf_op jit(solution)/shard_map/ppermute | solution.py:582
  64.0 1.1 dynamic-slice_add_fusion.7
  65.2 2.6 %collective-permute-start.9 = (f32[2,512,128]{2,1,0:T(8,128)S(1)}, f32[2,512,128]{2,1,0:T(8,128)S(1)}, u32[]{:S(2)}, u32[]{:S(2)}) collective-permute-start(f32[2,512,128]{2,1,0:T(8,128)S(1)} %pad_maximum_fusion.1), channel_id=1, source_target_pairs={{0,24},{4,28},{8,16},{12,20},{16,8},{20,12},{24,0},{28,4},{32,56},... | collective-permute-start | bytes 1572872 | tf_op jit(solution)/shard_map/ppermute | solution.py:594
  67.8 12.7 %collective-permute-done.9 = f32[2,512,128]{2,1,0:T(8,128)S(1)} collective-permute-done((f32[2,512,128]{2,1,0:T(8,128)S(1)}, f32[2,512,128]{2,1,0:T(8,128)S(1)}, u32[]{:S(2)}, u32[]{:S(2)}) %collective-permute-start.9) | collective-permute-done | bytes 524320 | tf_op jit(solution)/shard_map/ppermute | solution.py:594
  80.4 0.8 fusion.10
  81.2 13.4 %collective-permute-done.6.refs_1_ = f32[1024,1024]{1,0:T(8,128)} collective-permute-done((f32[1024,1024]{1,0:T(8,128)}, f32[1024,1024]{1,0:T(8,128)}, u32[]{:S(2)}, u32[]{:S(2)}) %collective-permute-start.6) | collective-permute-done | bytes 4194336 | tf_op jit(solution)/shard_map/ppermute | solution.py:682
  94.6 2.7 %fusion.17 = (f32[512,512]{1,0:T(8,128)S(1)}, f32[512,512]{1,0:T(8,128)}) fusion(f32[1024,1024]{1,0:T(8,128)} %collective-permute-done.6.refs_1_), kind=kLoop, calls=%fused_computation.69 | loop fusion | bytes 4194304 | tf_op jit(solution)/shard_map/slice | solution.py:719
  97.4 1.6 collective-permute-start.12
  99.0 3.0 %fusion.16 = (f32[512,512]{1,0:T(8,128)}, f32[512,512]{1,0:T(8,128)}) fusion(f32[1024,1024]{1,0:T(8,128)} %collective-permute-done.7.refs_2_), kind=kLoop, calls=%fused_computation.68 | loop fusion | bytes 4194304 | tf_op jit(solution)/shard_map/slice | solution.py:719
  102.0 1.7 collective-permute-start.13
  103.6 0.7 add_add_fusion.2
  104.3 21.3 %round.3 = (f32[1024,512]{1,0:T(8,128)}, f32[8,512,128]{2,1,0:T(8,128)}, f32[8,512,128]{2,1,0:T(8,128)}) custom-call(s32[3]{0:T(128)} %get-tuple-element.205.at_ref, f32[1024,512]{1,0:T(8,128)} %get-tuple-element.103.refs_0_, f32[1024,1024]{1,0:T(8,128)} %collective-permute-done.6.refs_1_, ...), custom_call_target="tpu_custom_call", output_to_operand_aliasing={{0}: (1, {})} | custom-call | flops 65536 | bytes 65536 | tf_op jit(solution)/shard_map/round/pallas_call | solution.py:365
  125.7 1.1 collective-permute-start.10
  126.9 2.2 collective-permute-start.11
  129.1 10.3 %tail.2 = (f32[512,512]{1,0:T(8,128)}, f32[4,136,128]{2,1,0:T(8,128)}, f32[4,512,128]{2,1,0:T(8,128)}, f32[4,512,128]{2,1,0:T(8,128)}) custom-call(s32[3]{0:T(128)} %get-tuple-element.204.at_ref, f32[1024,512]{1,0:T(8,128)} %get-tuple-element.108.refs_0_, f32[512,512]{1,0:T(8,128)} %copy-done.3, f32[512,512]{1,0:T(8,128)} %copy-done.4, f32[512,4096]{1,0:T(8,128)} %refs_4_.5, ...), custom_call_target="tpu_custom_call" | custom-call | flops 65536 | bytes 65536 | tf_op jit(solution)/shard_map/tail/pallas_call | solution.py:395
  139.4 1.3 dynamic-slice_add_fusion.3
  140.7 0.8 pad_maximum_fusion.2
  141.5 4.1 %collective-permute-start.15 = (f32[2,512,128]{2,1,0:T(8,128)}, f32[2,512,128]{2,1,0:T(8,128)}, u32[]{:S(2)}, u32[]{:S(2)}) collective-permute-start(f32[2,512,128]{2,1,0:T(8,128)} %pad_maximum_fusion.2), channel_id=1, source_target_pairs={{0,24},{4,28},{8,16},{12,20},{16,8},{20,12},{24,0},{28,4},{32,56},... | collective-permute-start | bytes 1572872 | tf_op jit(solution)/shard_map/ppermute | solution.py:594
  145.7 2.0 collective-permute-start.17
  147.7 17.1 %collective-permute-done.17 = f32[512,128]{1,0:T(8,128)S(1)} collective-permute-done((f32[512,128]{1,0:T(8,128)}, f32[512,128]{1,0:T(8,128)S(1)}, u32[]{:S(2)}, u32[]{:S(2)}) %collective-permute-start.17) | collective-permute-done | bytes 262176 | tf_op jit(solution)/shard_map/ppermute | solution.py:594
  164.9 8.9 %backward.3 = (f32[1024,512]{1,0:T(8,128)}, f32[512,512]{1,0:T(8,128)}, f32[512,512]{1,0:T(8,128)}) custom-call(f32[1024,512]{1,0:T(8,128)} %refs_0_.7, f32[1024,512]{1,0:T(8,128)} %k_ref.7, f32[1024,512]{1,0:T(8,128)} %v_ref.7, f32[512,512]{1,0:T(8,128)} %get-tuple-element.117.refs_3_, f32[1024,512]{1,0:T(8,128)} %get-tuple-element.99.local_ref.refs_7_.refs_4_, ...), custom_call_target="tpu_custom_call" | custom-call | flops 65536 | bytes 65536 | tf_op jit(solution)/shard_map/backward/pallas_call | solution.py:479
  173.8 2.5 fusion.6
  176.3 10.8 %tail.3 = (f32[512,512]{1,0:T(8,128)}, f32[4,136,128]{2,1,0:T(8,128)}, f32[4,512,128]{2,1,0:T(8,128)}, f32[4,512,128]{2,1,0:T(8,128)}) custom-call(s32[3]{0:T(128)} %get-tuple-element.204.at_ref, f32[1024,512]{1,0:T(8,128)} %get-tuple-element.108.refs_0_, f32[512,512]{1,0:T(8,128)} %collective-permute-done.10.refs_1_, ...), custom_call_target="tpu_custom_call" | custom-call | flops 65536 | bytes 65536 | tf_op jit(solution)/shard_map/tail/pallas_call | solution.py:395
  187.2 2.9 %collective-permute-done.23 = f32[4,512,128]{2,1,0:T(8,128)S(1)} collective-permute-done((f32[4,512,128]{2,1,0:T(8,128)}, f32[4,512,128]{2,1,0:T(8,128)S(1)}, u32[]{:S(2)}, u32[]{:S(2)}) %collective-permute-start.23) | collective-permute-done | bytes 1048608 | tf_op jit(solution)/shard_map/ppermute | solution.py:582
  190.1 1.1 dynamic-slice_add_fusion.1
  191.2 0.3 collective-permute-start.24
  191.7 3.1 %collective-permute-start.21 = (f32[512,128]{1,0:T(8,128)S(1)}, f32[512,128]{1,0:T(8,128)S(1)}, u32[]{:S(2)}, u32[]{:S(2)}) collective-permute-start(f32[512,128]{1,0:T(8,128)S(1)} %copy-done.7), channel_id=1, source_target_pairs={{0,24},{4,28},{8,16},{12,20},{16,8},{20,12},{24,0},{28,4},{32,56},... | collective-permute-start | bytes 786440 | tf_op jit(solution)/shard_map/ppermute | solution.py:594
  194.8 2.1 collective-permute-start.19
  196.9 8.5 %backward.4 = (f32[1024,512]{1,0:T(8,128)}, f32[1024,512]{1,0:T(8,128)}, f32[1024,512]{1,0:T(8,128)}) custom-call(f32[1024,512]{1,0:T(8,128)} %refs_0_.7, f32[1024,512]{1,0:T(8,128)} %k_ref.7, f32[1024,512]{1,0:T(8,128)} %v_ref.7, f32[512,512]{1,0:T(8,128)} %get-tuple-element.132.refs_3_, ...), custom_call_target="tpu_custom_call", output_to_operand_aliasing={{0}: (11, {})} | custom-call | flops 65536 | bytes 21600000 | tf_op jit(solution)/shard_map/backward/pallas_call | solution.py:479
  205.4 6.7 %collective-permute-done.21 = f32[512,128]{1,0:T(8,128)S(1)} collective-permute-done((f32[512,128]{1,0:T(8,128)S(1)}, f32[512,128]{1,0:T(8,128)S(1)}, u32[]{:S(2)}, u32[]{:S(2)}) %collective-permute-start.21) | collective-permute-done | bytes 262176 | tf_op jit(solution)/shard_map/ppermute | solution.py:594
  212.2 0.4 collective-permute-start.22
  212.6 1.1 fusion.4
  213.7 4.9 %collective-permute-done.22 = f32[2,136,128]{2,1,0:T(8,128)S(1)} collective-permute-done((f32[2,136,128]{2,1,0:T(8,128)S(1)}, f32[2,136,128]{2,1,0:T(8,128)S(1)}, u32[]{:S(2)}, u32[]{:S(2)}) %collective-permute-start.22) | collective-permute-done | bytes 139296 | tf_op jit(solution)/shard_map/ppermute | solution.py:594
  218.6 1.5 collective-permute-start.25
  220.1 8.5 %backward.5 = (f32[1024,512]{1,0:T(8,128)}, f32[1024,512]{1,0:T(8,128)}, f32[1024,512]{1,0:T(8,128)}) custom-call(f32[1024,512]{1,0:T(8,128)} %refs_0_.7, f32[1024,512]{1,0:T(8,128)} %k_ref.7, f32[1024,512]{1,0:T(8,128)} %v_ref.7, f32[512,512]{1,0:T(8,128)} %get-tuple-element.132.refs_3_, ...), custom_call_target="tpu_custom_call", output_to_operand_aliasing={{0}: (11, {}), {1}: (12, {}), {2}: (13, {})} | custom-call | flops 65536 | bytes 21600000 | tf_op jit(solution)/shard_map/backward/pallas_call | solution.py:479
  229.0 5.6 %collective-permute-done.27 = f32[2,136,128]{2,1,0:T(8,128)S(1)} collective-permute-done((f32[2,136,128]{2,1,0:T(8,128)S(1)}, f32[2,136,128]{2,1,0:T(8,128)S(1)}, u32[]{:S(2)}, u32[]{:S(2)}) %collective-permute-start.27) | collective-permute-done | bytes 139296 | tf_op jit(solution)/shard_map/ppermute | solution.py:594
  234.8 1.3 collective-permute-done.28
  236.2 8.9 %collective-permute-done.29 = f32[2,512,128]{2,1,0:T(8,128)S(1)} collective-permute-done((f32[2,512,128]{2,1,0:T(8,128)S(1)}, f32[2,512,128]{2,1,0:T(8,128)S(1)}, u32[]{:S(2)}, u32[]{:S(2)}) %collective-permute-start.29) | collective-permute-done | bytes 524320 | tf_op jit(solution)/shard_map/ppermute | solution.py:594
  245.1 2.7 %collective-permute-start.30 = (f32[512,128]{1,0:T(8,128)S(1)}, f32[512,128]{1,0:T(8,128)S(1)}, u32[]{:S(2)}, u32[]{:S(2)}) collective-permute-start(f32[512,128]{1,0:T(8,128)S(1)} %fusion), channel_id=1, source_target_pairs={{0,32},{4,36},{8,40},{12,44},{16,48},{20,52},{24,56},{28,60},{32,0... | collective-permute-start | bytes 786440 | tf_op jit(solution)/shard_map/ppermute | solution.py:594
  247.8 0.7 pad_maximum_fusion.6.state_ref
  248.5 6.8 %finish.1 = (f32[1024,512]{1,0:T(8,128)}, f32[1024,512]{1,0:T(8,128)}) custom-call(f32[1024,512]{1,0:T(8,128)} %k_ref.7, f32[1024,512]{1,0:T(8,128)} %v_ref.7, f32[1024,512]{1,0:T(8,128)} %get-tuple-element.156.dk_ref, f32[1024,512]{1,0:T(8,128)} %get-tuple-element.157.dv_ref, f32[4,136,128]{2,1,0:T(8,128)} %pad_maximum_fusion.6.state_ref), custom_call_target="tpu_custom_call" | custom-call | flops 65536 | bytes 65536 | tf_op jit(solution)/shard_map/finish/pallas_call | solution.py:774
  255.3 0.1 fusion.15
  255.4 0.5 subtract_multiply_fusion
  256.0 0.8 copy.18
  (75 shorter events, 1.9 us)
Async XLA Ops:
  0.6 94.0 %collective-permute-start.6 = (f32[1024,1024]{1,0:T(8,128)}, f32[1024,1024]{1,0:T(8,128)}, u32[]{:S(2)}, u32[]{:S(2)}) collective-permute-start(f32[1024,1024]{1,0:T(8,128)} %refs_0_.4), channel_id=1, source_target_pairs={{0,1},{1,2},{2,3},{3,0},{4,5},{5,6},{6,7},{7,4},{8,9},{9,10},{10,1... | collective-permute-start | bytes 12582920 | tf_op jit(solution)/shard_map/ppermute | solution.py:682
  2.3 92.3 %collective-permute-start.7 = (f32[1024,1024]{1,0:T(8,128)}, f32[1024,1024]{1,0:T(8,128)}, u32[]{:S(2)}, u32[]{:S(2)}) collective-permute-start(f32[1024,1024]{1,0:T(8,128)} %refs_0_.4), channel_id=1, source_target_pairs={{0,3},{1,0},{2,1},{3,2},{4,7},{5,4},{6,5},{7,6},{8,11},{9,8},{10,9... | collective-permute-start | bytes 12582920 | tf_op jit(solution)/shard_map/ppermute | solution.py:685
  9.7 1.4 collective-permute-start
  12.1 8.4 %collective-permute-start.1 = (f32[2,136,128]{2,1,0:T(8,128)S(1)}, f32[2,136,128]{2,1,0:T(8,128)S(1)}, u32[]{:S(2)}, u32[]{:S(2)}) collective-permute-start(f32[2,136,128]{2,1,0:T(8,128)S(1)} %fusion.13), channel_id=1, source_target_pairs={{0,8},{4,12},{8,0},{12,4},{16,24},{20,28},{24,16},{28,20},{32,40},... | collective-permute-start | bytes 417800 | tf_op jit(solution)/shard_map/ppermute | solution.py:594
  20.5 6.7 %collective-permute-start.2 = (f32[2,136,128]{2,1,0:T(8,128)S(1)}, f32[2,136,128]{2,1,0:T(8,128)S(1)}, u32[]{:S(2)}, u32[]{:S(2)}) collective-permute-start(f32[2,136,128]{2,1,0:T(8,128)S(1)} %add.378), channel_id=1, source_target_pairs={{0,24},{4,28},{8,16},{12,20},{16,8},{20,12},{24,0},{28,4},{32,56},... | collective-permute-start | bytes 417800 | tf_op jit(solution)/shard_map/ppermute | solution.py:594
  27.3 12.9 %copy-start = (f32[4,136,128]{2,1,0:T(8,128)S(1)}, f32[4,136,128]{2,1,0:T(8,128)}, u32[]{:S(2)}) copy-start(f32[4,136,128]{2,1,0:T(8,128)} %update.1) | copy-start | bytes 835588
  27.3 13.1 %copy-start.8 = (f32[4]{0:T(128)S(1)}, f32[4]{0:T(128)}, u32[]{:S(2)}) copy-start(f32[4]{0:T(128)} %param.9) | copy-start | bytes 52
  27.3 7.7 %collective-permute-start.3 = (f32[2,136,128]{2,1,0:T(8,128)S(1)}, f32[2,136,128]{2,1,0:T(8,128)S(1)}, u32[]{:S(2)}, u32[]{:S(2)}) collective-permute-start(f32[2,136,128]{2,1,0:T(8,128)S(1)} %add.379), channel_id=1, source_target_pairs={{0,32},{4,36},{8,40},{12,44},{16,48},{20,52},{24,56},{28,60},{32,0... | collective-permute-start | bytes 417800 | tf_op jit(solution)/shard_map/ppermute | solution.py:594
  35.0 5.1 %collective-permute-start.4 = (f32[2,136,128]{2,1,0:T(8,128)S(1)}, f32[2,136,128]{2,1,0:T(8,128)S(1)}, u32[]{:S(2)}, u32[]{:S(2)}) collective-permute-start(f32[2,136,128]{2,1,0:T(8,128)S(1)} %add.380), channel_id=1, source_target_pairs={{0,96},{4,100},{8,104},{12,108},{16,112},{20,116},{24,120},{28,124... | collective-permute-start | bytes 417800 | tf_op jit(solution)/shard_map/ppermute | solution.py:594
  40.3 1.4 collective-permute-start.5
  61.1 19.4 %copy-start.6 = (f32[4,512,128]{2,1,0:T(8,128)S(1)}, f32[4,512,128]{2,1,0:T(8,128)}, u32[]{:S(2)}) copy-start(f32[4,512,128]{2,1,0:T(8,128)} %get-tuple-element.104) | copy-start | bytes 3145732
  61.1 3.0 %collective-permute-start.8 = (f32[4,512,128]{2,1,0:T(8,128)}, f32[4,512,128]{2,1,0:T(8,128)S(1)}, u32[]{:S(2)}, u32[]{:S(2)}) collective-permute-start(f32[4,512,128]{2,1,0:T(8,128)} %get-tuple-element.105), channel_id=1, source_target_pairs={{0,4},{4,0},{8,12},{12,8},{16,20},{20,16},{24,28},{28,24},{32,36},... | collective-permute-start | bytes 3145736 | tf_op jit(solution)/shard_map/ppermute | solution.py:582
  65.2 15.3 %collective-permute-start.9 = (f32[2,512,128]{2,1,0:T(8,128)S(1)}, f32[2,512,128]{2,1,0:T(8,128)S(1)}, u32[]{:S(2)}, u32[]{:S(2)}) collective-permute-start(f32[2,512,128]{2,1,0:T(8,128)S(1)} %pad_maximum_fusion.1), channel_id=1, source_target_pairs={{0,24},{4,28},{8,16},{12,20},{16,8},{20,12},{24,0},{28,4},{32,56},... | collective-permute-start | bytes 1572872 | tf_op jit(solution)/shard_map/ppermute | solution.py:594
  97.4 28.2 %collective-permute-start.12 = (f32[512,512]{1,0:T(8,128)S(1)}, f32[512,512]{1,0:T(8,128)S(1)}, u32[]{:S(2)}, u32[]{:S(2)}) collective-permute-start(f32[512,512]{1,0:T(8,128)S(1)} %get-tuple-element.188), channel_id=1, source_target_pairs={{0,1},{1,2},{2,3},{3,0},{4,5},{5,6},{6,7},{7,4},{8,9},{9,10},{10,1... | collective-permute-start | bytes 3145736 | tf_op jit(solution)/shard_map/ppermute | solution.py:682
  102.0 23.6 %collective-permute-start.13 = (f32[512,512]{1,0:T(8,128)}, f32[512,512]{1,0:T(8,128)S(1)}, u32[]{:S(2)}, u32[]{:S(2)}) collective-permute-start(f32[512,512]{1,0:T(8,128)} %get-tuple-element.186), channel_id=1, source_target_pairs={{0,3},{1,0},{2,1},{3,2},{4,7},{5,4},{6,5},{7,6},{8,11},{9,8},{10,9... | collective-permute-start | bytes 3145736 | tf_op jit(solution)/shard_map/ppermute | solution.py:685
  125.6 3.5 %copy-start.3 = (f32[512,512]{1,0:T(8,128)}, f32[512,512]{1,0:T(8,128)S(1)}, u32[]{:S(2)}) copy-start(f32[512,512]{1,0:T(8,128)S(1)} %collective-permute-done.12.refs_1_) | copy-start | bytes 3145732
  125.6 3.5 %copy-start.4 = (f32[512,512]{1,0:T(8,128)}, f32[512,512]{1,0:T(8,128)S(1)}, u32[]{:S(2)}) copy-start(f32[512,512]{1,0:T(8,128)S(1)} %collective-permute-done.13.refs_2_) | copy-start | bytes 3145732
  125.6 13.8 %collective-permute-start.14 = (f32[8,512,128]{2,1,0:T(8,128)}, f32[8,512,128]{2,1,0:T(8,128)}, u32[]{:S(2)}, u32[]{:S(2)}) collective-permute-start(f32[8,512,128]{2,1,0:T(8,128)} %get-tuple-element.116), channel_id=1, source_target_pairs={{0,4},{4,0},{8,12},{12,8},{16,20},{20,16},{24,28},{28,24},{32,36},... | collective-permute-start | bytes 6291464 | tf_op jit(solution)/shard_map/ppermute | solution.py:582
  125.7 50.5 %collective-permute-start.10 = (f32[512,512]{1,0:T(8,128)}, f32[512,512]{1,0:T(8,128)}, u32[]{:S(2)}, u32[]{:S(2)}) collective-permute-start(f32[512,512]{1,0:T(8,128)} %get-tuple-element.189), channel_id=1, source_target_pairs={{0,1},{1,2},{2,3},{3,0},{4,5},{5,6},{6,7},{7,4},{8,9},{9,10},{10,1... | collective-permute-start | bytes 3145736 | tf_op jit(solution)/shard_map/ppermute | solution.py:682
  126.9 49.4 %collective-permute-start.11 = (f32[512,512]{1,0:T(8,128)}, f32[512,512]{1,0:T(8,128)}, u32[]{:S(2)}, u32[]{:S(2)}) collective-permute-start(f32[512,512]{1,0:T(8,128)} %get-tuple-element.187), channel_id=1, source_target_pairs={{0,3},{1,0},{2,1},{3,2},{4,7},{5,4},{6,5},{7,6},{8,11},{9,8},{10,9... | collective-permute-start | bytes 3145736 | tf_op jit(solution)/shard_map/ppermute | solution.py:685
  129.1 10.3 %copy-start.2 = (f32[8,512,128]{2,1,0:T(8,128)S(1)}, f32[8,512,128]{2,1,0:T(8,128)}, u32[]{:S(2)}) copy-start(f32[8,512,128]{2,1,0:T(8,128)} %get-tuple-element.122) | copy-start | bytes 6291460
  141.5 32.3 %collective-permute-start.15 = (f32[2,512,128]{2,1,0:T(8,128)}, f32[2,512,128]{2,1,0:T(8,128)}, u32[]{:S(2)}, u32[]{:S(2)}) collective-permute-start(f32[2,512,128]{2,1,0:T(8,128)} %pad_maximum_fusion.2), channel_id=1, source_target_pairs={{0,24},{4,28},{8,16},{12,20},{16,8},{20,12},{24,0},{28,4},{32,56},... | collective-permute-start | bytes 1572872 | tf_op jit(solution)/shard_map/ppermute | solution.py:594
  145.6 28.2 %collective-permute-start.16 = (f32[2,512,128]{2,1,0:T(8,128)S(1)}, f32[2,512,128]{2,1,0:T(8,128)}, u32[]{:S(2)}, u32[]{:S(2)}) collective-permute-start(f32[2,512,128]{2,1,0:T(8,128)S(1)} %pad_maximum_fusion.3), channel_id=1, source_target_pairs={{0,8},{4,12},{8,0},{12,4},{16,24},{20,28},{24,16},{28,20},{32,40},... | collective-permute-start | bytes 1572872 | tf_op jit(solution)/shard_map/ppermute | solution.py:594
  145.7 19.1 %collective-permute-start.17 = (f32[512,128]{1,0:T(8,128)}, f32[512,128]{1,0:T(8,128)S(1)}, u32[]{:S(2)}, u32[]{:S(2)}) collective-permute-start(f32[512,128]{1,0:T(8,128)} %get-tuple-element.125), channel_id=1, source_target_pairs={{0,8},{4,12},{8,0},{12,4},{16,24},{20,28},{24,16},{28,20},{32,40},... | collective-permute-start | bytes 786440 | tf_op jit(solution)/shard_map/ppermute | solution.py:594
  187.1 4.4 %copy-start.1 = (f32[4,136,128]{2,1,0:T(8,128)S(1)}, f32[4,136,128]{2,1,0:T(8,128)}, u32[]{:S(2)}) copy-start(f32[4,136,128]{2,1,0:T(8,128)} %get-tuple-element.131) | copy-start | bytes 835588
  187.1 4.6 %copy-start.7 = (f32[512,128]{1,0:T(8,128)S(1)}, f32[512,128]{1,0:T(8,128)}, u32[]{:S(2)}) copy-start(f32[512,128]{1,0:T(8,128)} %get-tuple-element.142) | copy-start | bytes 786436
  187.2 3.0 %collective-permute-start.23 = (f32[4,512,128]{2,1,0:T(8,128)}, f32[4,512,128]{2,1,0:T(8,128)S(1)}, u32[]{:S(2)}, u32[]{:S(2)}) collective-permute-start(f32[4,512,128]{2,1,0:T(8,128)} %get-tuple-element.145), channel_id=1, source_target_pairs={{0,4},{4,0},{8,12},{12,8},{16,20},{20,16},{24,28},{28,24},{32,36},... | collective-permute-start | bytes 3145736 | tf_op jit(solution)/shard_map/ppermute | solution.py:582
  191.2 21.4 %collective-permute-start.24 = (f32[2,512,128]{2,1,0:T(8,128)S(1)}, f32[2,512,128]{2,1,0:T(8,128)}, u32[]{:S(2)}, u32[]{:S(2)}) collective-permute-start(f32[2,512,128]{2,1,0:T(8,128)S(1)} %pad_maximum_fusion.4), channel_id=1, source_target_pairs={{0,24},{4,28},{8,16},{12,20},{16,8},{20,12},{24,0},{28,4},{32,56},... | collective-permute-start | bytes 1572872 | tf_op jit(solution)/shard_map/ppermute | solution.py:594
  191.6 3.2 %collective-permute-start.18 = (f32[2,136,128]{2,1,0:T(8,128)S(1)}, f32[2,136,128]{2,1,0:T(8,128)S(1)}, u32[]{:S(2)}, u32[]{:S(2)}) collective-permute-start(f32[2,136,128]{2,1,0:T(8,128)S(1)} %slice_select_fusion.2), channel_id=1, source_target_pairs={{0,4},{4,0},{8,12},{12,8},{16,20},{20,16},{24,28},{28,24},{32,36},... | collective-permute-start | bytes 417800 | tf_op jit(solution)/shard_map/ppermute | solution.py:582
  191.7 20.4 %collective-permute-start.21 = (f32[512,128]{1,0:T(8,128)S(1)}, f32[512,128]{1,0:T(8,128)S(1)}, u32[]{:S(2)}, u32[]{:S(2)}) collective-permute-start(f32[512,128]{1,0:T(8,128)S(1)} %copy-done.7), channel_id=1, source_target_pairs={{0,24},{4,28},{8,16},{12,20},{16,8},{20,12},{24,0},{28,4},{32,56},... | collective-permute-start | bytes 786440 | tf_op jit(solution)/shard_map/ppermute | solution.py:594
  194.8 17.4 %collective-permute-start.20 = (f32[512,128]{1,0:T(8,128)}, f32[512,128]{1,0:T(8,128)S(1)}, u32[]{:S(2)}, u32[]{:S(2)}) collective-permute-start(f32[512,128]{1,0:T(8,128)} %get-tuple-element.140), channel_id=1, source_target_pairs={{0,8},{4,12},{8,0},{12,4},{16,24},{20,28},{24,16},{28,20},{32,40},... | collective-permute-start | bytes 786440 | tf_op jit(solution)/shard_map/ppermute | solution.py:594
  194.8 17.4 %collective-permute-start.19 = (f32[2,136,128]{2,1,0:T(8,128)S(1)}, f32[2,136,128]{2,1,0:T(8,128)S(1)}, u32[]{:S(2)}, u32[]{:S(2)}) collective-permute-start(f32[2,136,128]{2,1,0:T(8,128)S(1)} %fusion.12), channel_id=1, source_target_pairs={{0,8},{4,12},{8,0},{12,4},{16,24},{20,28},{24,16},{28,20},{32,40},... | collective-permute-start | bytes 417800 | tf_op jit(solution)/shard_map/ppermute | solution.py:594
  205.4 7.2 %copy-start.5 = (f32[4,512,128]{2,1,0:T(8,128)S(1)}, f32[4,512,128]{2,1,0:T(8,128)}, u32[]{:S(2)}) copy-start(f32[4,512,128]{2,1,0:T(8,128)} %get-tuple-element.144) | copy-start | bytes 3145732
  212.2 6.3 %collective-permute-start.22 = (f32[2,136,128]{2,1,0:T(8,128)S(1)}, f32[2,136,128]{2,1,0:T(8,128)S(1)}, u32[]{:S(2)}, u32[]{:S(2)}) collective-permute-start(f32[2,136,128]{2,1,0:T(8,128)S(1)} %add.434), channel_id=1, source_target_pairs={{0,24},{4,28},{8,16},{12,20},{16,8},{20,12},{24,0},{28,4},{32,56},... | collective-permute-start | bytes 417800 | tf_op jit(solution)/shard_map/ppermute | solution.py:594
  218.6 10.0 %collective-permute-start.26 = (f32[512,128]{1,0:T(8,128)S(1)}, f32[512,128]{1,0:T(8,128)S(1)}, u32[]{:S(2)}, u32[]{:S(2)}) collective-permute-start(f32[512,128]{1,0:T(8,128)S(1)} %get-tuple-element.154), channel_id=1, source_target_pairs={{0,8},{4,12},{8,0},{12,4},{16,24},{20,28},{24,16},{28,20},{32,40},... | collective-permute-start | bytes 786440 | tf_op jit(solution)/shard_map/ppermute | solution.py:594
  218.6 10.1 %collective-permute-start.25 = (f32[2,136,128]{2,1,0:T(8,128)S(1)}, f32[2,136,128]{2,1,0:T(8,128)S(1)}, u32[]{:S(2)}, u32[]{:S(2)}) collective-permute-start(f32[2,136,128]{2,1,0:T(8,128)S(1)} %add.443), channel_id=1, source_target_pairs={{0,32},{4,36},{8,40},{12,44},{16,48},{20,52},{24,56},{28,60},{32,0... | collective-permute-start | bytes 417800 | tf_op jit(solution)/shard_map/ppermute | solution.py:594
  228.7 5.8 %collective-permute-start.27 = (f32[2,136,128]{2,1,0:T(8,128)S(1)}, f32[2,136,128]{2,1,0:T(8,128)S(1)}, u32[]{:S(2)}, u32[]{:S(2)}) collective-permute-start(f32[2,136,128]{2,1,0:T(8,128)S(1)} %add.446), channel_id=1, source_target_pairs={{0,96},{4,100},{8,104},{12,108},{16,112},{20,116},{24,120},{28,124... | collective-permute-start | bytes 417800 | tf_op jit(solution)/shard_map/ppermute | solution.py:594
  234.5 10.5 %collective-permute-start.29 = (f32[2,512,128]{2,1,0:T(8,128)S(1)}, f32[2,512,128]{2,1,0:T(8,128)S(1)}, u32[]{:S(2)}, u32[]{:S(2)}) collective-permute-start(f32[2,512,128]{2,1,0:T(8,128)S(1)} %pad_maximum_fusion.5), channel_id=1, source_target_pairs={{0,96},{4,100},{8,104},{12,108},{16,112},{20,116},{24,120},{28,124... | collective-permute-start | bytes 1572872 | tf_op jit(solution)/shard_map/ppermute | solution.py:594
  234.6 1.4 collective-permute-start.28
  245.1 10.8 %collective-permute-start.30 = (f32[512,128]{1,0:T(8,128)S(1)}, f32[512,128]{1,0:T(8,128)S(1)}, u32[]{:S(2)}, u32[]{:S(2)}) collective-permute-start(f32[512,128]{1,0:T(8,128)S(1)} %fusion), channel_id=1, source_target_pairs={{0,32},{4,36},{8,40},{12,44},{16,48},{20,52},{24,56},{28,60},{32,0... | collective-permute-start | bytes 786440 | tf_op jit(solution)/shard_map/ppermute | solution.py:594
where the time goes:
time: 257 us
  Pallas kernels  110 us (43%)
  waiting for transfers between devices  87.3 us (34%)
  starting transfers between devices  35.5 us (14%)
  other arithmetic  14.9 us (6%)
  local copies, waits for them, and re-layouts  7.34 us (3%)
    ppermute x18, waiting for transfers between devices, moved(): return lax.ppermute(block, 'ctx', pairs)  64.9 us
    pallas_call x2, Pallas kernels, round_of(): pl.pallas_call(functools.partial(block_kernel, blocks=n, added=len(acc),...  33.4 us
    pallas_call x3, Pallas kernels, backward_of(): pl.pallas_call(functools.partial(backward_kernel, first=second * MOST), g...  25.9 us
    ppermute x18, starting transfers between devices, moved(): return lax.ppermute(block, 'ctx', pairs)  24.9 us
    pallas_call x2, Pallas kernels, tail_of(): pl.pallas_call(tail_kernel, grid_spec=pltpu.PrefetchScalarGridSpec(num_sc...  21.1 us
    ppermute x3, waiting for transfers between devices, up(): return lax.ppermute(block, 'head', ring(hs, 1))  13.4 us
    pallas_call x2, Pallas kernels, forward_of(): pl.pallas_call(forward_kernel, grid=(count,), in_specs=[column] * 3 + [pl...  12.8 us
    ppermute x7, waiting for transfers between devices, core_swap(): return lax.ppermute(block, 'ctx', [(i, i ^ 1) for i in range(n)])  8.96 us
  transfers between devices with their start and end apart: 31, of which 14 were waited for; matrix products, arithmetic and copies ran while one was open for 7% of the time, Pallas kernels for 39%

commit v1 on v0

--- a/solution.py
+++ b/solution.py
@@ -595,9 +595,9 @@
 
 
 def scan_of_four(block, axis, at, later, beside_first, beside_second):
-    near = beside_first(moved(block, axis, lambda i: i ^ 1))
+    near = beside_first(block, moved(block, axis, lambda i: i ^ 1))
     pair = block + near
-    other = beside_second(moved(pair, axis, lambda i: 3 - i))
+    other = beside_second(pair, moved(pair, axis, lambda i: 3 - i))
     counts_near = (at % 2 == 0) if later else (at % 2 == 1)
     counts_other = (at < 2) if later else (at >= 2)
     return jnp.where(counts_near, near, 0.0) + jnp.where(counts_other, other, 0.0), pair + other
@@ -614,10 +614,10 @@
     chip = mine + theirs
 
     def beside_step(i):
-        def tie(arrived):
+        def tie(block, arrived):
             if work is None:
                 return arrived
-            done = work(i)
+            done = work(i, block)
             arrived, *done[:] = lax.optimization_barrier((arrived, *done))
             return arrived
 
@@ -692,7 +692,7 @@
     (packed,) = per_head(update_kernel, heads, "cc", "s", "update")(keys, values)
     forwards = []
 
-    def forward(step):
+    def forward(step, block):
         if step % 2 == 0:
             forwards[:] = forward_of((step, heads // 2), (queries, keys, values), forwards)
         return forwards
@@ -720,7 +720,10 @@
     far_2 = up(left[MOST:, :half]), down(right[MOST:, half:])
 
     mg, mine_sides, send_sides = add(mg, [left, right], [left_at, right_at])
-    *far_1, mine_sides, send_sides = lax.optimization_barrier((*far_1, mine_sides, send_sides))
+    sum_own = scattered(*own_parts, "z", beside)
+    *far_1, mine_sides, send_sides, sum_own = lax.optimization_barrier(
+        (*far_1, mine_sides, send_sides, sum_own)
+    )
     came_sides = core_swap(send_sides)
     far_places = [2 * far_at, 2 * far_at + 1]
     tail = functools.partial(
@@ -733,43 +736,46 @@
     def backward_ins(part):
         return (*attended, part, local_out, memory_out, lse, before, g)
 
-    sum_own = scattered(*own_parts, "z", beside)
     mg_1, came_sides = lax.optimization_barrier((mg_1, came_sides))
     left_parts = half_scattered(chip_piece(mine_sides, came_sides), "z", z, across, beside)
     right_parts = half_scattered(chip_piece(mine_sides, came_sides, zs), "z", z, beside, across)
     early = backward_of(0, (0, heads), backward_ins(mg_1), (), (), 0)
-    *far_2, dq, dk, dv, left_kept, left_passed, right_kept, right_passed, sum_own = (
-        lax.optimization_barrier((*far_2, *early, *left_parts, *right_parts, sum_own))
+    *far_2, dq, dk, dv, left_kept, left_passed, right_kept, right_passed = (
+        lax.optimization_barrier((*far_2, *early, *left_parts, *right_parts))
     )
     mg_2, back, mine_far, send_far = tail(1, mg, far_2, before=far_sums)
     sum_left = scattered(left_kept, left_passed, "z", beside)
     sum_right = scattered(right_kept, right_passed, "z", across)
+    back, send_far, sum_left, sum_right = lax.optimization_barrier(
+        (back, send_far, sum_left, sum_right)
+    )
     came_far = core_swap(send_far)
     far_parts = half_scattered(chip_piece(mine_far, came_far), "z", z, across, beside)
 
     pairs = [(0, heads // 2), (heads // 2, heads // 2)]
     held = {}
 
-    def beside_scan(step):
+    def piece_x(i):
+        parts = jnp.stack([sum_own, sum_left, held[1][0], sum_right])
+        return at_place(parts, (head + hs - i) % hs)
+
+    def beside_scan(step, block):
         if step == 0:
-            grads = backward_of(1, pairs[0], backward_ins(mg_2), (dk, dv), [dq], 6)
-            held[0] = [*grads, sum_left, sum_right]
+            part, _ = lax.optimization_barrier((mg_2, block))
+            grads = backward_of(1, pairs[0], backward_ins(part), (dk, dv), [dq], 6)
+            held[0] = [*grads, *far_parts]
         elif step == 1:
-            held[1] = list(far_parts)
+            held[1] = [scattered(*held[0][3:], "z", beside)]
         elif step == 2:
-            grads = backward_of(1, pairs[1], backward_ins(mg_2), (dk, dv), held[0][:3], 6)
-            held[2] = [*grads, scattered(*held[1], "z", beside)]
+            sent = outgoing(piece_x, x, across, beside)
+            held["sent"], part, _ = lax.optimization_barrier((sent, mg_2, block))
+            held[2] = [*backward_of(1, pairs[1], backward_ins(part), (dk, dv), held[0][:3], 6)]
         else:
-            held[3] = [outgoing(piece_x, x, across, beside)]
+            held[3] = [*half_scattered(piece_x, "x", x, across, beside, held["sent"])]
         return held[step]
 
-    def piece_x(i):
-        parts = jnp.stack([sum_own, held[0][3], held[2][3], held[0][4]])
-        return at_place(parts, (head + hs - i) % hs)
-
     after = scan_over_ctx(back, True, beside_scan)
-    x_parts = half_scattered(piece_x, "x", x, across, beside, held[3][0])
-    weight_grad = scattered(*x_parts, "x", beside).T
+    weight_grad = scattered(*held[3], "x", beside).T
 
     key_grad, value_grad = per_head(finish_kernel, heads, "ccccs", "cc", "finish")(
         keys, values, *held[2][1:3], after

time: 257 us -> 235 us (0.914); the launches traced: 257 us -> 232 us
  waiting for transfers between devices: 87.3 us -> 57.1 us
  starting transfers between devices: 35.5 us -> 38.3 us
  other arithmetic: 14.9 us -> 17.6 us
    ppermute x18, waiting for transfers between devices: 64.9 us -> 34.7 us  [moved(): return lax.ppermute(block, 'ctx', pairs)]
    ppermute x18, starting transfers between devices: 24.9 us -> 27.7 us  [moved(): return lax.ppermute(block, 'ctx', pairs)]
  transfers between devices with their start and end apart: 31 -> 31, of which waited for: 14 -> 15; matrix products, arithmetic and copies ran while one was open for 7% -> 8% of each run, Pallas kernels for 39% -> 48%
where the time goes in v1:
time: 235 us; the launch traced here: 232 us
  Pallas kernels  111 us (47%)
  waiting for transfers between devices  57.1 us (24%)
  starting transfers between devices  38.3 us (16%)
  other arithmetic  17.6 us (7%)
  local copies, waits for them, and re-layouts  7.34 us (3%)
    ppermute x18, waiting for transfers between devices, moved(): return lax.ppermute(block, 'ctx', pairs)  34.7 us
    pallas_call x2, Pallas kernels, round_of(): pl.pallas_call(functools.partial(block_kernel, blocks=n, added=len(acc),...  33.5 us
    ppermute x18, starting transfers between devices, moved(): return lax.ppermute(block, 'ctx', pairs)  27.7 us
    pallas_call x3, Pallas kernels, backward_of(): pl.pallas_call(functools.partial(backward_kernel, first=second * MOST), g...  25.9 us
    pallas_call x2, Pallas kernels, tail_of(): pl.pallas_call(tail_kernel, grid_spec=pltpu.PrefetchScalarGridSpec(num_sc...  21.1 us
    ppermute x3, waiting for transfers between devices, up(): return lax.ppermute(block, 'head', ring(hs, 1))  13.4 us
    pallas_call x2, Pallas kernels, forward_of(): pl.pallas_call(forward_kernel, grid=(count,), in_specs=[column] * 3 + [pl...  12.8 us
    ppermute x7, waiting for transfers between devices, core_swap(): return lax.ppermute(block, 'ctx', [(i, i ^ 1) for i in range(n)])  9 us
  transfers between devices with their start and end apart: 31, of which 15 were waited for; matrix products, arithmetic and copies ran while one was open for 8% of the time, Pallas kernels for 48%

profile of v1, /device:TPU:4, one launch (start us, length us, event | category | flops | bytes accessed | tf_op | source)
XLA Modules:
  0.0 232.2 jit_solution(10881754093077214515)
XLA Ops:
  0.6 1.6 collective-permute-start.6
  2.3 1.7 collective-permute-start.7
  3.9 4.7 %update.1 = f32[4,136,128]{2,1,0:T(8,128)} custom-call(f32[1024,512]{1,0:T(8,128)} %k_ref.7, f32[1024,512]{1,0:T(8,128)} %v_ref.7), custom_call_target="tpu_custom_call" | custom-call | flops 65536 | bytes 65536 | tf_op jit(solution)/shard_map/update/pallas_call | solution.py:692
  8.7 1.0 slice_select_fusion
  9.8 1.3 collective-permute-done
  11.1 1.0 fusion.11
  12.1 2.0 collective-permute-start.1
  14.1 6.4 %forward.2 = (f32[1024,512]{1,0:T(8,128)}, f32[4,1,1024]{2,1,0:T(1,128)}) custom-call(f32[1024,512]{1,0:T(8,128)} %refs_0_.7, f32[1024,512]{1,0:T(8,128)} %k_ref.7, f32[1024,512]{1,0:T(8,128)} %v_ref.7), custom_call_target="tpu_custom_call" | custom-call | flops 65536 | bytes 65536 | tf_op jit(solution)/shard_map/forward/pallas_call | solution.py:502
  20.5 2.6 %collective-permute-start.2 = (f32[2,136,128]{2,1,0:T(8,128)S(1)}, f32[2,136,128]{2,1,0:T(8,128)S(1)}, u32[]{:S(2)}, u32[]{:S(2)}) collective-permute-start(f32[2,136,128]{2,1,0:T(8,128)S(1)} %add.378), channel_id=1, source_target_pairs={{0,24},{4,28},{8,16},{12,20},{16,8},{20,12},{24,0},{28,4},{32,56},... | collective-permute-start | bytes 417800 | tf_op jit(solution)/shard_map/ppermute | solution.py:594
  23.1 4.1 %collective-permute-done.2 = f32[2,136,128]{2,1,0:T(8,128)S(1)} collective-permute-done((f32[2,136,128]{2,1,0:T(8,128)S(1)}, f32[2,136,128]{2,1,0:T(8,128)S(1)}, u32[]{:S(2)}, u32[]{:S(2)}) %collective-permute-start.2) | collective-permute-done | bytes 139296 | tf_op jit(solution)/shard_map/ppermute | solution.py:594
  27.3 1.3 collective-permute-start.3
  28.6 6.4 %forward.3 = (f32[1024,512]{1,0:T(8,128)}, f32[4,1,1024]{2,1,0:T(1,128)}) custom-call(f32[1024,512]{1,0:T(8,128)} %refs_0_.7, f32[1024,512]{1,0:T(8,128)} %k_ref.7, f32[1024,512]{1,0:T(8,128)} %v_ref.7, f32[1024,512]{1,0:T(8,128)} %get-tuple-element.98.refs_0_, f32[4,1,1024]{2,1,0:T(1,128)} %get-tuple-element.99.refs_1_), custom_call_target="tpu_custom_call", output_to_operand_aliasing={{0}: (3, {}), {1}: (4, {})} | custom-call | flops 65536 | bytes 65536 | tf_op jit(solution)/shard_map/forward/pallas_call | solution.py:502
  35.2 4.9 %collective-permute-done.4 = f32[2,136,128]{2,1,0:T(8,128)S(1)} collective-permute-done((f32[2,136,128]{2,1,0:T(8,128)S(1)}, f32[2,136,128]{2,1,0:T(8,128)S(1)}, u32[]{:S(2)}, u32[]{:S(2)}) %collective-permute-start.4) | collective-permute-done | bytes 139296 | tf_op jit(solution)/shard_map/ppermute | solution.py:594
  41.0 0.7 collective-permute-done.5
  41.8 0.7 pad_maximum_fusion.7.mem_ref.refs_7_
  43.2 5.8 %mix.1 = (bf16[512,1024]{1,0:T(8,128)(2,1)}, bf16[512,1024]{1,0:T(8,128)(2,1)}, f32[1024,512]{1,0:T(8,128)}, f32[1024,512]{1,0:T(8,128)}) custom-call(f32[1024,512]{1,0:T(8,128)} %refs_0_.7, f32[1024,512]{1,0:T(8,128)} %get-tuple-element.105.local_ref.refs_7_.refs_4_, f32[4,136,128]{2,1,0:T(8,128)} %pad_maximum_fusion.7.mem_ref.refs_7_, ...), custom_call_target="tpu_custom_call" | custom-call | flops 65536 | bytes 65536 | tf_op jit(solution)/shard_map/mix/pallas_call | solution.py:702
  49.0 12.1 %round.2 = (f32[1024,512]{1,0:T(8,128)}, f32[4,512,128]{2,1,0:T(8,128)}, f32[4,512,128]{2,1,0:T(8,128)}) custom-call(s32[2]{0:T(128)} %pad_add_fusion.at_ref, f32[1024,1024]{1,0:T(8,128)} %refs_0_.4, f32[512,4096]{1,0:T(8,128)} %refs_4_.5, bf16[512,1024]{1,0:T(8,128)(2,1)} %get-tuple-element.107.refs_2_.refs_5_.refs_8_, ...), custom_call_target="tpu_custom_call" | custom-call | flops 65536 | bytes 65536 | tf_op jit(solution)/shard_map/round/pallas_call | solution.py:365
  61.3 2.7 %collective-permute-done.8 = f32[4,512,128]{2,1,0:T(8,128)S(1)} collective-permute-done((f32[4,512,128]{2,1,0:T(8,128)}, f32[4,512,128]{2,1,0:T(8,128)S(1)}, u32[]{:S(2)}, u32[]{:S(2)}) %collective-permute-start.8) | collective-permute-done | bytes 1048608 | tf_op jit(solution)/shard_map/ppermute | solution.py:582
  64.0 1.1 dynamic-slice_add_fusion.7
  65.2 2.6 %collective-permute-start.9 = (f32[2,512,128]{2,1,0:T(8,128)S(1)}, f32[2,512,128]{2,1,0:T(8,128)S(1)}, u32[]{:S(2)}, u32[]{:S(2)}) collective-permute-start(f32[2,512,128]{2,1,0:T(8,128)S(1)} %pad_maximum_fusion.1), channel_id=1, source_target_pairs={{0,24},{4,28},{8,16},{12,20},{16,8},{20,12},{24,0},{28,4},{32,56},... | collective-permute-start | bytes 1572872 | tf_op jit(solution)/shard_map/ppermute | solution.py:594
  67.8 12.7 %collective-permute-done.9 = f32[2,512,128]{2,1,0:T(8,128)S(1)} collective-permute-done((f32[2,512,128]{2,1,0:T(8,128)S(1)}, f32[2,512,128]{2,1,0:T(8,128)S(1)}, u32[]{:S(2)}, u32[]{:S(2)}) %collective-permute-start.9) | collective-permute-done | bytes 524320 | tf_op jit(solution)/shard_map/ppermute | solution.py:594
  80.4 0.8 fusion.8
  81.2 13.4 %collective-permute-done.6.refs_1_ = f32[1024,1024]{1,0:T(8,128)} collective-permute-done((f32[1024,1024]{1,0:T(8,128)}, f32[1024,1024]{1,0:T(8,128)}, u32[]{:S(2)}, u32[]{:S(2)}) %collective-permute-start.6) | collective-permute-done | bytes 4194336 | tf_op jit(solution)/shard_map/ppermute | solution.py:682
  94.6 2.7 %fusion.15 = (f32[512,512]{1,0:T(8,128)S(1)}, f32[512,512]{1,0:T(8,128)}) fusion(f32[1024,1024]{1,0:T(8,128)} %collective-permute-done.6.refs_1_), kind=kLoop, calls=%fused_computation.68 | loop fusion | bytes 4194304 | tf_op jit(solution)/shard_map/slice | solution.py:719
  97.4 1.6 collective-permute-start.12
  98.9 3.0 %fusion.14 = (f32[512,512]{1,0:T(8,128)}, f32[512,512]{1,0:T(8,128)}) fusion(f32[1024,1024]{1,0:T(8,128)} %collective-permute-done.7.refs_2_), kind=kLoop, calls=%fused_computation.67 | loop fusion | bytes 4194304 | tf_op jit(solution)/shard_map/slice | solution.py:719
  102.0 1.7 collective-permute-start.13
  103.6 1.9 collective-permute-start.14
  106.2 21.5 %round.3 = (f32[1024,512]{1,0:T(8,128)}, f32[8,512,128]{2,1,0:T(8,128)}, f32[8,512,128]{2,1,0:T(8,128)}) custom-call(s32[3]{0:T(128)} %get-tuple-element.219.at_ref, f32[1024,512]{1,0:T(8,128)} %get-tuple-element.109.refs_0_, f32[1024,1024]{1,0:T(8,128)} %collective-permute-done.6.refs_1_, ...), custom_call_target="tpu_custom_call", output_to_operand_aliasing={{0}: (1, {})} | custom-call | flops 65536 | bytes 65536 | tf_op jit(solution)/shard_map/round/pallas_call | solution.py:365
  127.7 1.0 add.405
  129.3 2.9 %collective-permute-start.11 = (f32[512,512]{1,0:T(8,128)}, f32[512,512]{1,0:T(8,128)}, u32[]{:S(2)}, u32[]{:S(2)}) collective-permute-start(f32[512,512]{1,0:T(8,128)} %get-tuple-element.199), channel_id=1, source_target_pairs={{0,3},{1,0},{2,1},{3,2},{4,7},{5,4},{6,5},{7,6},{8,11},{9,8},{10,9... | collective-permute-start | bytes 3145736 | tf_op jit(solution)/shard_map/ppermute | solution.py:685
  132.1 10.3 %tail.2 = (f32[512,512]{1,0:T(8,128)}, f32[4,136,128]{2,1,0:T(8,128)}, f32[4,512,128]{2,1,0:T(8,128)}, f32[4,512,128]{2,1,0:T(8,128)}) custom-call(s32[3]{0:T(128)} %get-tuple-element.218.at_ref, f32[1024,512]{1,0:T(8,128)} %get-tuple-element.114.refs_0_, f32[512,512]{1,0:T(8,128)} %copy-done.3, f32[512,512]{1,0:T(8,128)} %copy-done.4, f32[512,4096]{1,0:T(8,128)} %refs_4_.5, ...), custom_call_target="tpu_custom_call" | custom-call | flops 65536 | bytes 65536 | tf_op jit(solution)/shard_map/tail/pallas_call | solution.py:395
  142.5 1.3 dynamic-slice_add_fusion.3
  143.8 0.8 pad_maximum_fusion.2
  144.6 2.5 %collective-permute-start.16 = (f32[2,512,128]{2,1,0:T(8,128)}, f32[2,512,128]{2,1,0:T(8,128)}, u32[]{:S(2)}, u32[]{:S(2)}) collective-permute-start(f32[2,512,128]{2,1,0:T(8,128)} %pad_maximum_fusion.2), channel_id=1, source_target_pairs={{0,24},{4,28},{8,16},{12,20},{16,8},{20,12},{24,0},{28,4},{32,56},... | collective-permute-start | bytes 1572872 | tf_op jit(solution)/shard_map/ppermute | solution.py:594
  147.1 1.1 collective-permute-start.17
  148.2 8.9 %backward.3 = (f32[1024,512]{1,0:T(8,128)}, f32[512,512]{1,0:T(8,128)}, f32[512,512]{1,0:T(8,128)}) custom-call(f32[1024,512]{1,0:T(8,128)} %refs_0_.7, f32[1024,512]{1,0:T(8,128)} %k_ref.7, f32[1024,512]{1,0:T(8,128)} %v_ref.7, f32[512,512]{1,0:T(8,128)} %get-tuple-element.125.refs_3_, f32[1024,512]{1,0:T(8,128)} %get-tuple-element.105.local_ref.refs_7_.refs_4_, ...), custom_call_target="tpu_custom_call" | custom-call | flops 65536 | bytes 65536 | tf_op jit(solution)/shard_map/backward/pallas_call | solution.py:479
  157.1 2.6 %collective-permute-done.16 = f32[2,512,128]{2,1,0:T(8,128)} collective-permute-done((f32[2,512,128]{2,1,0:T(8,128)}, f32[2,512,128]{2,1,0:T(8,128)}, u32[]{:S(2)}, u32[]{:S(2)}) %collective-permute-start.16) | collective-permute-done | bytes 524320 | tf_op jit(solution)/shard_map/ppermute | solution.py:594
  159.7 0.9 collective-permute-done.17
  160.6 1.6 fusion.4
  162.3 1.7 collective-permute-start.19
  164.0 10.8 %tail.3 = (f32[512,512]{1,0:T(8,128)}, f32[4,136,128]{2,1,0:T(8,128)}, f32[4,512,128]{2,1,0:T(8,128)}, f32[4,512,128]{2,1,0:T(8,128)}) custom-call(s32[3]{0:T(128)} %get-tuple-element.218.at_ref, f32[1024,512]{1,0:T(8,128)} %get-tuple-element.114.refs_0_, f32[512,512]{1,0:T(8,128)} %collective-permute-done.10.refs_1_, ...), custom_call_target="tpu_custom_call" | custom-call | flops 65536 | bytes 65536 | tf_op jit(solution)/shard_map/tail/pallas_call | solution.py:395
  175.0 2.9 %collective-permute-done.22 = f32[4,512,128]{2,1,0:T(8,128)S(1)} collective-permute-done((f32[4,512,128]{2,1,0:T(8,128)}, f32[4,512,128]{2,1,0:T(8,128)S(1)}, u32[]{:S(2)}, u32[]{:S(2)}) %collective-permute-start.22) | collective-permute-done | bytes 1048608 | tf_op jit(solution)/shard_map/ppermute | solution.py:582
  177.9 1.1 dynamic-slice_add_fusion.1
  178.9 0.8 pad_maximum_fusion.4
  179.8 2.1 collective-permute-start.23
  182.0 1.3 collective-permute-done.20
  183.4 1.1 collective-permute-start.21
  184.4 8.6 %backward.4 = (f32[1024,512]{1,0:T(8,128)}, f32[1024,512]{1,0:T(8,128)}, f32[1024,512]{1,0:T(8,128)}) custom-call(f32[1024,512]{1,0:T(8,128)} %refs_0_.7, f32[1024,512]{1,0:T(8,128)} %k_ref.7, f32[1024,512]{1,0:T(8,128)} %v_ref.7, f32[512,512]{1,0:T(8,128)} %get-tuple-element.162.refs_3_, ...), custom_call_target="tpu_custom_call", output_to_operand_aliasing={{0}: (11, {})} | custom-call | flops 65536 | bytes 21600000 | tf_op jit(solution)/shard_map/backward/pallas_call | solution.py:479
  193.0 2.3 collective-permute-done.23
  195.3 1.8 fusion.2
  197.1 0.8 collective-permute-start.25
  197.9 1.7 collective-permute-start.24
  199.6 5.2 %collective-permute-done.25 = f32[512,128]{1,0:T(8,128)S(1)} collective-permute-done((f32[512,128]{1,0:T(8,128)}, f32[512,128]{1,0:T(8,128)S(1)}, u32[]{:S(2)}, u32[]{:S(2)}) %collective-permute-start.25) | collective-permute-done | bytes 262176 | tf_op jit(solution)/shard_map/ppermute | solution.py:594
  205.7 1.1 collective-permute-start.26
  206.9 8.5 %backward.5 = (f32[1024,512]{1,0:T(8,128)}, f32[1024,512]{1,0:T(8,128)}, f32[1024,512]{1,0:T(8,128)}) custom-call(f32[1024,512]{1,0:T(8,128)} %refs_0_.7, f32[1024,512]{1,0:T(8,128)} %k_ref.7, f32[1024,512]{1,0:T(8,128)} %v_ref.7, f32[512,512]{1,0:T(8,128)} %get-tuple-element.162.refs_3_, ...), custom_call_target="tpu_custom_call", output_to_operand_aliasing={{0}: (11, {}), {1}: (12, {}), {2}: (13, {})} | custom-call | flops 65536 | bytes 21600000 | tf_op jit(solution)/shard_map/backward/pallas_call | solution.py:479
  215.4 2.2 collective-permute-start.27
  217.6 0.9 collective-permute-done.28
  218.5 1.1 fusion
  219.6 1.0 collective-permute-done.27
  220.8 2.2 collective-permute-start.30
  223.1 0.7 pad_maximum_fusion.6.state_ref
  223.9 6.8 %finish.1 = (f32[1024,512]{1,0:T(8,128)}, f32[1024,512]{1,0:T(8,128)}) custom-call(f32[1024,512]{1,0:T(8,128)} %k_ref.7, f32[1024,512]{1,0:T(8,128)} %v_ref.7, f32[1024,512]{1,0:T(8,128)} %get-tuple-element.170.dk_ref, f32[1024,512]{1,0:T(8,128)} %get-tuple-element.171.dv_ref, f32[4,136,128]{2,1,0:T(8,128)} %pad_maximum_fusion.6.state_ref), custom_call_target="tpu_custom_call" | custom-call | flops 65536 | bytes 65536 | tf_op jit(solution)/shard_map/finish/pallas_call | solution.py:780
  231.3 0.8 copy.18
  (75 shorter events, 5.5 us)
Async XLA Ops:
  0.6 94.0 %collective-permute-start.6 = (f32[1024,1024]{1,0:T(8,128)}, f32[1024,1024]{1,0:T(8,128)}, u32[]{:S(2)}, u32[]{:S(2)}) collective-permute-start(f32[1024,1024]{1,0:T(8,128)} %refs_0_.4), channel_id=1, source_target_pairs={{0,1},{1,2},{2,3},{3,0},{4,5},{5,6},{6,7},{7,4},{8,9},{9,10},{10,1... | collective-permute-start | bytes 12582920 | tf_op jit(solution)/shard_map/ppermute | solution.py:682
  2.3 92.3 %collective-permute-start.7 = (f32[1024,1024]{1,0:T(8,128)}, f32[1024,1024]{1,0:T(8,128)}, u32[]{:S(2)}, u32[]{:S(2)}) collective-permute-start(f32[1024,1024]{1,0:T(8,128)} %refs_0_.4), channel_id=1, source_target_pairs={{0,3},{1,0},{2,1},{3,2},{4,7},{5,4},{6,5},{7,6},{8,11},{9,8},{10,9... | collective-permute-start | bytes 12582920 | tf_op jit(solution)/shard_map/ppermute | solution.py:685
  9.7 1.4 collective-permute-start
  12.1 8.4 %collective-permute-start.1 = (f32[2,136,128]{2,1,0:T(8,128)S(1)}, f32[2,136,128]{2,1,0:T(8,128)S(1)}, u32[]{:S(2)}, u32[]{:S(2)}) collective-permute-start(f32[2,136,128]{2,1,0:T(8,128)S(1)} %fusion.11), channel_id=1, source_target_pairs={{0,8},{4,12},{8,0},{12,4},{16,24},{20,28},{24,16},{28,20},{32,40},... | collective-permute-start | bytes 417800 | tf_op jit(solution)/shard_map/ppermute | solution.py:594
  20.5 6.7 %collective-permute-start.2 = (f32[2,136,128]{2,1,0:T(8,128)S(1)}, f32[2,136,128]{2,1,0:T(8,128)S(1)}, u32[]{:S(2)}, u32[]{:S(2)}) collective-permute-start(f32[2,136,128]{2,1,0:T(8,128)S(1)} %add.378), channel_id=1, source_target_pairs={{0,24},{4,28},{8,16},{12,20},{16,8},{20,12},{24,0},{28,4},{32,56},... | collective-permute-start | bytes 417800 | tf_op jit(solution)/shard_map/ppermute | solution.py:594
  27.3 12.9 %copy-start = (f32[4,136,128]{2,1,0:T(8,128)S(1)}, f32[4,136,128]{2,1,0:T(8,128)}, u32[]{:S(2)}) copy-start(f32[4,136,128]{2,1,0:T(8,128)} %update.1) | copy-start | bytes 835588
  27.3 13.1 %copy-start.8 = (f32[4]{0:T(128)S(1)}, f32[4]{0:T(128)}, u32[]{:S(2)}) copy-start(f32[4]{0:T(128)} %param.9) | copy-start | bytes 52
  27.3 7.7 %collective-permute-start.3 = (f32[2,136,128]{2,1,0:T(8,128)S(1)}, f32[2,136,128]{2,1,0:T(8,128)S(1)}, u32[]{:S(2)}, u32[]{:S(2)}) collective-permute-start(f32[2,136,128]{2,1,0:T(8,128)S(1)} %add.379), channel_id=1, source_target_pairs={{0,32},{4,36},{8,40},{12,44},{16,48},{20,52},{24,56},{28,60},{32,0... | collective-permute-start | bytes 417800 | tf_op jit(solution)/shard_map/ppermute | solution.py:594
  35.0 5.1 %collective-permute-start.4 = (f32[2,136,128]{2,1,0:T(8,128)S(1)}, f32[2,136,128]{2,1,0:T(8,128)S(1)}, u32[]{:S(2)}, u32[]{:S(2)}) collective-permute-start(f32[2,136,128]{2,1,0:T(8,128)S(1)} %add.380), channel_id=1, source_target_pairs={{0,96},{4,100},{8,104},{12,108},{16,112},{20,116},{24,120},{28,124... | collective-permute-start | bytes 417800 | tf_op jit(solution)/shard_map/ppermute | solution.py:594
  40.3 1.4 collective-permute-start.5
  61.1 19.4 %copy-start.6 = (f32[4,512,128]{2,1,0:T(8,128)S(1)}, f32[4,512,128]{2,1,0:T(8,128)}, u32[]{:S(2)}) copy-start(f32[4,512,128]{2,1,0:T(8,128)} %get-tuple-element.110) | copy-start | bytes 3145732
  61.1 3.0 %collective-permute-start.8 = (f32[4,512,128]{2,1,0:T(8,128)}, f32[4,512,128]{2,1,0:T(8,128)S(1)}, u32[]{:S(2)}, u32[]{:S(2)}) collective-permute-start(f32[4,512,128]{2,1,0:T(8,128)} %get-tuple-element.111), channel_id=1, source_target_pairs={{0,4},{4,0},{8,12},{12,8},{16,20},{20,16},{24,28},{28,24},{32,36},... | collective-permute-start | bytes 3145736 | tf_op jit(solution)/shard_map/ppermute | solution.py:582
  65.2 15.3 %collective-permute-start.9 = (f32[2,512,128]{2,1,0:T(8,128)S(1)}, f32[2,512,128]{2,1,0:T(8,128)S(1)}, u32[]{:S(2)}, u32[]{:S(2)}) collective-permute-start(f32[2,512,128]{2,1,0:T(8,128)S(1)} %pad_maximum_fusion.1), channel_id=1, source_target_pairs={{0,24},{4,28},{8,16},{12,20},{16,8},{20,12},{24,0},{28,4},{32,56},... | collective-permute-start | bytes 1572872 | tf_op jit(solution)/shard_map/ppermute | solution.py:594
  97.4 31.3 %collective-permute-start.12 = (f32[512,512]{1,0:T(8,128)S(1)}, f32[512,512]{1,0:T(8,128)S(1)}, u32[]{:S(2)}, u32[]{:S(2)}) collective-permute-start(f32[512,512]{1,0:T(8,128)S(1)} %get-tuple-element.200), channel_id=1, source_target_pairs={{0,1},{1,2},{2,3},{3,0},{4,5},{5,6},{6,7},{7,4},{8,9},{9,10},{10,1... | collective-permute-start | bytes 3145736 | tf_op jit(solution)/shard_map/ppermute | solution.py:682
  102.0 26.7 %collective-permute-start.13 = (f32[512,512]{1,0:T(8,128)}, f32[512,512]{1,0:T(8,128)S(1)}, u32[]{:S(2)}, u32[]{:S(2)}) collective-permute-start(f32[512,512]{1,0:T(8,128)} %get-tuple-element.198), channel_id=1, source_target_pairs={{0,3},{1,0},{2,1},{3,2},{4,7},{5,4},{6,5},{7,6},{8,11},{9,8},{10,9... | collective-permute-start | bytes 3145736 | tf_op jit(solution)/shard_map/ppermute | solution.py:685
  103.6 24.0 %collective-permute-start.14 = (f32[512,128]{1,0:T(8,128)S(1)}, f32[512,128]{1,0:T(8,128)}, u32[]{:S(2)}, u32[]{:S(2)}) collective-permute-start(f32[512,128]{1,0:T(8,128)S(1)} %get-tuple-element.118), channel_id=1, source_target_pairs={{0,8},{4,12},{8,0},{12,4},{16,24},{20,28},{24,16},{28,20},{32,40},... | collective-permute-start | bytes 786440 | tf_op jit(solution)/shard_map/ppermute | solution.py:594
  106.2 21.5 %copy-start.7 = (f32[512,128]{1,0:T(8,128)S(1)}, f32[512,128]{1,0:T(8,128)}, u32[]{:S(2)}) copy-start(f32[512,128]{1,0:T(8,128)} %get-tuple-element.117) | copy-start | bytes 786436
  128.6 3.5 %copy-start.3 = (f32[512,512]{1,0:T(8,128)}, f32[512,512]{1,0:T(8,128)S(1)}, u32[]{:S(2)}) copy-start(f32[512,512]{1,0:T(8,128)S(1)} %collective-permute-done.12.refs_1_) | copy-start | bytes 3145732
  128.7 3.5 %copy-start.4 = (f32[512,512]{1,0:T(8,128)}, f32[512,512]{1,0:T(8,128)S(1)}, u32[]{:S(2)}) copy-start(f32[512,512]{1,0:T(8,128)S(1)} %collective-permute-done.13.refs_2_) | copy-start | bytes 3145732
  128.7 13.8 %collective-permute-start.15 = (f32[8,512,128]{2,1,0:T(8,128)}, f32[8,512,128]{2,1,0:T(8,128)}, u32[]{:S(2)}, u32[]{:S(2)}) collective-permute-start(f32[8,512,128]{2,1,0:T(8,128)} %get-tuple-element.124), channel_id=1, source_target_pairs={{0,4},{4,0},{8,12},{12,8},{16,20},{20,16},{24,28},{28,24},{32,36},... | collective-permute-start | bytes 6291464 | tf_op jit(solution)/shard_map/ppermute | solution.py:582
  128.8 33.5 %collective-permute-start.10 = (f32[512,512]{1,0:T(8,128)}, f32[512,512]{1,0:T(8,128)}, u32[]{:S(2)}, u32[]{:S(2)}) collective-permute-start(f32[512,512]{1,0:T(8,128)} %get-tuple-element.201), channel_id=1, source_target_pairs={{0,1},{1,2},{2,3},{3,0},{4,5},{5,6},{6,7},{7,4},{8,9},{9,10},{10,1... | collective-permute-start | bytes 3145736 | tf_op jit(solution)/shard_map/ppermute | solution.py:682
  129.3 33.0 %collective-permute-start.11 = (f32[512,512]{1,0:T(8,128)}, f32[512,512]{1,0:T(8,128)}, u32[]{:S(2)}, u32[]{:S(2)}) collective-permute-start(f32[512,512]{1,0:T(8,128)} %get-tuple-element.199), channel_id=1, source_target_pairs={{0,3},{1,0},{2,1},{3,2},{4,7},{5,4},{6,5},{7,6},{8,11},{9,8},{10,9... | collective-permute-start | bytes 3145736 | tf_op jit(solution)/shard_map/ppermute | solution.py:685
  132.1 10.3 %copy-start.2 = (f32[8,512,128]{2,1,0:T(8,128)S(1)}, f32[8,512,128]{2,1,0:T(8,128)}, u32[]{:S(2)}) copy-start(f32[8,512,128]{2,1,0:T(8,128)} %get-tuple-element.130) | copy-start | bytes 6291460
  144.6 15.2 %collective-permute-start.16 = (f32[2,512,128]{2,1,0:T(8,128)}, f32[2,512,128]{2,1,0:T(8,128)}, u32[]{:S(2)}, u32[]{:S(2)}) collective-permute-start(f32[2,512,128]{2,1,0:T(8,128)} %pad_maximum_fusion.2), channel_id=1, source_target_pairs={{0,24},{4,28},{8,16},{12,20},{16,8},{20,12},{24,0},{28,4},{32,56},... | collective-permute-start | bytes 1572872 | tf_op jit(solution)/shard_map/ppermute | solution.py:594
  147.1 13.5 %collective-permute-start.17 = (f32[2,512,128]{2,1,0:T(8,128)S(1)}, f32[2,512,128]{2,1,0:T(8,128)}, u32[]{:S(2)}, u32[]{:S(2)}) collective-permute-start(f32[2,512,128]{2,1,0:T(8,128)S(1)} %pad_maximum_fusion.3), channel_id=1, source_target_pairs={{0,8},{4,12},{8,0},{12,4},{16,24},{20,28},{24,16},{28,20},{32,40},... | collective-permute-start | bytes 1572872 | tf_op jit(solution)/shard_map/ppermute | solution.py:594
  162.3 12.5 %collective-permute-start.19 = (f32[512,128]{1,0:T(8,128)S(1)}, f32[512,128]{1,0:T(8,128)S(1)}, u32[]{:S(2)}, u32[]{:S(2)}) collective-permute-start(f32[512,128]{1,0:T(8,128)S(1)} %get-tuple-element.142), channel_id=1, source_target_pairs={{0,24},{4,28},{8,16},{12,20},{16,8},{20,12},{24,0},{28,4},{32,56},... | collective-permute-start | bytes 786440 | tf_op jit(solution)/shard_map/ppermute | solution.py:594
  164.0 10.9 %collective-permute-start.18 = (f32[512,128]{1,0:T(8,128)S(1)}, f32[512,128]{1,0:T(8,128)S(1)}, u32[]{:S(2)}, u32[]{:S(2)}) collective-permute-start(f32[512,128]{1,0:T(8,128)S(1)} %get-tuple-element.140), channel_id=1, source_target_pairs={{0,8},{4,12},{8,0},{12,4},{16,24},{20,28},{24,16},{28,20},{32,40},... | collective-permute-start | bytes 786440 | tf_op jit(solution)/shard_map/ppermute | solution.py:594
  174.8 7.1 %copy-start.1 = (f32[4,136,128]{2,1,0:T(8,128)S(1)}, f32[4,136,128]{2,1,0:T(8,128)}, u32[]{:S(2)}) copy-start(f32[4,136,128]{2,1,0:T(8,128)} %get-tuple-element.143) | copy-start | bytes 835588
  174.9 3.0 %collective-permute-start.22 = (f32[4,512,128]{2,1,0:T(8,128)}, f32[4,512,128]{2,1,0:T(8,128)S(1)}, u32[]{:S(2)}, u32[]{:S(2)}) collective-permute-start(f32[4,512,128]{2,1,0:T(8,128)} %get-tuple-element.153), channel_id=1, source_target_pairs={{0,4},{4,0},{8,12},{12,8},{16,20},{20,16},{24,28},{28,24},{32,36},... | collective-permute-start | bytes 3145736 | tf_op jit(solution)/shard_map/ppermute | solution.py:582
  179.8 15.5 %collective-permute-start.23 = (f32[2,512,128]{2,1,0:T(8,128)}, f32[2,512,128]{2,1,0:T(8,128)}, u32[]{:S(2)}, u32[]{:S(2)}) collective-permute-start(f32[2,512,128]{2,1,0:T(8,128)} %pad_maximum_fusion.4), channel_id=1, source_target_pairs={{0,24},{4,28},{8,16},{12,20},{16,8},{20,12},{24,0},{28,4},{32,56},... | collective-permute-start | bytes 1572872 | tf_op jit(solution)/shard_map/ppermute | solution.py:594
  181.9 1.4 collective-permute-start.20
  183.4 13.7 %collective-permute-start.21 = (f32[2,136,128]{2,1,0:T(8,128)S(1)}, f32[2,136,128]{2,1,0:T(8,128)S(1)}, u32[]{:S(2)}, u32[]{:S(2)}) collective-permute-start(f32[2,136,128]{2,1,0:T(8,128)S(1)} %fusion.10), channel_id=1, source_target_pairs={{0,8},{4,12},{8,0},{12,4},{16,24},{20,28},{24,16},{28,20},{32,40},... | collective-permute-start | bytes 417800 | tf_op jit(solution)/shard_map/ppermute | solution.py:594
  184.4 10.9 %copy-start.5 = (f32[4,512,128]{2,1,0:T(8,128)S(1)}, f32[4,512,128]{2,1,0:T(8,128)}, u32[]{:S(2)}) copy-start(f32[4,512,128]{2,1,0:T(8,128)} %get-tuple-element.152) | copy-start | bytes 3145732
  197.1 7.7 %collective-permute-start.25 = (f32[512,128]{1,0:T(8,128)}, f32[512,128]{1,0:T(8,128)S(1)}, u32[]{:S(2)}, u32[]{:S(2)}) collective-permute-start(f32[512,128]{1,0:T(8,128)} %get-tuple-element.156), channel_id=1, source_target_pairs={{0,8},{4,12},{8,0},{12,4},{16,24},{20,28},{24,16},{28,20},{32,40},... | collective-permute-start | bytes 786440 | tf_op jit(solution)/shard_map/ppermute | solution.py:594
  197.9 6.9 %collective-permute-start.24 = (f32[2,136,128]{2,1,0:T(8,128)S(1)}, f32[2,136,128]{2,1,0:T(8,128)S(1)}, u32[]{:S(2)}, u32[]{:S(2)}) collective-permute-start(f32[2,136,128]{2,1,0:T(8,128)S(1)} %add.442), channel_id=1, source_target_pairs={{0,24},{4,28},{8,16},{12,20},{16,8},{20,12},{24,0},{28,4},{32,56},... | collective-permute-start | bytes 417800 | tf_op jit(solution)/shard_map/ppermute | solution.py:594
  205.1 13.4 %collective-permute-start.28 = (f32[2,512,128]{2,1,0:T(8,128)S(1)}, f32[2,512,128]{2,1,0:T(8,128)}, u32[]{:S(2)}, u32[]{:S(2)}) collective-permute-start(f32[2,512,128]{2,1,0:T(8,128)S(1)} %pad_maximum_fusion.5), channel_id=1, source_target_pairs={{0,96},{4,100},{8,104},{12,108},{16,112},{20,116},{24,120},{28,124... | collective-permute-start | bytes 1572872 | tf_op jit(solution)/shard_map/ppermute | solution.py:594
  205.7 9.6 %collective-permute-start.26 = (f32[2,136,128]{2,1,0:T(8,128)S(1)}, f32[2,136,128]{2,1,0:T(8,128)S(1)}, u32[]{:S(2)}, u32[]{:S(2)}) collective-permute-start(f32[2,136,128]{2,1,0:T(8,128)S(1)} %add.444), channel_id=1, source_target_pairs={{0,32},{4,36},{8,40},{12,44},{16,48},{20,52},{24,56},{28,60},{32,0... | collective-permute-start | bytes 417800 | tf_op jit(solution)/shard_map/ppermute | solution.py:594
  215.4 5.2 %collective-permute-start.27 = (f32[2,136,128]{2,1,0:T(8,128)S(1)}, f32[2,136,128]{2,1,0:T(8,128)S(1)}, u32[]{:S(2)}, u32[]{:S(2)}) collective-permute-start(f32[2,136,128]{2,1,0:T(8,128)S(1)} %add.450), channel_id=1, source_target_pairs={{0,96},{4,100},{8,104},{12,108},{16,112},{20,116},{24,120},{28,124... | collective-permute-start | bytes 417800 | tf_op jit(solution)/shard_map/ppermute | solution.py:594
  220.7 2.3 %collective-permute-start.29 = (f32[2,136,128]{2,1,0:T(8,128)S(1)}, f32[2,136,128]{2,1,0:T(8,128)S(1)}, u32[]{:S(2)}, u32[]{:S(2)}) collective-permute-start(f32[2,136,128]{2,1,0:T(8,128)S(1)} %get-tuple-element.184), channel_id=1, source_target_pairs={{0,4},{4,0},{8,12},{12,8},{16,20},{20,16},{24,28},{28,24},{32,36},... | collective-permute-start | bytes 417800 | tf_op jit(solution)/shard_map/ppermute | solution.py:582
  220.8 10.5 %collective-permute-start.30 = (f32[512,128]{1,0:T(8,128)S(1)}, f32[512,128]{1,0:T(8,128)S(1)}, u32[]{:S(2)}, u32[]{:S(2)}) collective-permute-start(f32[512,128]{1,0:T(8,128)S(1)} %get-tuple-element.178), channel_id=1, source_target_pairs={{0,32},{4,36},{8,40},{12,44},{16,48},{20,52},{24,56},{28,60},{32,0... | collective-permute-start | bytes 786440 | tf_op jit(solution)/shard_map/ppermute | solution.py:594

commit v2 on v1

--- a/solution.py
+++ b/solution.py
@@ -351,6 +351,29 @@
         )
         for k, block in enumerate(blocks)
     ]
+
+
+def onward_kernel(*refs):
+    for source, target in zip(refs[:4], refs[4:]):
+        target[...] = source[...]
+
+
+def onward_of(left, right):
+    rows, half, step = MOST, left.shape[1] // 2, MOST // 2
+
+    def rows_from(first, column):
+        return pl.BlockSpec((step, half), lambda i: (i + first // step, column))
+
+    return pl.pallas_call(
+        onward_kernel,
+        grid=(rows // step,),
+        in_specs=[rows_from(0, 0), rows_from(0, 1), rows_from(MOST, 0), rows_from(MOST, 1)],
+        out_specs=[rows_from(0, 0)] * 4,
+        out_shape=[jax.ShapeDtypeStruct((rows, half), f32)] * 4,
+        compiler_params=pltpu.CompilerParams(vmem_limit_bytes=VMEM_LIMIT),
+        cost_estimate=pl.CostEstimate(flops=LIGHT, bytes_accessed=LIGHT, transcendentals=0),
+        name="onward",
+    )(left, right, left, right)
 
 
 def round_of(acc, blocks, places, out_weight, mixed, core, first=0, before=(), micros=0):
@@ -676,7 +699,6 @@
     x, z, core = place()
     rows, cols = out_grad.shape
 
-    half = cols // 2
 
     def up(block):
         return lax.ppermute(block, "head", ring(hs, 1))
@@ -716,8 +738,9 @@
     came_own = core_swap(send_own)
     own_parts = half_scattered(chip_piece(mine_own, came_own), "z", z, across, beside)
     left, right, *own_parts = lax.optimization_barrier((left, right, *own_parts))
-    far_1 = up(left[:MOST, :half]), down(right[:MOST, half:])
-    far_2 = up(left[MOST:, :half]), down(right[MOST:, half:])
+    onward = onward_of(left, right)
+    far_1 = up(onward[0]), down(onward[1])
+    far_2 = up(onward[2]), down(onward[3])
 
     mg, mine_sides, send_sides = add(mg, [left, right], [left_at, right_at])
     sum_own = scattered(*own_parts, "z", beside)
@@ -750,7 +773,6 @@
         (back, send_far, sum_left, sum_right)
     )
     came_far = core_swap(send_far)
-    far_parts = half_scattered(chip_piece(mine_far, came_far), "z", z, across, beside)
 
     pairs = [(0, heads // 2), (heads // 2, heads // 2)]
     held = {}
@@ -761,9 +783,12 @@
 
     def beside_scan(step, block):
         if step == 0:
-            part, _ = lax.optimization_barrier((mg_2, block))
+            part, came, _ = lax.optimization_barrier((mg_2, came_far, block))
+            far_piece = chip_piece(mine_far, came)
+            sent = outgoing(far_piece, z, across, beside)
+            sent, part = lax.optimization_barrier((sent, part))
             grads = backward_of(1, pairs[0], backward_ins(part), (dk, dv), [dq], 6)
-            held[0] = [*grads, *far_parts]
+            held[0] = [*grads, *half_scattered(far_piece, "z", z, across, beside, sent)]
         elif step == 1:
             held[1] = [scattered(*held[0][3:], "z", beside)]
         elif step == 2:

time: 235 us -> 236 us (level)
  local copies, waits for them, and re-layouts: 7.34 us -> 1.59 us
  Pallas kernels: 111 us -> 114 us
    ppermute x3, waiting for transfers between devices: 0.02 us -> 12.8 us  [down(): return lax.ppermute(block, 'head', ring(hs, -1))]
    ppermute x3, waiting for transfers between devices: 13.4 us -> 3.42 us  [up(): return lax.ppermute(block, 'head', ring(hs, 1))]
    slice x2 -> x0, local copies, waits for them, and re-layouts: 5.76 us -> none  [on_device(): far_1 = (up(left[:MOST, :half]), down(right[:MOST, half:]))]
    pallas_call x0 -> x1, Pallas kernels: none -> 3.66 us  [onward_of(): pl.pallas_call(onward_kernel, grid=(rows // step,), in_specs=[rows_from(0...]
    ppermute x3, starting transfers between devices: 3.69 us -> 0.08 us  [up(): return lax.ppermute(block, 'head', ring(hs, 1))]
    ppermute x3, starting transfers between devices: 6.19 us -> 9.57 us  [down(): return lax.ppermute(block, 'head', ring(hs, -1))]
    ppermute x7, waiting for transfers between devices: 9 us -> 6.08 us  [core_swap(): return lax.ppermute(block, 'ctx', [(i, i ^ 1) for i in range(n)])]
where the time goes in v2:
time: 236 us; the launch traced here: 232 us
  Pallas kernels  114 us (48%)
  waiting for transfers between devices  58.8 us (25%)
  starting transfers between devices  37.7 us (16%)
  other arithmetic  18.9 us (8%)
    ppermute x18, waiting for transfers between devices, moved(): return lax.ppermute(block, 'ctx', pairs)  36.5 us
    pallas_call x2, Pallas kernels, round_of(): pl.pallas_call(functools.partial(block_kernel, blocks=n, added=len(acc),...  33.5 us
    ppermute x18, starting transfers between devices, moved(): return lax.ppermute(block, 'ctx', pairs)  27 us
    pallas_call x3, Pallas kernels, backward_of(): pl.pallas_call(functools.partial(backward_kernel, first=second * MOST), g...  25.8 us
    pallas_call x2, Pallas kernels, tail_of(): pl.pallas_call(tail_kernel, grid_spec=pltpu.PrefetchScalarGridSpec(num_sc...  21.1 us
    ppermute x3, waiting for transfers between devices, down(): return lax.ppermute(block, 'head', ring(hs, -1))  12.8 us
    pallas_call x2, Pallas kernels, forward_of(): pl.pallas_call(forward_kernel, grid=(count,), in_specs=[column] * 3 + [pl...  12.8 us
    ppermute x3, starting transfers between devices, down(): return lax.ppermute(block, 'head', ring(hs, -1))  9.57 us
  transfers between devices with their start and end apart: 31, of which 15 were waited for; matrix products, arithmetic and copies ran while one was open for 8% of the time, Pallas kernels for 48%

profile of v2, /device:TPU:4, one launch (start us, length us, event | category | flops | bytes accessed | tf_op | source)
XLA Modules:
  0.0 232.5 jit_solution(11729590124160837655)
XLA Ops:
  0.6 3.1 %collective-permute-start.7 = (f32[1024,1024]{1,0:T(8,128)}, f32[1024,1024]{1,0:T(8,128)}, u32[]{:S(2)}, u32[]{:S(2)}) collective-permute-start(f32[1024,1024]{1,0:T(8,128)} %refs_0_.4), channel_id=1, source_target_pairs={{0,3},{1,0},{2,1},{3,2},{4,7},{5,4},{6,5},{7,6},{8,11},{9,8},{10,9... | collective-permute-start | bytes 12582920 | tf_op jit(solution)/shard_map/ppermute | solution.py:707
  3.7 4.7 %update.1 = f32[4,136,128]{2,1,0:T(8,128)} custom-call(f32[1024,512]{1,0:T(8,128)} %k_ref.7, f32[1024,512]{1,0:T(8,128)} %v_ref.7), custom_call_target="tpu_custom_call" | custom-call | flops 65536 | bytes 65536 | tf_op jit(solution)/shard_map/update/pallas_call | solution.py:714
  8.4 1.0 slice_select_fusion
  9.5 1.3 collective-permute-done
  10.9 1.0 fusion.11
  11.9 2.0 collective-permute-start.1
  13.9 6.4 %forward.2 = (f32[1024,512]{1,0:T(8,128)}, f32[4,1,1024]{2,1,0:T(1,128)}) custom-call(f32[1024,512]{1,0:T(8,128)} %refs_0_.7, f32[1024,512]{1,0:T(8,128)} %k_ref.7, f32[1024,512]{1,0:T(8,128)} %v_ref.7), custom_call_target="tpu_custom_call" | custom-call | flops 65536 | bytes 65536 | tf_op jit(solution)/shard_map/forward/pallas_call | solution.py:525
  20.3 2.6 %collective-permute-start.2 = (f32[2,136,128]{2,1,0:T(8,128)S(1)}, f32[2,136,128]{2,1,0:T(8,128)S(1)}, u32[]{:S(2)}, u32[]{:S(2)}) collective-permute-start(f32[2,136,128]{2,1,0:T(8,128)S(1)} %add.378), channel_id=1, source_target_pairs={{0,24},{4,28},{8,16},{12,20},{16,8},{20,12},{24,0},{28,4},{32,56},... | collective-permute-start | bytes 417800 | tf_op jit(solution)/shard_map/ppermute | solution.py:617
  22.9 4.1 %collective-permute-done.2 = f32[2,136,128]{2,1,0:T(8,128)S(1)} collective-permute-done((f32[2,136,128]{2,1,0:T(8,128)S(1)}, f32[2,136,128]{2,1,0:T(8,128)S(1)}, u32[]{:S(2)}, u32[]{:S(2)}) %collective-permute-start.2) | collective-permute-done | bytes 139296 | tf_op jit(solution)/shard_map/ppermute | solution.py:617
  27.1 1.3 collective-permute-start.3
  28.4 6.4 %forward.3 = (f32[1024,512]{1,0:T(8,128)}, f32[4,1,1024]{2,1,0:T(1,128)}) custom-call(f32[1024,512]{1,0:T(8,128)} %refs_0_.7, f32[1024,512]{1,0:T(8,128)} %k_ref.7, f32[1024,512]{1,0:T(8,128)} %v_ref.7, f32[1024,512]{1,0:T(8,128)} %get-tuple-element.105.refs_0_, f32[4,1,1024]{2,1,0:T(1,128)} %get-tuple-element.106.refs_1_), custom_call_target="tpu_custom_call", output_to_operand_aliasing={{0}: (3, {}), {1}: (4, {})} | custom-call | flops 65536 | bytes 65536 | tf_op jit(solution)/shard_map/forward/pallas_call | solution.py:525
  35.0 4.9 %collective-permute-done.4 = f32[2,136,128]{2,1,0:T(8,128)S(1)} collective-permute-done((f32[2,136,128]{2,1,0:T(8,128)S(1)}, f32[2,136,128]{2,1,0:T(8,128)S(1)}, u32[]{:S(2)}, u32[]{:S(2)}) %collective-permute-start.4) | collective-permute-done | bytes 139296 | tf_op jit(solution)/shard_map/ppermute | solution.py:617
  40.8 0.7 collective-permute-done.5
  41.6 0.7 pad_maximum_fusion.7.mem_ref.refs_7_
  42.3 0.7 broadcast_in_dim.59.g_ref.refs_8_
  43.0 5.8 %mix.1 = (bf16[512,1024]{1,0:T(8,128)(2,1)}, bf16[512,1024]{1,0:T(8,128)(2,1)}, f32[1024,512]{1,0:T(8,128)}, f32[1024,512]{1,0:T(8,128)}) custom-call(f32[1024,512]{1,0:T(8,128)} %refs_0_.7, f32[1024,512]{1,0:T(8,128)} %get-tuple-element.112.local_ref.refs_7_.refs_4_, f32[4,136,128]{2,1,0:T(8,128)} %pad_maximum_fusion.7.mem_ref.refs_7_, ...), custom_call_target="tpu_custom_call" | custom-call | flops 65536 | bytes 65536 | tf_op jit(solution)/shard_map/mix/pallas_call | solution.py:724
  48.8 12.1 %round.2 = (f32[1024,512]{1,0:T(8,128)}, f32[4,512,128]{2,1,0:T(8,128)}, f32[4,512,128]{2,1,0:T(8,128)}) custom-call(s32[2]{0:T(128)} %pad_add_fusion.at_ref, f32[1024,1024]{1,0:T(8,128)} %refs_0_.4, f32[512,4096]{1,0:T(8,128)} %refs_4_.5, bf16[512,1024]{1,0:T(8,128)(2,1)} %get-tuple-element.114.refs_2_.refs_5_.refs_8_, ...), custom_call_target="tpu_custom_call" | custom-call | flops 65536 | bytes 65536 | tf_op jit(solution)/shard_map/round/pallas_call | solution.py:388
  61.1 2.7 %collective-permute-done.8 = f32[4,512,128]{2,1,0:T(8,128)S(1)} collective-permute-done((f32[4,512,128]{2,1,0:T(8,128)}, f32[4,512,128]{2,1,0:T(8,128)S(1)}, u32[]{:S(2)}, u32[]{:S(2)}) %collective-permute-start.8) | collective-permute-done | bytes 1048608 | tf_op jit(solution)/shard_map/ppermute | solution.py:605
  63.9 1.1 dynamic-slice_add_fusion.7
  65.0 2.6 %collective-permute-start.9 = (f32[2,512,128]{2,1,0:T(8,128)S(1)}, f32[2,512,128]{2,1,0:T(8,128)S(1)}, u32[]{:S(2)}, u32[]{:S(2)}) collective-permute-start(f32[2,512,128]{2,1,0:T(8,128)S(1)} %pad_maximum_fusion.1), channel_id=1, source_target_pairs={{0,24},{4,28},{8,16},{12,20},{16,8},{20,12},{24,0},{28,4},{32,56},... | collective-permute-start | bytes 1572872 | tf_op jit(solution)/shard_map/ppermute | solution.py:617
  67.6 12.7 %collective-permute-done.9 = f32[2,512,128]{2,1,0:T(8,128)S(1)} collective-permute-done((f32[2,512,128]{2,1,0:T(8,128)S(1)}, f32[2,512,128]{2,1,0:T(8,128)S(1)}, u32[]{:S(2)}, u32[]{:S(2)}) %collective-permute-start.9) | collective-permute-done | bytes 524320 | tf_op jit(solution)/shard_map/ppermute | solution.py:617
  80.3 0.8 fusion.8
  81.0 12.8 %collective-permute-done.7.refs_2_.refs_1_.refs_3_ = f32[1024,1024]{1,0:T(8,128)} collective-permute-done((f32[1024,1024]{1,0:T(8,128)}, f32[1024,1024]{1,0:T(8,128)}, u32[]{:S(2)}, u32[]{:S(2)}) %collective-permute-start.7) | collective-permute-done | bytes 4194336 | tf_op jit(solution)/shard_map/ppermute | solution.py:707
  93.9 3.4 %collective-permute-done.6.refs_1_.refs_0_.refs_2_ = f32[1024,1024]{1,0:T(8,128)} collective-permute-done((f32[1024,1024]{1,0:T(8,128)}, f32[1024,1024]{1,0:T(8,128)}, u32[]{:S(2)}, u32[]{:S(2)}) %collective-permute-start.6) | collective-permute-done | bytes 4194336 | tf_op jit(solution)/shard_map/ppermute | solution.py:704
  97.3 3.7 %onward.1 = (f32[512,512]{1,0:T(8,128)}, f32[512,512]{1,0:T(8,128)}, f32[512,512]{1,0:T(8,128)}, f32[512,512]{1,0:T(8,128)}) custom-call(f32[1024,1024]{1,0:T(8,128)} %collective-permute-done.6.refs_1_.refs_0_.refs_2_, f32[1024,1024]{1,0:T(8,128)} %collective-permute-done.7.refs_2_.refs_1_.refs_3_, ...), custom_call_target="tpu_custom_call" | custom-call | flops 65536 | bytes 65536 | tf_op jit(solution)/shard_map/onward/pallas_call | solution.py:367
  100.9 3.2 %collective-permute-start.13 = (f32[512,512]{1,0:T(8,128)}, f32[512,512]{1,0:T(8,128)S(1)}, u32[]{:S(2)}, u32[]{:S(2)}) collective-permute-start(f32[512,512]{1,0:T(8,128)} %get-tuple-element.125), channel_id=1, source_target_pairs={{0,3},{1,0},{2,1},{3,2},{4,7},{5,4},{6,5},{7,6},{8,11},{9,8},{10,9... | collective-permute-start | bytes 3145736 | tf_op jit(solution)/shard_map/ppermute | solution.py:707
  104.2 1.9 collective-permute-start.14
  106.1 0.6 add_add_fusion.2
  106.7 21.5 %round.3 = (f32[1024,512]{1,0:T(8,128)}, f32[8,512,128]{2,1,0:T(8,128)}, f32[8,512,128]{2,1,0:T(8,128)}) custom-call(s32[3]{0:T(128)} %get-tuple-element.229.at_ref, f32[1024,512]{1,0:T(8,128)} %get-tuple-element.116.refs_0_, f32[1024,1024]{1,0:T(8,128)} %collective-permute-done.6.refs_1_.refs_0_.refs_2_, ...), custom_call_target="tpu_custom_call", output_to_operand_aliasing={{0}: (1, {})} | custom-call | flops 65536 | bytes 65536 | tf_op jit(solution)/shard_map/round/pallas_call | solution.py:388
  128.5 3.3 %collective-permute-start.11 = (f32[512,512]{1,0:T(8,128)}, f32[512,512]{1,0:T(8,128)}, u32[]{:S(2)}, u32[]{:S(2)}) collective-permute-start(f32[512,512]{1,0:T(8,128)} %get-tuple-element.123), channel_id=1, source_target_pairs={{0,3},{1,0},{2,1},{3,2},{4,7},{5,4},{6,5},{7,6},{8,11},{9,8},{10,9... | collective-permute-start | bytes 3145736 | tf_op jit(solution)/shard_map/ppermute | solution.py:707
  131.7 10.3 %tail.2 = (f32[512,512]{1,0:T(8,128)}, f32[4,136,128]{2,1,0:T(8,128)}, f32[4,512,128]{2,1,0:T(8,128)}, f32[4,512,128]{2,1,0:T(8,128)}) custom-call(s32[3]{0:T(128)} %get-tuple-element.228.at_ref, f32[1024,512]{1,0:T(8,128)} %get-tuple-element.121.refs_0_, f32[512,512]{1,0:T(8,128)} %copy-done.3, f32[512,512]{1,0:T(8,128)} %copy-done.4, f32[512,4096]{1,0:T(8,128)} %refs_4_.5, ...), custom_call_target="tpu_custom_call" | custom-call | flops 65536 | bytes 65536 | tf_op jit(solution)/shard_map/tail/pallas_call | solution.py:418
  142.0 1.3 dynamic-slice_add_fusion.3
  143.3 0.8 pad_maximum_fusion.2
  144.2 2.5 %collective-permute-start.16 = (f32[2,512,128]{2,1,0:T(8,128)}, f32[2,512,128]{2,1,0:T(8,128)}, u32[]{:S(2)}, u32[]{:S(2)}) collective-permute-start(f32[2,512,128]{2,1,0:T(8,128)} %pad_maximum_fusion.2), channel_id=1, source_target_pairs={{0,24},{4,28},{8,16},{12,20},{16,8},{20,12},{24,0},{28,4},{32,56},... | collective-permute-start | bytes 1572872 | tf_op jit(solution)/shard_map/ppermute | solution.py:617
  146.7 1.1 collective-permute-start.17
  147.8 8.9 %backward.3 = (f32[1024,512]{1,0:T(8,128)}, f32[512,512]{1,0:T(8,128)}, f32[512,512]{1,0:T(8,128)}) custom-call(f32[1024,512]{1,0:T(8,128)} %refs_0_.7, f32[1024,512]{1,0:T(8,128)} %k_ref.7, f32[1024,512]{1,0:T(8,128)} %v_ref.7, f32[512,512]{1,0:T(8,128)} %get-tuple-element.136.refs_3_, f32[1024,512]{1,0:T(8,128)} %get-tuple-element.112.local_ref.refs_7_.refs_4_, ...), custom_call_target="tpu_custom_call" | custom-call | flops 65536 | bytes 65536 | tf_op jit(solution)/shard_map/backward/pallas_call | solution.py:502
  156.7 2.6 %collective-permute-done.16 = f32[2,512,128]{2,1,0:T(8,128)} collective-permute-done((f32[2,512,128]{2,1,0:T(8,128)}, f32[2,512,128]{2,1,0:T(8,128)}, u32[]{:S(2)}, u32[]{:S(2)}) %collective-permute-start.16) | collective-permute-done | bytes 524320 | tf_op jit(solution)/shard_map/ppermute | solution.py:617
  159.3 0.9 collective-permute-done.17
  160.2 2.3 %fusion.4 = (f32[512,128]{1,0:T(8,128)}, f32[512,128]{1,0:T(8,128)S(1)}, f32[512,128]{1,0:T(8,128)S(1)}, f32[512,128]{1,0:T(8,128)S(1)}) fusion(f32[2,512,128]{2,1,0:T(8,128)} %collective-permute-done.17, f32[8,512,128]{2,1,0:T(8,128)} %collective-permute-done.15, s32[]{:T(128)S(6)} %select_n.295, f32[8,512,128]{2,1,0:T(8,128)S(1)} %copy-done.2, ...), kind=kLoop, calls=%fused_computation.19 | loop fusion | flops 524288 | bytes 4194320 | tf_op jit(solution)/shard_map/add | solution.py:682
  162.6 1.1 collective-permute-start.18
  163.7 1.0 collective-permute-start.19
  164.7 10.8 %tail.3 = (f32[512,512]{1,0:T(8,128)}, f32[4,136,128]{2,1,0:T(8,128)}, f32[4,512,128]{2,1,0:T(8,128)}, f32[4,512,128]{2,1,0:T(8,128)}) custom-call(s32[3]{0:T(128)} %get-tuple-element.228.at_ref, f32[1024,512]{1,0:T(8,128)} %get-tuple-element.121.refs_0_, f32[512,512]{1,0:T(8,128)} %collective-permute-done.10.refs_1_, ...), custom_call_target="tpu_custom_call" | custom-call | flops 65536 | bytes 65536 | tf_op jit(solution)/shard_map/tail/pallas_call | solution.py:418
  175.7 1.1 slice_select_fusion.2
  177.3 1.3 collective-permute-done.20
  178.6 0.7 fusion.10
  179.3 0.8 pad_maximum_fusion.4
  180.1 2.2 collective-permute-start.23
  182.4 8.5 %backward.4 = (f32[1024,512]{1,0:T(8,128)}, f32[1024,512]{1,0:T(8,128)}, f32[1024,512]{1,0:T(8,128)}) custom-call(f32[1024,512]{1,0:T(8,128)} %refs_0_.7, f32[1024,512]{1,0:T(8,128)} %k_ref.7, f32[1024,512]{1,0:T(8,128)} %v_ref.7, f32[512,512]{1,0:T(8,128)} %get-tuple-element.176.refs_3_, ...), custom_call_target="tpu_custom_call", output_to_operand_aliasing={{0}: (11, {})} | custom-call | flops 65536 | bytes 21600000 | tf_op jit(solution)/shard_map/backward/pallas_call | solution.py:502
  190.9 4.8 %collective-permute-done.23 = f32[2,512,128]{2,1,0:T(8,128)} collective-permute-done((f32[2,512,128]{2,1,0:T(8,128)}, f32[2,512,128]{2,1,0:T(8,128)}, u32[]{:S(2)}, u32[]{:S(2)}) %collective-permute-start.23) | collective-permute-done | bytes 524320 | tf_op jit(solution)/shard_map/ppermute | solution.py:617
  195.6 1.8 fusion.2
  197.4 0.9 add.442
  198.4 2.3 %collective-permute-start.24 = (f32[2,136,128]{2,1,0:T(8,128)S(1)}, f32[2,136,128]{2,1,0:T(8,128)S(1)}, u32[]{:S(2)}, u32[]{:S(2)}) collective-permute-start(f32[2,136,128]{2,1,0:T(8,128)S(1)} %add.442), channel_id=1, source_target_pairs={{0,24},{4,28},{8,16},{12,20},{16,8},{20,12},{24,0},{28,4},{32,56},... | collective-permute-start | bytes 417800 | tf_op jit(solution)/shard_map/ppermute | solution.py:617
  200.7 4.5 %collective-permute-done.25 = f32[512,128]{1,0:T(8,128)S(1)} collective-permute-done((f32[512,128]{1,0:T(8,128)}, f32[512,128]{1,0:T(8,128)S(1)}, u32[]{:S(2)}, u32[]{:S(2)}) %collective-permute-start.25) | collective-permute-done | bytes 262176 | tf_op jit(solution)/shard_map/ppermute | solution.py:617
  205.4 0.6 collective-permute-start.28
  206.0 1.1 collective-permute-start.26
  207.2 8.5 %backward.5 = (f32[1024,512]{1,0:T(8,128)}, f32[1024,512]{1,0:T(8,128)}, f32[1024,512]{1,0:T(8,128)}) custom-call(f32[1024,512]{1,0:T(8,128)} %refs_0_.7, f32[1024,512]{1,0:T(8,128)} %k_ref.7, f32[1024,512]{1,0:T(8,128)} %v_ref.7, f32[512,512]{1,0:T(8,128)} %get-tuple-element.176.refs_3_, ...), custom_call_target="tpu_custom_call", output_to_operand_aliasing={{0}: (11, {}), {1}: (12, {}), {2}: (13, {})} | custom-call | flops 65536 | bytes 21600000 | tf_op jit(solution)/shard_map/backward/pallas_call | solution.py:502
  215.7 2.2 collective-permute-start.27
  217.9 1.0 collective-permute-done.28
  218.9 1.1 fusion
  220.0 1.0 collective-permute-done.27
  221.1 2.2 collective-permute-start.30
  223.5 0.7 pad_maximum_fusion.6.state_ref
  224.2 6.8 %finish.1 = (f32[1024,512]{1,0:T(8,128)}, f32[1024,512]{1,0:T(8,128)}) custom-call(f32[1024,512]{1,0:T(8,128)} %k_ref.7, f32[1024,512]{1,0:T(8,128)} %v_ref.7, f32[1024,512]{1,0:T(8,128)} %get-tuple-element.184.dk_ref, f32[1024,512]{1,0:T(8,128)} %get-tuple-element.185.dv_ref, f32[4,136,128]{2,1,0:T(8,128)} %pad_maximum_fusion.6.state_ref), custom_call_target="tpu_custom_call" | custom-call | flops 65536 | bytes 65536 | tf_op jit(solution)/shard_map/finish/pallas_call | solution.py:805
  231.6 0.8 copy.18
  (74 shorter events, 3.5 us)
Async XLA Ops:
  0.6 93.2 %collective-permute-start.7 = (f32[1024,1024]{1,0:T(8,128)}, f32[1024,1024]{1,0:T(8,128)}, u32[]{:S(2)}, u32[]{:S(2)}) collective-permute-start(f32[1024,1024]{1,0:T(8,128)} %refs_0_.4), channel_id=1, source_target_pairs={{0,3},{1,0},{2,1},{3,2},{4,7},{5,4},{6,5},{7,6},{8,11},{9,8},{10,9... | collective-permute-start | bytes 12582920 | tf_op jit(solution)/shard_map/ppermute | solution.py:707
  3.7 93.6 %collective-permute-start.6 = (f32[1024,1024]{1,0:T(8,128)}, f32[1024,1024]{1,0:T(8,128)}, u32[]{:S(2)}, u32[]{:S(2)}) collective-permute-start(f32[1024,1024]{1,0:T(8,128)} %refs_0_.4), channel_id=1, source_target_pairs={{0,1},{1,2},{2,3},{3,0},{4,5},{5,6},{6,7},{7,4},{8,9},{9,10},{10,1... | collective-permute-start | bytes 12582920 | tf_op jit(solution)/shard_map/ppermute | solution.py:704
  9.4 1.4 collective-permute-start
  11.9 8.4 %collective-permute-start.1 = (f32[2,136,128]{2,1,0:T(8,128)S(1)}, f32[2,136,128]{2,1,0:T(8,128)S(1)}, u32[]{:S(2)}, u32[]{:S(2)}) collective-permute-start(f32[2,136,128]{2,1,0:T(8,128)S(1)} %fusion.11), channel_id=1, source_target_pairs={{0,8},{4,12},{8,0},{12,4},{16,24},{20,28},{24,16},{28,20},{32,40},... | collective-permute-start | bytes 417800 | tf_op jit(solution)/shard_map/ppermute | solution.py:617
  20.3 6.7 %collective-permute-start.2 = (f32[2,136,128]{2,1,0:T(8,128)S(1)}, f32[2,136,128]{2,1,0:T(8,128)S(1)}, u32[]{:S(2)}, u32[]{:S(2)}) collective-permute-start(f32[2,136,128]{2,1,0:T(8,128)S(1)} %add.378), channel_id=1, source_target_pairs={{0,24},{4,28},{8,16},{12,20},{16,8},{20,12},{24,0},{28,4},{32,56},... | collective-permute-start | bytes 417800 | tf_op jit(solution)/shard_map/ppermute | solution.py:617
  27.1 12.9 %copy-start = (f32[4,136,128]{2,1,0:T(8,128)S(1)}, f32[4,136,128]{2,1,0:T(8,128)}, u32[]{:S(2)}) copy-start(f32[4,136,128]{2,1,0:T(8,128)} %update.1) | copy-start | bytes 835588
  27.1 13.1 %copy-start.8 = (f32[4]{0:T(128)S(1)}, f32[4]{0:T(128)}, u32[]{:S(2)}) copy-start(f32[4]{0:T(128)} %param.9) | copy-start | bytes 52
  27.1 7.7 %collective-permute-start.3 = (f32[2,136,128]{2,1,0:T(8,128)S(1)}, f32[2,136,128]{2,1,0:T(8,128)S(1)}, u32[]{:S(2)}, u32[]{:S(2)}) collective-permute-start(f32[2,136,128]{2,1,0:T(8,128)S(1)} %add.379), channel_id=1, source_target_pairs={{0,32},{4,36},{8,40},{12,44},{16,48},{20,52},{24,56},{28,60},{32,0... | collective-permute-start | bytes 417800 | tf_op jit(solution)/shard_map/ppermute | solution.py:617
  34.8 5.1 %collective-permute-start.4 = (f32[2,136,128]{2,1,0:T(8,128)S(1)}, f32[2,136,128]{2,1,0:T(8,128)S(1)}, u32[]{:S(2)}, u32[]{:S(2)}) collective-permute-start(f32[2,136,128]{2,1,0:T(8,128)S(1)} %add.380), channel_id=1, source_target_pairs={{0,96},{4,100},{8,104},{12,108},{16,112},{20,116},{24,120},{28,124... | collective-permute-start | bytes 417800 | tf_op jit(solution)/shard_map/ppermute | solution.py:617
  40.0 1.4 collective-permute-start.5
  60.9 19.4 %copy-start.6 = (f32[4,512,128]{2,1,0:T(8,128)S(1)}, f32[4,512,128]{2,1,0:T(8,128)}, u32[]{:S(2)}) copy-start(f32[4,512,128]{2,1,0:T(8,128)} %get-tuple-element.117) | copy-start | bytes 3145732
  60.9 3.0 %collective-permute-start.8 = (f32[4,512,128]{2,1,0:T(8,128)}, f32[4,512,128]{2,1,0:T(8,128)S(1)}, u32[]{:S(2)}, u32[]{:S(2)}) collective-permute-start(f32[4,512,128]{2,1,0:T(8,128)} %get-tuple-element.118), channel_id=1, source_target_pairs={{0,4},{4,0},{8,12},{12,8},{16,20},{20,16},{24,28},{28,24},{32,36},... | collective-permute-start | bytes 3145736 | tf_op jit(solution)/shard_map/ppermute | solution.py:605
  65.0 15.3 %collective-permute-start.9 = (f32[2,512,128]{2,1,0:T(8,128)S(1)}, f32[2,512,128]{2,1,0:T(8,128)S(1)}, u32[]{:S(2)}, u32[]{:S(2)}) collective-permute-start(f32[2,512,128]{2,1,0:T(8,128)S(1)} %pad_maximum_fusion.1), channel_id=1, source_target_pairs={{0,24},{4,28},{8,16},{12,20},{16,8},{20,12},{24,0},{28,4},{32,56},... | collective-permute-start | bytes 1572872 | tf_op jit(solution)/shard_map/ppermute | solution.py:617
  100.9 27.3 %collective-permute-start.12 = (f32[512,512]{1,0:T(8,128)}, f32[512,512]{1,0:T(8,128)S(1)}, u32[]{:S(2)}, u32[]{:S(2)}) collective-permute-start(f32[512,512]{1,0:T(8,128)} %get-tuple-element.124), channel_id=1, source_target_pairs={{0,1},{1,2},{2,3},{3,0},{4,5},{5,6},{6,7},{7,4},{8,9},{9,10},{10,1... | collective-permute-start | bytes 3145736 | tf_op jit(solution)/shard_map/ppermute | solution.py:704
  100.9 27.3 %collective-permute-start.13 = (f32[512,512]{1,0:T(8,128)}, f32[512,512]{1,0:T(8,128)S(1)}, u32[]{:S(2)}, u32[]{:S(2)}) collective-permute-start(f32[512,512]{1,0:T(8,128)} %get-tuple-element.125), channel_id=1, source_target_pairs={{0,3},{1,0},{2,1},{3,2},{4,7},{5,4},{6,5},{7,6},{8,11},{9,8},{10,9... | collective-permute-start | bytes 3145736 | tf_op jit(solution)/shard_map/ppermute | solution.py:707
  104.2 24.0 %collective-permute-start.14 = (f32[512,128]{1,0:T(8,128)S(1)}, f32[512,128]{1,0:T(8,128)S(1)}, u32[]{:S(2)}, u32[]{:S(2)}) collective-permute-start(f32[512,128]{1,0:T(8,128)S(1)} %get-tuple-element.129), channel_id=1, source_target_pairs={{0,8},{4,12},{8,0},{12,4},{16,24},{20,28},{24,16},{28,20},{32,40},... | collective-permute-start | bytes 786440 | tf_op jit(solution)/shard_map/ppermute | solution.py:617
  106.7 21.5 %copy-start.7 = (f32[512,128]{1,0:T(8,128)S(1)}, f32[512,128]{1,0:T(8,128)}, u32[]{:S(2)}) copy-start(f32[512,128]{1,0:T(8,128)} %get-tuple-element.128) | copy-start | bytes 786436
  128.2 3.5 %copy-start.3 = (f32[512,512]{1,0:T(8,128)}, f32[512,512]{1,0:T(8,128)S(1)}, u32[]{:S(2)}) copy-start(f32[512,512]{1,0:T(8,128)S(1)} %collective-permute-done.12.refs_1_) | copy-start | bytes 3145732
  128.3 3.5 %copy-start.4 = (f32[512,512]{1,0:T(8,128)}, f32[512,512]{1,0:T(8,128)S(1)}, u32[]{:S(2)}) copy-start(f32[512,512]{1,0:T(8,128)S(1)} %collective-permute-done.13.refs_2_) | copy-start | bytes 3145732
  128.3 13.7 %collective-permute-start.15 = (f32[8,512,128]{2,1,0:T(8,128)}, f32[8,512,128]{2,1,0:T(8,128)}, u32[]{:S(2)}, u32[]{:S(2)}) collective-permute-start(f32[8,512,128]{2,1,0:T(8,128)} %get-tuple-element.135), channel_id=1, source_target_pairs={{0,4},{4,0},{8,12},{12,8},{16,20},{20,16},{24,28},{28,24},{32,36},... | collective-permute-start | bytes 6291464 | tf_op jit(solution)/shard_map/ppermute | solution.py:605
  128.4 34.2 %collective-permute-start.10 = (f32[512,512]{1,0:T(8,128)}, f32[512,512]{1,0:T(8,128)}, u32[]{:S(2)}, u32[]{:S(2)}) collective-permute-start(f32[512,512]{1,0:T(8,128)} %get-tuple-element.122), channel_id=1, source_target_pairs={{0,1},{1,2},{2,3},{3,0},{4,5},{5,6},{6,7},{7,4},{8,9},{9,10},{10,1... | collective-permute-start | bytes 3145736 | tf_op jit(solution)/shard_map/ppermute | solution.py:704
  128.5 34.1 %collective-permute-start.11 = (f32[512,512]{1,0:T(8,128)}, f32[512,512]{1,0:T(8,128)}, u32[]{:S(2)}, u32[]{:S(2)}) collective-permute-start(f32[512,512]{1,0:T(8,128)} %get-tuple-element.123), channel_id=1, source_target_pairs={{0,3},{1,0},{2,1},{3,2},{4,7},{5,4},{6,5},{7,6},{8,11},{9,8},{10,9... | collective-permute-start | bytes 3145736 | tf_op jit(solution)/shard_map/ppermute | solution.py:707
  131.7 10.3 %copy-start.2 = (f32[8,512,128]{2,1,0:T(8,128)S(1)}, f32[8,512,128]{2,1,0:T(8,128)}, u32[]{:S(2)}) copy-start(f32[8,512,128]{2,1,0:T(8,128)} %get-tuple-element.141) | copy-start | bytes 6291460
  144.2 15.2 %collective-permute-start.16 = (f32[2,512,128]{2,1,0:T(8,128)}, f32[2,512,128]{2,1,0:T(8,128)}, u32[]{:S(2)}, u32[]{:S(2)}) collective-permute-start(f32[2,512,128]{2,1,0:T(8,128)} %pad_maximum_fusion.2), channel_id=1, source_target_pairs={{0,24},{4,28},{8,16},{12,20},{16,8},{20,12},{24,0},{28,4},{32,56},... | collective-permute-start | bytes 1572872 | tf_op jit(solution)/shard_map/ppermute | solution.py:617
  146.7 13.5 %collective-permute-start.17 = (f32[2,512,128]{2,1,0:T(8,128)S(1)}, f32[2,512,128]{2,1,0:T(8,128)}, u32[]{:S(2)}, u32[]{:S(2)}) collective-permute-start(f32[2,512,128]{2,1,0:T(8,128)S(1)} %pad_maximum_fusion.3), channel_id=1, source_target_pairs={{0,8},{4,12},{8,0},{12,4},{16,24},{20,28},{24,16},{28,20},{32,40},... | collective-permute-start | bytes 1572872 | tf_op jit(solution)/shard_map/ppermute | solution.py:617
  162.6 12.9 %collective-permute-start.18 = (f32[512,128]{1,0:T(8,128)S(1)}, f32[512,128]{1,0:T(8,128)S(1)}, u32[]{:S(2)}, u32[]{:S(2)}) collective-permute-start(f32[512,128]{1,0:T(8,128)S(1)} %get-tuple-element.151), channel_id=1, source_target_pairs={{0,8},{4,12},{8,0},{12,4},{16,24},{20,28},{24,16},{28,20},{32,40},... | collective-permute-start | bytes 786440 | tf_op jit(solution)/shard_map/ppermute | solution.py:617
  163.7 11.9 %collective-permute-start.19 = (f32[512,128]{1,0:T(8,128)}, f32[512,128]{1,0:T(8,128)S(1)}, u32[]{:S(2)}, u32[]{:S(2)}) collective-permute-start(f32[512,128]{1,0:T(8,128)} %get-tuple-element.153), channel_id=1, source_target_pairs={{0,24},{4,28},{8,16},{12,20},{16,8},{20,12},{24,0},{28,4},{32,56},... | collective-permute-start | bytes 786440 | tf_op jit(solution)/shard_map/ppermute | solution.py:617
  175.5 3.1 %copy-start.1 = (f32[4,136,128]{2,1,0:T(8,128)S(1)}, f32[4,136,128]{2,1,0:T(8,128)}, u32[]{:S(2)}) copy-start(f32[4,136,128]{2,1,0:T(8,128)} %get-tuple-element.154) | copy-start | bytes 835588
  175.5 3.7 %copy-start.5 = (f32[4,512,128]{2,1,0:T(8,128)S(1)}, f32[4,512,128]{2,1,0:T(8,128)}, u32[]{:S(2)}) copy-start(f32[4,512,128]{2,1,0:T(8,128)} %get-tuple-element.155) | copy-start | bytes 3145732
  175.6 3.6 %collective-permute-start.22 = (f32[4,512,128]{2,1,0:T(8,128)}, f32[4,512,128]{2,1,0:T(8,128)S(1)}, u32[]{:S(2)}, u32[]{:S(2)}) collective-permute-start(f32[4,512,128]{2,1,0:T(8,128)} %get-tuple-element.157), channel_id=1, source_target_pairs={{0,4},{4,0},{8,12},{12,8},{16,20},{20,16},{24,28},{28,24},{32,36},... | collective-permute-start | bytes 3145736 | tf_op jit(solution)/shard_map/ppermute | solution.py:605
  176.8 1.7 collective-permute-start.20
  180.1 15.5 %collective-permute-start.23 = (f32[2,512,128]{2,1,0:T(8,128)}, f32[2,512,128]{2,1,0:T(8,128)}, u32[]{:S(2)}, u32[]{:S(2)}) collective-permute-start(f32[2,512,128]{2,1,0:T(8,128)} %pad_maximum_fusion.4), channel_id=1, source_target_pairs={{0,24},{4,28},{8,16},{12,20},{16,8},{20,12},{24,0},{28,4},{32,56},... | collective-permute-start | bytes 1572872 | tf_op jit(solution)/shard_map/ppermute | solution.py:617
  182.4 15.0 %collective-permute-start.21 = (f32[2,136,128]{2,1,0:T(8,128)}, f32[2,136,128]{2,1,0:T(8,128)S(1)}, u32[]{:S(2)}, u32[]{:S(2)}) collective-permute-start(f32[2,136,128]{2,1,0:T(8,128)} %fusion.10), channel_id=1, source_target_pairs={{0,8},{4,12},{8,0},{12,4},{16,24},{20,28},{24,16},{28,20},{32,40},... | collective-permute-start | bytes 417800 | tf_op jit(solution)/shard_map/ppermute | solution.py:617
  197.4 7.7 %collective-permute-start.25 = (f32[512,128]{1,0:T(8,128)}, f32[512,128]{1,0:T(8,128)S(1)}, u32[]{:S(2)}, u32[]{:S(2)}) collective-permute-start(f32[512,128]{1,0:T(8,128)} %get-tuple-element.170), channel_id=1, source_target_pairs={{0,8},{4,12},{8,0},{12,4},{16,24},{20,28},{24,16},{28,20},{32,40},... | collective-permute-start | bytes 786440 | tf_op jit(solution)/shard_map/ppermute | solution.py:617
  198.4 6.8 %collective-permute-start.24 = (f32[2,136,128]{2,1,0:T(8,128)S(1)}, f32[2,136,128]{2,1,0:T(8,128)S(1)}, u32[]{:S(2)}, u32[]{:S(2)}) collective-permute-start(f32[2,136,128]{2,1,0:T(8,128)S(1)} %add.442), channel_id=1, source_target_pairs={{0,24},{4,28},{8,16},{12,20},{16,8},{20,12},{24,0},{28,4},{32,56},... | collective-permute-start | bytes 417800 | tf_op jit(solution)/shard_map/ppermute | solution.py:617
  205.4 13.5 %collective-permute-start.28 = (f32[2,512,128]{2,1,0:T(8,128)S(1)}, f32[2,512,128]{2,1,0:T(8,128)}, u32[]{:S(2)}, u32[]{:S(2)}) collective-permute-start(f32[2,512,128]{2,1,0:T(8,128)S(1)} %pad_maximum_fusion.5), channel_id=1, source_target_pairs={{0,96},{4,100},{8,104},{12,108},{16,112},{20,116},{24,120},{28,124... | collective-permute-start | bytes 1572872 | tf_op jit(solution)/shard_map/ppermute | solution.py:617
  206.0 9.6 %collective-permute-start.26 = (f32[2,136,128]{2,1,0:T(8,128)S(1)}, f32[2,136,128]{2,1,0:T(8,128)S(1)}, u32[]{:S(2)}, u32[]{:S(2)}) collective-permute-start(f32[2,136,128]{2,1,0:T(8,128)S(1)} %add.444), channel_id=1, source_target_pairs={{0,32},{4,36},{8,40},{12,44},{16,48},{20,52},{24,56},{28,60},{32,0... | collective-permute-start | bytes 417800 | tf_op jit(solution)/shard_map/ppermute | solution.py:617
  215.7 5.3 %collective-permute-start.27 = (f32[2,136,128]{2,1,0:T(8,128)S(1)}, f32[2,136,128]{2,1,0:T(8,128)S(1)}, u32[]{:S(2)}, u32[]{:S(2)}) collective-permute-start(f32[2,136,128]{2,1,0:T(8,128)S(1)} %add.450), channel_id=1, source_target_pairs={{0,96},{4,100},{8,104},{12,108},{16,112},{20,116},{24,120},{28,124... | collective-permute-start | bytes 417800 | tf_op jit(solution)/shard_map/ppermute | solution.py:617
  221.0 2.3 %collective-permute-start.29 = (f32[2,136,128]{2,1,0:T(8,128)S(1)}, f32[2,136,128]{2,1,0:T(8,128)S(1)}, u32[]{:S(2)}, u32[]{:S(2)}) collective-permute-start(f32[2,136,128]{2,1,0:T(8,128)S(1)} %get-tuple-element.198), channel_id=1, source_target_pairs={{0,4},{4,0},{8,12},{12,8},{16,20},{20,16},{24,28},{28,24},{32,36},... | collective-permute-start | bytes 417800 | tf_op jit(solution)/shard_map/ppermute | solution.py:605
  221.1 10.5 %collective-permute-start.30 = (f32[512,128]{1,0:T(8,128)S(1)}, f32[512,128]{1,0:T(8,128)S(1)}, u32[]{:S(2)}, u32[]{:S(2)}) collective-permute-start(f32[512,128]{1,0:T(8,128)S(1)} %get-tuple-element.192), channel_id=1, source_target_pairs={{0,32},{4,36},{8,40},{12,44},{16,48},{20,52},{24,56},{28,60},{32,0... | collective-permute-start | bytes 786440 | tf_op jit(solution)/shard_map/ppermute | solution.py:617

commit v3 on v2

--- a/solution.py
+++ b/solution.py
@@ -354,12 +354,12 @@
 
 
 def onward_kernel(*refs):
-    for source, target in zip(refs[:4], refs[4:]):
+    for source, target in zip(refs[:2], refs[2:]):
         target[...] = source[...]
 
 
-def onward_of(left, right):
-    rows, half, step = MOST, left.shape[1] // 2, MOST // 2
+def onward_of(block, column):
+    rows, half, step = MOST, block.shape[1] // 2, MOST // 2
 
     def rows_from(first, column):
         return pl.BlockSpec((step, half), lambda i: (i + first // step, column))
@@ -367,13 +367,13 @@
     return pl.pallas_call(
         onward_kernel,
         grid=(rows // step,),
-        in_specs=[rows_from(0, 0), rows_from(0, 1), rows_from(MOST, 0), rows_from(MOST, 1)],
-        out_specs=[rows_from(0, 0)] * 4,
-        out_shape=[jax.ShapeDtypeStruct((rows, half), f32)] * 4,
+        in_specs=[rows_from(0, column), rows_from(MOST, column)],
+        out_specs=[rows_from(0, 0)] * 2,
+        out_shape=[jax.ShapeDtypeStruct((rows, half), f32)] * 2,
         compiler_params=pltpu.CompilerParams(vmem_limit_bytes=VMEM_LIMIT),
         cost_estimate=pl.CostEstimate(flops=LIGHT, bytes_accessed=LIGHT, transcendentals=0),
         name="onward",
-    )(left, right, left, right)
+    )(block, block)
 
 
 def round_of(acc, blocks, places, out_weight, mixed, core, first=0, before=(), micros=0):
@@ -738,9 +738,9 @@
     came_own = core_swap(send_own)
     own_parts = half_scattered(chip_piece(mine_own, came_own), "z", z, across, beside)
     left, right, *own_parts = lax.optimization_barrier((left, right, *own_parts))
-    onward = onward_of(left, right)
-    far_1 = up(onward[0]), down(onward[1])
-    far_2 = up(onward[2]), down(onward[3])
+    left_on, right_on = onward_of(left, 0), onward_of(right, 1)
+    far_1 = up(left_on[0]), down(right_on[0])
+    far_2 = up(left_on[1]), down(right_on[1])
 
     mg, mine_sides, send_sides = add(mg, [left, right], [left_at, right_at])
     sum_own = scattered(*own_parts, "z", beside)

time: 236 us -> 235 us (level)
  waiting for transfers between devices: 58.8 us -> 55.2 us
    ppermute x3, waiting for transfers between devices: 12.8 us -> 0.02 us  [down(): return lax.ppermute(block, 'head', ring(hs, -1))]
    ppermute x3, waiting for transfers between devices: 3.42 us -> 13.4 us  [up(): return lax.ppermute(block, 'head', ring(hs, 1))]
    ppermute x3, starting transfers between devices: 0.08 us -> 3.69 us  [up(): return lax.ppermute(block, 'head', ring(hs, 1))]
    ppermute x3, starting transfers between devices: 9.57 us -> 6.19 us  [down(): return lax.ppermute(block, 'head', ring(hs, -1))]
    pallas_call x1 -> x2, Pallas kernels: 3.66 us -> 5.24 us  [onward_of(): pl.pallas_call(onward_kernel, grid=(rows // step,), in_specs=[rows_from(0...]
  transfers between devices with their start and end apart: 31 -> 31, of which waited for: 15 -> 15; matrix products, arithmetic and copies ran while one was open for 8% -> 8% of each run, Pallas kernels for 48% -> 49%
where the time goes in v3:
time: 235 us; the launch traced here: 231 us
  Pallas kernels  116 us (49%)
  waiting for transfers between devices  55.2 us (23%)
  starting transfers between devices  38.5 us (16%)
  other arithmetic  18.9 us (8%)
    ppermute x18, waiting for transfers between devices, moved(): return lax.ppermute(block, 'ctx', pairs)  35.7 us
    pallas_call x2, Pallas kernels, round_of(): pl.pallas_call(functools.partial(block_kernel, blocks=n, added=len(acc),...  33.5 us
    ppermute x18, starting transfers between devices, moved(): return lax.ppermute(block, 'ctx', pairs)  27.5 us
    pallas_call x3, Pallas kernels, backward_of(): pl.pallas_call(functools.partial(backward_kernel, first=second * MOST), g...  25.8 us
    pallas_call x2, Pallas kernels, tail_of(): pl.pallas_call(tail_kernel, grid_spec=pltpu.PrefetchScalarGridSpec(num_sc...  21.1 us
    ppermute x3, waiting for transfers between devices, up(): return lax.ppermute(block, 'head', ring(hs, 1))  13.4 us
    pallas_call x2, Pallas kernels, forward_of(): pl.pallas_call(forward_kernel, grid=(count,), in_specs=[column] * 3 + [pl...  12.8 us
    pallas_call x1, Pallas kernels, on_device(): per_head(finish_kernel, heads, 'ccccs', 'cc', 'finish')  6.77 us
  transfers between devices with their start and end apart: 31, of which 15 were waited for; matrix products, arithmetic and copies ran while one was open for 8% of the time, Pallas kernels for 49%

profile of v3, /device:TPU:4, one launch (start us, length us, event | category | flops | bytes accessed | tf_op | source)
XLA Modules:
  0.0 231.1 jit_solution(17268940244463750244)
XLA Ops:
  0.6 1.6 collective-permute-start.6
  2.3 1.7 collective-permute-start.7
  3.9 4.7 %update.1 = f32[4,136,128]{2,1,0:T(8,128)} custom-call(f32[1024,512]{1,0:T(8,128)} %k_ref.7, f32[1024,512]{1,0:T(8,128)} %v_ref.7), custom_call_target="tpu_custom_call" | custom-call | flops 65536 | bytes 65536 | tf_op jit(solution)/shard_map/update/pallas_call | solution.py:714
  8.7 1.0 slice_select_fusion
  9.8 1.3 collective-permute-done
  11.1 1.0 fusion.11
  12.1 2.0 collective-permute-start.1
  14.1 6.4 %forward.2 = (f32[1024,512]{1,0:T(8,128)}, f32[4,1,1024]{2,1,0:T(1,128)}) custom-call(f32[1024,512]{1,0:T(8,128)} %refs_0_.7, f32[1024,512]{1,0:T(8,128)} %k_ref.7, f32[1024,512]{1,0:T(8,128)} %v_ref.7), custom_call_target="tpu_custom_call" | custom-call | flops 65536 | bytes 65536 | tf_op jit(solution)/shard_map/forward/pallas_call | solution.py:525
  20.5 2.6 %collective-permute-start.2 = (f32[2,136,128]{2,1,0:T(8,128)S(1)}, f32[2,136,128]{2,1,0:T(8,128)S(1)}, u32[]{:S(2)}, u32[]{:S(2)}) collective-permute-start(f32[2,136,128]{2,1,0:T(8,128)S(1)} %add.378), channel_id=1, source_target_pairs={{0,24},{4,28},{8,16},{12,20},{16,8},{20,12},{24,0},{28,4},{32,56},... | collective-permute-start | bytes 417800 | tf_op jit(solution)/shard_map/ppermute | solution.py:617
  23.1 4.1 %collective-permute-done.2 = f32[2,136,128]{2,1,0:T(8,128)S(1)} collective-permute-done((f32[2,136,128]{2,1,0:T(8,128)S(1)}, f32[2,136,128]{2,1,0:T(8,128)S(1)}, u32[]{:S(2)}, u32[]{:S(2)}) %collective-permute-start.2) | collective-permute-done | bytes 139296 | tf_op jit(solution)/shard_map/ppermute | solution.py:617
  27.3 1.3 collective-permute-start.3
  28.6 6.4 %forward.3 = (f32[1024,512]{1,0:T(8,128)}, f32[4,1,1024]{2,1,0:T(1,128)}) custom-call(f32[1024,512]{1,0:T(8,128)} %refs_0_.7, f32[1024,512]{1,0:T(8,128)} %k_ref.7, f32[1024,512]{1,0:T(8,128)} %v_ref.7, f32[1024,512]{1,0:T(8,128)} %get-tuple-element.105.refs_0_, f32[4,1,1024]{2,1,0:T(1,128)} %get-tuple-element.106.refs_1_), custom_call_target="tpu_custom_call", output_to_operand_aliasing={{0}: (3, {}), {1}: (4, {})} | custom-call | flops 65536 | bytes 65536 | tf_op jit(solution)/shard_map/forward/pallas_call | solution.py:525
  35.2 4.9 %collective-permute-done.4 = f32[2,136,128]{2,1,0:T(8,128)S(1)} collective-permute-done((f32[2,136,128]{2,1,0:T(8,128)S(1)}, f32[2,136,128]{2,1,0:T(8,128)S(1)}, u32[]{:S(2)}, u32[]{:S(2)}) %collective-permute-start.4) | collective-permute-done | bytes 139296 | tf_op jit(solution)/shard_map/ppermute | solution.py:617
  41.0 0.7 collective-permute-done.5
  41.8 0.7 pad_maximum_fusion.7.mem_ref.refs_7_
  42.5 0.6 broadcast_in_dim.59.g_ref.refs_8_
  43.2 5.8 %mix.1 = (bf16[512,1024]{1,0:T(8,128)(2,1)}, bf16[512,1024]{1,0:T(8,128)(2,1)}, f32[1024,512]{1,0:T(8,128)}, f32[1024,512]{1,0:T(8,128)}) custom-call(f32[1024,512]{1,0:T(8,128)} %refs_0_.7, f32[1024,512]{1,0:T(8,128)} %get-tuple-element.112.local_ref.refs_7_.refs_4_, f32[4,136,128]{2,1,0:T(8,128)} %pad_maximum_fusion.7.mem_ref.refs_7_, ...), custom_call_target="tpu_custom_call" | custom-call | flops 65536 | bytes 65536 | tf_op jit(solution)/shard_map/mix/pallas_call | solution.py:724
  49.0 12.1 %round.2 = (f32[1024,512]{1,0:T(8,128)}, f32[4,512,128]{2,1,0:T(8,128)}, f32[4,512,128]{2,1,0:T(8,128)}) custom-call(s32[2]{0:T(128)} %pad_add_fusion.at_ref, f32[1024,1024]{1,0:T(8,128)} %refs_0_.4, f32[512,4096]{1,0:T(8,128)} %refs_4_.5, bf16[512,1024]{1,0:T(8,128)(2,1)} %get-tuple-element.114.refs_2_.refs_5_.refs_8_, ...), custom_call_target="tpu_custom_call" | custom-call | flops 65536 | bytes 65536 | tf_op jit(solution)/shard_map/round/pallas_call | solution.py:388
  61.3 2.7 %collective-permute-done.8 = f32[4,512,128]{2,1,0:T(8,128)S(1)} collective-permute-done((f32[4,512,128]{2,1,0:T(8,128)}, f32[4,512,128]{2,1,0:T(8,128)S(1)}, u32[]{:S(2)}, u32[]{:S(2)}) %collective-permute-start.8) | collective-permute-done | bytes 1048608 | tf_op jit(solution)/shard_map/ppermute | solution.py:605
  64.1 1.1 dynamic-slice_add_fusion.7
  65.2 2.6 %collective-permute-start.9 = (f32[2,512,128]{2,1,0:T(8,128)S(1)}, f32[2,512,128]{2,1,0:T(8,128)S(1)}, u32[]{:S(2)}, u32[]{:S(2)}) collective-permute-start(f32[2,512,128]{2,1,0:T(8,128)S(1)} %pad_maximum_fusion.1), channel_id=1, source_target_pairs={{0,24},{4,28},{8,16},{12,20},{16,8},{20,12},{24,0},{28,4},{32,56},... | collective-permute-start | bytes 1572872 | tf_op jit(solution)/shard_map/ppermute | solution.py:617
  67.8 12.7 %collective-permute-done.9 = f32[2,512,128]{2,1,0:T(8,128)S(1)} collective-permute-done((f32[2,512,128]{2,1,0:T(8,128)S(1)}, f32[2,512,128]{2,1,0:T(8,128)S(1)}, u32[]{:S(2)}, u32[]{:S(2)}) %collective-permute-start.9) | collective-permute-done | bytes 524320 | tf_op jit(solution)/shard_map/ppermute | solution.py:617
  80.5 0.8 fusion.8
  81.2 13.4 %collective-permute-done.6.refs_1_.refs_0_ = f32[1024,1024]{1,0:T(8,128)} collective-permute-done((f32[1024,1024]{1,0:T(8,128)}, f32[1024,1024]{1,0:T(8,128)}, u32[]{:S(2)}, u32[]{:S(2)}) %collective-permute-start.6) | collective-permute-done | bytes 4194336 | tf_op jit(solution)/shard_map/ppermute | solution.py:704
  94.6 2.6 %onward.2 = (f32[512,512]{1,0:T(8,128)}, f32[512,512]{1,0:T(8,128)}) custom-call(f32[1024,1024]{1,0:T(8,128)} %collective-permute-done.6.refs_1_.refs_0_, f32[1024,1024]{1,0:T(8,128)} %collective-permute-done.6.refs_1_.refs_0_), custom_call_target="tpu_custom_call" | custom-call | flops 65536 | bytes 65536 | tf_op jit(solution)/shard_map/onward/pallas_call | solution.py:367
  97.3 1.6 collective-permute-start.12
  98.8 2.6 %onward.3 = (f32[512,512]{1,0:T(8,128)}, f32[512,512]{1,0:T(8,128)}) custom-call(f32[1024,1024]{1,0:T(8,128)} %collective-permute-done.7.refs_2_.refs_0_.refs_1_, f32[1024,1024]{1,0:T(8,128)} %collective-permute-done.7.refs_2_.refs_0_.refs_1_), custom_call_target="tpu_custom_call" | custom-call | flops 65536 | bytes 65536 | tf_op jit(solution)/shard_map/onward/pallas_call | solution.py:367
  101.4 1.7 collective-permute-start.13
  103.1 1.9 collective-permute-start.14
  105.6 21.4 %round.3 = (f32[1024,512]{1,0:T(8,128)}, f32[8,512,128]{2,1,0:T(8,128)}, f32[8,512,128]{2,1,0:T(8,128)}) custom-call(s32[3]{0:T(128)} %get-tuple-element.229.at_ref, f32[1024,512]{1,0:T(8,128)} %get-tuple-element.116.refs_0_, f32[1024,1024]{1,0:T(8,128)} %collective-permute-done.6.refs_1_.refs_0_, ...), custom_call_target="tpu_custom_call", output_to_operand_aliasing={{0}: (1, {})} | custom-call | flops 65536 | bytes 65536 | tf_op jit(solution)/shard_map/round/pallas_call | solution.py:388
  127.7 2.9 %collective-permute-start.11 = (f32[512,512]{1,0:T(8,128)}, f32[512,512]{1,0:T(8,128)}, u32[]{:S(2)}, u32[]{:S(2)}) collective-permute-start(f32[512,512]{1,0:T(8,128)} %get-tuple-element.123), channel_id=1, source_target_pairs={{0,3},{1,0},{2,1},{3,2},{4,7},{5,4},{6,5},{7,6},{8,11},{9,8},{10,9... | collective-permute-start | bytes 3145736 | tf_op jit(solution)/shard_map/ppermute | solution.py:707
  130.6 10.3 %tail.2 = (f32[512,512]{1,0:T(8,128)}, f32[4,136,128]{2,1,0:T(8,128)}, f32[4,512,128]{2,1,0:T(8,128)}, f32[4,512,128]{2,1,0:T(8,128)}) custom-call(s32[3]{0:T(128)} %get-tuple-element.228.at_ref, f32[1024,512]{1,0:T(8,128)} %get-tuple-element.121.refs_0_, f32[512,512]{1,0:T(8,128)} %copy-done.3, f32[512,512]{1,0:T(8,128)} %copy-done.4, f32[512,4096]{1,0:T(8,128)} %refs_4_.5, ...), custom_call_target="tpu_custom_call" | custom-call | flops 65536 | bytes 65536 | tf_op jit(solution)/shard_map/tail/pallas_call | solution.py:418
  140.9 1.3 dynamic-slice_add_fusion.3
  142.2 0.8 pad_maximum_fusion.2
  143.0 2.5 %collective-permute-start.16 = (f32[2,512,128]{2,1,0:T(8,128)}, f32[2,512,128]{2,1,0:T(8,128)}, u32[]{:S(2)}, u32[]{:S(2)}) collective-permute-start(f32[2,512,128]{2,1,0:T(8,128)} %pad_maximum_fusion.2), channel_id=1, source_target_pairs={{0,24},{4,28},{8,16},{12,20},{16,8},{20,12},{24,0},{28,4},{32,56},... | collective-permute-start | bytes 1572872 | tf_op jit(solution)/shard_map/ppermute | solution.py:617
  145.6 1.1 collective-permute-start.17
  146.7 8.9 %backward.3 = (f32[1024,512]{1,0:T(8,128)}, f32[512,512]{1,0:T(8,128)}, f32[512,512]{1,0:T(8,128)}) custom-call(f32[1024,512]{1,0:T(8,128)} %refs_0_.7, f32[1024,512]{1,0:T(8,128)} %k_ref.7, f32[1024,512]{1,0:T(8,128)} %v_ref.7, f32[512,512]{1,0:T(8,128)} %get-tuple-element.136.refs_3_, f32[1024,512]{1,0:T(8,128)} %get-tuple-element.112.local_ref.refs_7_.refs_4_, ...), custom_call_target="tpu_custom_call" | custom-call | flops 65536 | bytes 65536 | tf_op jit(solution)/shard_map/backward/pallas_call | solution.py:502
  155.6 2.6 %collective-permute-done.16 = f32[2,512,128]{2,1,0:T(8,128)} collective-permute-done((f32[2,512,128]{2,1,0:T(8,128)}, f32[2,512,128]{2,1,0:T(8,128)}, u32[]{:S(2)}, u32[]{:S(2)}) %collective-permute-start.16) | collective-permute-done | bytes 524320 | tf_op jit(solution)/shard_map/ppermute | solution.py:617
  158.2 0.9 collective-permute-done.17
  159.1 2.3 %fusion.4 = (f32[512,128]{1,0:T(8,128)S(1)}, f32[512,128]{1,0:T(8,128)S(1)}, f32[512,128]{1,0:T(8,128)S(1)}, f32[512,128]{1,0:T(8,128)}) fusion(f32[2,512,128]{2,1,0:T(8,128)} %collective-permute-done.17, f32[8,512,128]{2,1,0:T(8,128)} %collective-permute-done.15, s32[]{:T(128)S(6)} %select_n.295, f32[8,512,128]{2,1,0:T(8,128)S(1)} %copy-done.2, ...), kind=kLoop, calls=%fused_computation.19 | loop fusion | flops 524288 | bytes 4194320 | tf_op jit(solution)/shard_map/add | solution.py:682
  161.5 1.7 collective-permute-start.19
  163.2 10.8 %tail.3 = (f32[512,512]{1,0:T(8,128)}, f32[4,136,128]{2,1,0:T(8,128)}, f32[4,512,128]{2,1,0:T(8,128)}, f32[4,512,128]{2,1,0:T(8,128)}) custom-call(s32[3]{0:T(128)} %get-tuple-element.228.at_ref, f32[1024,512]{1,0:T(8,128)} %get-tuple-element.121.refs_0_, f32[512,512]{1,0:T(8,128)} %collective-permute-done.10.refs_1_, ...), custom_call_target="tpu_custom_call" | custom-call | flops 65536 | bytes 65536 | tf_op jit(solution)/shard_map/tail/pallas_call | solution.py:418
  174.2 1.1 slice_select_fusion.2
  175.7 1.3 collective-permute-done.20
  177.0 0.7 fusion.10
  177.8 0.8 pad_maximum_fusion.4
  178.6 2.1 collective-permute-start.23
  180.7 1.0 collective-permute-start.21
  181.7 8.5 %backward.4 = (f32[1024,512]{1,0:T(8,128)}, f32[1024,512]{1,0:T(8,128)}, f32[1024,512]{1,0:T(8,128)}) custom-call(f32[1024,512]{1,0:T(8,128)} %refs_0_.7, f32[1024,512]{1,0:T(8,128)} %k_ref.7, f32[1024,512]{1,0:T(8,128)} %v_ref.7, f32[512,512]{1,0:T(8,128)} %get-tuple-element.176.refs_3_, ...), custom_call_target="tpu_custom_call", output_to_operand_aliasing={{0}: (11, {})} | custom-call | flops 65536 | bytes 21600000 | tf_op jit(solution)/shard_map/backward/pallas_call | solution.py:502
  190.2 3.9 %collective-permute-done.23 = f32[2,512,128]{2,1,0:T(8,128)} collective-permute-done((f32[2,512,128]{2,1,0:T(8,128)}, f32[2,512,128]{2,1,0:T(8,128)}, u32[]{:S(2)}, u32[]{:S(2)}) %collective-permute-start.23) | collective-permute-done | bytes 524320 | tf_op jit(solution)/shard_map/ppermute | solution.py:617
  194.1 1.8 fusion.2
  195.9 0.8 collective-permute-start.25
  196.7 0.9 add.442
  197.7 1.7 collective-permute-start.24
  199.4 4.2 %collective-permute-done.25 = f32[512,128]{1,0:T(8,128)S(1)} collective-permute-done((f32[512,128]{1,0:T(8,128)}, f32[512,128]{1,0:T(8,128)S(1)}, u32[]{:S(2)}, u32[]{:S(2)}) %collective-permute-start.25) | collective-permute-done | bytes 262176 | tf_op jit(solution)/shard_map/ppermute | solution.py:617
  204.8 1.2 collective-permute-start.26
  206.0 8.5 %backward.5 = (f32[1024,512]{1,0:T(8,128)}, f32[1024,512]{1,0:T(8,128)}, f32[1024,512]{1,0:T(8,128)}) custom-call(f32[1024,512]{1,0:T(8,128)} %refs_0_.7, f32[1024,512]{1,0:T(8,128)} %k_ref.7, f32[1024,512]{1,0:T(8,128)} %v_ref.7, f32[512,512]{1,0:T(8,128)} %get-tuple-element.176.refs_3_, ...), custom_call_target="tpu_custom_call", output_to_operand_aliasing={{0}: (11, {}), {1}: (12, {}), {2}: (13, {})} | custom-call | flops 65536 | bytes 21600000 | tf_op jit(solution)/shard_map/backward/pallas_call | solution.py:502
  214.5 2.2 collective-permute-start.27
  217.3 1.1 fusion
  218.4 1.4 collective-permute-done.27
  219.9 2.0 collective-permute-start.30
  222.1 0.7 pad_maximum_fusion.6.state_ref
  222.8 6.8 %finish.1 = (f32[1024,512]{1,0:T(8,128)}, f32[1024,512]{1,0:T(8,128)}) custom-call(f32[1024,512]{1,0:T(8,128)} %k_ref.7, f32[1024,512]{1,0:T(8,128)} %v_ref.7, f32[1024,512]{1,0:T(8,128)} %get-tuple-element.184.dk_ref, f32[1024,512]{1,0:T(8,128)} %get-tuple-element.185.dv_ref, f32[4,136,128]{2,1,0:T(8,128)} %pad_maximum_fusion.6.state_ref), custom_call_target="tpu_custom_call" | custom-call | flops 65536 | bytes 65536 | tf_op jit(solution)/shard_map/finish/pallas_call | solution.py:805
  230.3 0.8 copy.18
  (75 shorter events, 6.0 us)
Async XLA Ops:
  0.6 94.0 %collective-permute-start.6 = (f32[1024,1024]{1,0:T(8,128)}, f32[1024,1024]{1,0:T(8,128)}, u32[]{:S(2)}, u32[]{:S(2)}) collective-permute-start(f32[1024,1024]{1,0:T(8,128)} %refs_0_.4), channel_id=1, source_target_pairs={{0,1},{1,2},{2,3},{3,0},{4,5},{5,6},{6,7},{7,4},{8,9},{9,10},{10,1... | collective-permute-start | bytes 12582920 | tf_op jit(solution)/shard_map/ppermute | solution.py:704
  2.3 92.3 %collective-permute-start.7 = (f32[1024,1024]{1,0:T(8,128)}, f32[1024,1024]{1,0:T(8,128)}, u32[]{:S(2)}, u32[]{:S(2)}) collective-permute-start(f32[1024,1024]{1,0:T(8,128)} %refs_0_.4), channel_id=1, source_target_pairs={{0,3},{1,0},{2,1},{3,2},{4,7},{5,4},{6,5},{7,6},{8,11},{9,8},{10,9... | collective-permute-start | bytes 12582920 | tf_op jit(solution)/shard_map/ppermute | solution.py:707
  9.7 1.4 collective-permute-start
  12.1 8.4 %collective-permute-start.1 = (f32[2,136,128]{2,1,0:T(8,128)S(1)}, f32[2,136,128]{2,1,0:T(8,128)S(1)}, u32[]{:S(2)}, u32[]{:S(2)}) collective-permute-start(f32[2,136,128]{2,1,0:T(8,128)S(1)} %fusion.11), channel_id=1, source_target_pairs={{0,8},{4,12},{8,0},{12,4},{16,24},{20,28},{24,16},{28,20},{32,40},... | collective-permute-start | bytes 417800 | tf_op jit(solution)/shard_map/ppermute | solution.py:617
  20.5 6.7 %collective-permute-start.2 = (f32[2,136,128]{2,1,0:T(8,128)S(1)}, f32[2,136,128]{2,1,0:T(8,128)S(1)}, u32[]{:S(2)}, u32[]{:S(2)}) collective-permute-start(f32[2,136,128]{2,1,0:T(8,128)S(1)} %add.378), channel_id=1, source_target_pairs={{0,24},{4,28},{8,16},{12,20},{16,8},{20,12},{24,0},{28,4},{32,56},... | collective-permute-start | bytes 417800 | tf_op jit(solution)/shard_map/ppermute | solution.py:617
  27.3 12.9 %copy-start = (f32[4,136,128]{2,1,0:T(8,128)S(1)}, f32[4,136,128]{2,1,0:T(8,128)}, u32[]{:S(2)}) copy-start(f32[4,136,128]{2,1,0:T(8,128)} %update.1) | copy-start | bytes 835588
  27.3 13.1 %copy-start.8 = (f32[4]{0:T(128)S(1)}, f32[4]{0:T(128)}, u32[]{:S(2)}) copy-start(f32[4]{0:T(128)} %param.9) | copy-start | bytes 52
  27.3 7.7 %collective-permute-start.3 = (f32[2,136,128]{2,1,0:T(8,128)S(1)}, f32[2,136,128]{2,1,0:T(8,128)S(1)}, u32[]{:S(2)}, u32[]{:S(2)}) collective-permute-start(f32[2,136,128]{2,1,0:T(8,128)S(1)} %add.379), channel_id=1, source_target_pairs={{0,32},{4,36},{8,40},{12,44},{16,48},{20,52},{24,56},{28,60},{32,0... | collective-permute-start | bytes 417800 | tf_op jit(solution)/shard_map/ppermute | solution.py:617
  35.0 5.1 %collective-permute-start.4 = (f32[2,136,128]{2,1,0:T(8,128)S(1)}, f32[2,136,128]{2,1,0:T(8,128)S(1)}, u32[]{:S(2)}, u32[]{:S(2)}) collective-permute-start(f32[2,136,128]{2,1,0:T(8,128)S(1)} %add.380), channel_id=1, source_target_pairs={{0,96},{4,100},{8,104},{12,108},{16,112},{20,116},{24,120},{28,124... | collective-permute-start | bytes 417800 | tf_op jit(solution)/shard_map/ppermute | solution.py:617
  40.3 1.4 collective-permute-start.5
  61.1 19.4 %copy-start.6 = (f32[4,512,128]{2,1,0:T(8,128)S(1)}, f32[4,512,128]{2,1,0:T(8,128)}, u32[]{:S(2)}) copy-start(f32[4,512,128]{2,1,0:T(8,128)} %get-tuple-element.117) | copy-start | bytes 3145732
  61.1 3.0 %collective-permute-start.8 = (f32[4,512,128]{2,1,0:T(8,128)}, f32[4,512,128]{2,1,0:T(8,128)S(1)}, u32[]{:S(2)}, u32[]{:S(2)}) collective-permute-start(f32[4,512,128]{2,1,0:T(8,128)} %get-tuple-element.118), channel_id=1, source_target_pairs={{0,4},{4,0},{8,12},{12,8},{16,20},{20,16},{24,28},{28,24},{32,36},... | collective-permute-start | bytes 3145736 | tf_op jit(solution)/shard_map/ppermute | solution.py:605
  65.2 15.3 %collective-permute-start.9 = (f32[2,512,128]{2,1,0:T(8,128)S(1)}, f32[2,512,128]{2,1,0:T(8,128)S(1)}, u32[]{:S(2)}, u32[]{:S(2)}) collective-permute-start(f32[2,512,128]{2,1,0:T(8,128)S(1)} %pad_maximum_fusion.1), channel_id=1, source_target_pairs={{0,24},{4,28},{8,16},{12,20},{16,8},{20,12},{24,0},{28,4},{32,56},... | collective-permute-start | bytes 1572872 | tf_op jit(solution)/shard_map/ppermute | solution.py:617
  97.3 29.9 %collective-permute-start.12 = (f32[512,512]{1,0:T(8,128)}, f32[512,512]{1,0:T(8,128)S(1)}, u32[]{:S(2)}, u32[]{:S(2)}) collective-permute-start(f32[512,512]{1,0:T(8,128)} %get-tuple-element.124), channel_id=1, source_target_pairs={{0,1},{1,2},{2,3},{3,0},{4,5},{5,6},{6,7},{7,4},{8,9},{9,10},{10,1... | collective-permute-start | bytes 3145736 | tf_op jit(solution)/shard_map/ppermute | solution.py:704
  101.4 25.7 %collective-permute-start.13 = (f32[512,512]{1,0:T(8,128)}, f32[512,512]{1,0:T(8,128)S(1)}, u32[]{:S(2)}, u32[]{:S(2)}) collective-permute-start(f32[512,512]{1,0:T(8,128)} %get-tuple-element.125), channel_id=1, source_target_pairs={{0,3},{1,0},{2,1},{3,2},{4,7},{5,4},{6,5},{7,6},{8,11},{9,8},{10,9... | collective-permute-start | bytes 3145736 | tf_op jit(solution)/shard_map/ppermute | solution.py:707
  103.1 24.0 %collective-permute-start.14 = (f32[512,128]{1,0:T(8,128)S(1)}, f32[512,128]{1,0:T(8,128)S(1)}, u32[]{:S(2)}, u32[]{:S(2)}) collective-permute-start(f32[512,128]{1,0:T(8,128)S(1)} %get-tuple-element.129), channel_id=1, source_target_pairs={{0,8},{4,12},{8,0},{12,4},{16,24},{20,28},{24,16},{28,20},{32,40},... | collective-permute-start | bytes 786440 | tf_op jit(solution)/shard_map/ppermute | solution.py:617
  105.6 21.4 %copy-start.7 = (f32[512,128]{1,0:T(8,128)S(1)}, f32[512,128]{1,0:T(8,128)}, u32[]{:S(2)}) copy-start(f32[512,128]{1,0:T(8,128)} %get-tuple-element.128) | copy-start | bytes 786436
  127.1 3.5 %copy-start.3 = (f32[512,512]{1,0:T(8,128)}, f32[512,512]{1,0:T(8,128)S(1)}, u32[]{:S(2)}) copy-start(f32[512,512]{1,0:T(8,128)S(1)} %collective-permute-done.12.refs_1_) | copy-start | bytes 3145732
  127.1 3.5 %copy-start.4 = (f32[512,512]{1,0:T(8,128)}, f32[512,512]{1,0:T(8,128)S(1)}, u32[]{:S(2)}) copy-start(f32[512,512]{1,0:T(8,128)S(1)} %collective-permute-done.13.refs_2_) | copy-start | bytes 3145732
  127.2 13.7 %collective-permute-start.15 = (f32[8,512,128]{2,1,0:T(8,128)}, f32[8,512,128]{2,1,0:T(8,128)}, u32[]{:S(2)}, u32[]{:S(2)}) collective-permute-start(f32[8,512,128]{2,1,0:T(8,128)} %get-tuple-element.135), channel_id=1, source_target_pairs={{0,4},{4,0},{8,12},{12,8},{16,20},{20,16},{24,28},{28,24},{32,36},... | collective-permute-start | bytes 6291464 | tf_op jit(solution)/shard_map/ppermute | solution.py:605
  127.3 34.2 %collective-permute-start.10 = (f32[512,512]{1,0:T(8,128)}, f32[512,512]{1,0:T(8,128)}, u32[]{:S(2)}, u32[]{:S(2)}) collective-permute-start(f32[512,512]{1,0:T(8,128)} %get-tuple-element.122), channel_id=1, source_target_pairs={{0,1},{1,2},{2,3},{3,0},{4,5},{5,6},{6,7},{7,4},{8,9},{9,10},{10,1... | collective-permute-start | bytes 3145736 | tf_op jit(solution)/shard_map/ppermute | solution.py:704
  127.7 33.7 %collective-permute-start.11 = (f32[512,512]{1,0:T(8,128)}, f32[512,512]{1,0:T(8,128)}, u32[]{:S(2)}, u32[]{:S(2)}) collective-permute-start(f32[512,512]{1,0:T(8,128)} %get-tuple-element.123), channel_id=1, source_target_pairs={{0,3},{1,0},{2,1},{3,2},{4,7},{5,4},{6,5},{7,6},{8,11},{9,8},{10,9... | collective-permute-start | bytes 3145736 | tf_op jit(solution)/shard_map/ppermute | solution.py:707
  130.6 10.3 %copy-start.2 = (f32[8,512,128]{2,1,0:T(8,128)S(1)}, f32[8,512,128]{2,1,0:T(8,128)}, u32[]{:S(2)}) copy-start(f32[8,512,128]{2,1,0:T(8,128)} %get-tuple-element.141) | copy-start | bytes 6291460
  143.0 15.2 %collective-permute-start.16 = (f32[2,512,128]{2,1,0:T(8,128)}, f32[2,512,128]{2,1,0:T(8,128)}, u32[]{:S(2)}, u32[]{:S(2)}) collective-permute-start(f32[2,512,128]{2,1,0:T(8,128)} %pad_maximum_fusion.2), channel_id=1, source_target_pairs={{0,24},{4,28},{8,16},{12,20},{16,8},{20,12},{24,0},{28,4},{32,56},... | collective-permute-start | bytes 1572872 | tf_op jit(solution)/shard_map/ppermute | solution.py:617
  145.6 13.5 %collective-permute-start.17 = (f32[2,512,128]{2,1,0:T(8,128)S(1)}, f32[2,512,128]{2,1,0:T(8,128)}, u32[]{:S(2)}, u32[]{:S(2)}) collective-permute-start(f32[2,512,128]{2,1,0:T(8,128)S(1)} %pad_maximum_fusion.3), channel_id=1, source_target_pairs={{0,8},{4,12},{8,0},{12,4},{16,24},{20,28},{24,16},{28,20},{32,40},... | collective-permute-start | bytes 1572872 | tf_op jit(solution)/shard_map/ppermute | solution.py:617
  161.5 12.5 %collective-permute-start.19 = (f32[512,128]{1,0:T(8,128)S(1)}, f32[512,128]{1,0:T(8,128)S(1)}, u32[]{:S(2)}, u32[]{:S(2)}) collective-permute-start(f32[512,128]{1,0:T(8,128)S(1)} %get-tuple-element.153), channel_id=1, source_target_pairs={{0,24},{4,28},{8,16},{12,20},{16,8},{20,12},{24,0},{28,4},{32,56},... | collective-permute-start | bytes 786440 | tf_op jit(solution)/shard_map/ppermute | solution.py:617
  163.2 10.9 %collective-permute-start.18 = (f32[512,128]{1,0:T(8,128)}, f32[512,128]{1,0:T(8,128)S(1)}, u32[]{:S(2)}, u32[]{:S(2)}) collective-permute-start(f32[512,128]{1,0:T(8,128)} %get-tuple-element.151), channel_id=1, source_target_pairs={{0,8},{4,12},{8,0},{12,4},{16,24},{20,28},{24,16},{28,20},{32,40},... | collective-permute-start | bytes 786440 | tf_op jit(solution)/shard_map/ppermute | solution.py:617
  174.0 3.1 %copy-start.1 = (f32[4,136,128]{2,1,0:T(8,128)S(1)}, f32[4,136,128]{2,1,0:T(8,128)}, u32[]{:S(2)}) copy-start(f32[4,136,128]{2,1,0:T(8,128)} %get-tuple-element.154) | copy-start | bytes 835588
  174.0 3.7 %copy-start.5 = (f32[4,512,128]{2,1,0:T(8,128)S(1)}, f32[4,512,128]{2,1,0:T(8,128)}, u32[]{:S(2)}) copy-start(f32[4,512,128]{2,1,0:T(8,128)} %get-tuple-element.155) | copy-start | bytes 3145732
  174.1 3.6 %collective-permute-start.22 = (f32[4,512,128]{2,1,0:T(8,128)}, f32[4,512,128]{2,1,0:T(8,128)S(1)}, u32[]{:S(2)}, u32[]{:S(2)}) collective-permute-start(f32[4,512,128]{2,1,0:T(8,128)} %get-tuple-element.157), channel_id=1, source_target_pairs={{0,4},{4,0},{8,12},{12,8},{16,20},{20,16},{24,28},{28,24},{32,36},... | collective-permute-start | bytes 3145736 | tf_op jit(solution)/shard_map/ppermute | solution.py:605
  175.3 1.7 collective-permute-start.20
  178.6 15.5 %collective-permute-start.23 = (f32[2,512,128]{2,1,0:T(8,128)}, f32[2,512,128]{2,1,0:T(8,128)}, u32[]{:S(2)}, u32[]{:S(2)}) collective-permute-start(f32[2,512,128]{2,1,0:T(8,128)} %pad_maximum_fusion.4), channel_id=1, source_target_pairs={{0,24},{4,28},{8,16},{12,20},{16,8},{20,12},{24,0},{28,4},{32,56},... | collective-permute-start | bytes 1572872 | tf_op jit(solution)/shard_map/ppermute | solution.py:617
  180.7 15.2 %collective-permute-start.21 = (f32[2,136,128]{2,1,0:T(8,128)}, f32[2,136,128]{2,1,0:T(8,128)S(1)}, u32[]{:S(2)}, u32[]{:S(2)}) collective-permute-start(f32[2,136,128]{2,1,0:T(8,128)} %fusion.10), channel_id=1, source_target_pairs={{0,8},{4,12},{8,0},{12,4},{16,24},{20,28},{24,16},{28,20},{32,40},... | collective-permute-start | bytes 417800 | tf_op jit(solution)/shard_map/ppermute | solution.py:617
  195.9 7.7 %collective-permute-start.25 = (f32[512,128]{1,0:T(8,128)}, f32[512,128]{1,0:T(8,128)S(1)}, u32[]{:S(2)}, u32[]{:S(2)}) collective-permute-start(f32[512,128]{1,0:T(8,128)} %get-tuple-element.170), channel_id=1, source_target_pairs={{0,8},{4,12},{8,0},{12,4},{16,24},{20,28},{24,16},{28,20},{32,40},... | collective-permute-start | bytes 786440 | tf_op jit(solution)/shard_map/ppermute | solution.py:617
  197.7 6.3 %collective-permute-start.24 = (f32[2,136,128]{2,1,0:T(8,128)S(1)}, f32[2,136,128]{2,1,0:T(8,128)S(1)}, u32[]{:S(2)}, u32[]{:S(2)}) collective-permute-start(f32[2,136,128]{2,1,0:T(8,128)S(1)} %add.442), channel_id=1, source_target_pairs={{0,24},{4,28},{8,16},{12,20},{16,8},{20,12},{24,0},{28,4},{32,56},... | collective-permute-start | bytes 417800 | tf_op jit(solution)/shard_map/ppermute | solution.py:617
  204.2 13.1 %collective-permute-start.28 = (f32[2,512,128]{2,1,0:T(8,128)S(1)}, f32[2,512,128]{2,1,0:T(8,128)}, u32[]{:S(2)}, u32[]{:S(2)}) collective-permute-start(f32[2,512,128]{2,1,0:T(8,128)S(1)} %pad_maximum_fusion.5), channel_id=1, source_target_pairs={{0,96},{4,100},{8,104},{12,108},{16,112},{20,116},{24,120},{28,124... | collective-permute-start | bytes 1572872 | tf_op jit(solution)/shard_map/ppermute | solution.py:617
  204.8 9.6 %collective-permute-start.26 = (f32[2,136,128]{2,1,0:T(8,128)S(1)}, f32[2,136,128]{2,1,0:T(8,128)S(1)}, u32[]{:S(2)}, u32[]{:S(2)}) collective-permute-start(f32[2,136,128]{2,1,0:T(8,128)S(1)} %add.444), channel_id=1, source_target_pairs={{0,32},{4,36},{8,40},{12,44},{16,48},{20,52},{24,56},{28,60},{32,0... | collective-permute-start | bytes 417800 | tf_op jit(solution)/shard_map/ppermute | solution.py:617
  214.5 5.3 %collective-permute-start.27 = (f32[2,136,128]{2,1,0:T(8,128)S(1)}, f32[2,136,128]{2,1,0:T(8,128)S(1)}, u32[]{:S(2)}, u32[]{:S(2)}) collective-permute-start(f32[2,136,128]{2,1,0:T(8,128)S(1)} %add.450), channel_id=1, source_target_pairs={{0,96},{4,100},{8,104},{12,108},{16,112},{20,116},{24,120},{28,124... | collective-permute-start | bytes 417800 | tf_op jit(solution)/shard_map/ppermute | solution.py:617
  219.9 2.1 collective-permute-start.29
  219.9 10.3 %collective-permute-start.30 = (f32[512,128]{1,0:T(8,128)S(1)}, f32[512,128]{1,0:T(8,128)S(1)}, u32[]{:S(2)}, u32[]{:S(2)}) collective-permute-start(f32[512,128]{1,0:T(8,128)S(1)} %get-tuple-element.192), channel_id=1, source_target_pairs={{0,32},{4,36},{8,40},{12,44},{16,48},{20,52},{24,56},{28,60},{32,0... | collective-permute-start | bytes 786440 | tf_op jit(solution)/shard_map/ppermute | solution.py:617
